TPU v7x, 32 devices: a whole 2x2x4 slice. The times are simulated.
32 devices in a mesh: leaf: 8 (over z, y), rhs: 4 (over x, core).
Axes of the slice: x: 2, y: 2, z: 4, core: 2. Of those that a mesh axis runs over, the one named last changes fastest.
Arguments:
- rhs_in: float32 [16384, 512], P(('leaf', 'rhs')), may hold values from -6 to 6
- rhs_top: float32 [896, 512], P(None, 'rhs'), may hold values from -6 to 6
- leaf_inv: float32 [32, 512, 512], P('leaf')
- leaf_coupling: float32 [32, 384, 512], P('leaf'), may hold values from -0.125 to 0.125
- coupling_rows: int32 [32, 384], P('leaf'), may hold values from 0 to 383, each once within a row
- top_inv: float32 [7, 128, 128], replicated
- top_coupling: float32 [10, 128, 128], replicated, may hold values from -0.25 to 0.25
Outputs:
- solution_leaf: float32 [16384, 512], P(('leaf', 'rhs'))
- solution_top: float32 [896, 512], P(None, 'rhs')
All inputs are finite; a program needn't handle non-finite values.
Results may differ from a plain program's by a relative error of at most 0.0003.
Values sent between devices are 32-bit elements; how exact they have to be, the bound alone decides.
No kernel may reach another device: no remote copies, remote signals or barrier semaphores. Data moves between devices by JAX's collectives and lax.ppermute only.
A program may use at most 64 MiB of HBM per device.

v0:
```python
import jax
import jax.numpy as jnp
from jax import lax
from jax.sharding import PartitionSpec as P

highest = lax.Precision.HIGHEST


def matmul(left, right):
    return jnp.dot(left, right, precision=highest, preferred_element_type=jnp.float32)


def ancestor_pairs(levels):
    pairs = []
    for panel in range(1, 2**levels - 1):
        above = panel
        while above > 0:
            above = (above - 1) // 2
            pairs.append((panel, above))
    return pairs


def top_solve(rhs_panels, top_inv, top_coupling, levels):
    panel_count = 2**levels - 1
    pairs = ancestor_pairs(levels)
    forward = [None] * panel_count
    for panel in reversed(range(panel_count)):
        accum = rhs_panels[panel]
        for number, (below, above) in enumerate(pairs):
            if above == panel:
                accum = accum - matmul(top_coupling[number], forward[below])
        forward[panel] = matmul(top_inv[panel], accum)
    result = [None] * panel_count
    for panel in range(panel_count):
        accum = forward[panel]
        for number, (below, above) in enumerate(pairs):
            if below == panel:
                accum = accum - matmul(top_coupling[number].T, result[above])
        result[panel] = matmul(top_inv[panel].T, accum)
    return jnp.stack(result)


def lift_blocks(inverse, blocks, coupling, rows, path_length):
    columns = blocks.shape[2]
    lifted = jnp.einsum(
        "bij,bjr->bir", inverse, blocks, precision=highest, preferred_element_type=jnp.float32
    )
    updates = jnp.einsum(
        "bkj,bjr->bkr", coupling, lifted, precision=highest, preferred_element_type=jnp.float32
    )
    path_terms = (
        jnp.zeros((path_length, columns), jnp.float32)
        .at[rows.reshape(-1)]
        .add(updates.reshape(-1, columns))
    )
    return (lifted, path_terms)


def settle_blocks(inverse, lifted, coupling, rows, path_solution):
    picked = path_solution[rows]
    correction = jnp.einsum(
        "bkj,bkr->bjr", coupling, picked, precision=highest, preferred_element_type=jnp.float32
    )
    return jnp.einsum(
        "bji,bjr->bir",
        inverse,
        lifted - correction,
        precision=highest,
        preferred_element_type=jnp.float32,
    )


def per_device(rhs_in, rhs_top, leaf_inv, leaf_coupling, coupling_rows, top_inv, top_coupling):
    block_count, order, _ = leaf_inv.shape
    panel_count, panel_width, _ = top_inv.shape
    levels = (panel_count + 1).bit_length() - 1
    columns = rhs_top.shape[1]
    path_length = coupling_rows.shape[1]
    leaf_count = lax.axis_size("leaf")
    device = lax.axis_index("leaf")
    group_count = lax.axis_size("rhs")
    group = lax.axis_index("rhs")
    per_group = block_count // group_count
    first = group * per_group
    my_inv = lax.dynamic_slice_in_dim(leaf_inv, first, per_group, 0)
    my_coupling = lax.dynamic_slice_in_dim(leaf_coupling, first, per_group, 0)
    my_rows = lax.dynamic_slice_in_dim(coupling_rows, first, per_group, 0)
    blocks = rhs_in.reshape(per_group, order, rhs_in.shape[1])
    lifted, path_terms = lift_blocks(my_inv, blocks, my_coupling, my_rows, path_length)
    path_share = lax.psum_scatter(path_terms, "rhs", scatter_dimension=1, tiled=True)
    on_path = []
    current = 2 ** (levels - 1) - 1 + device * 2 ** (levels - 1) // leaf_count
    for level in range(levels):
        on_path.append(current)
        current = (current - 1) // 2
    placed = jnp.zeros((panel_count, panel_width, columns), jnp.float32)
    for level in range(levels):
        piece = path_share[level * panel_width : (level + 1) * panel_width][None]
        placed = lax.dynamic_update_slice(placed, piece, (on_path[level], 0, 0))
    top_rhs = rhs_top.reshape(panel_count, panel_width, columns)
    summed = lax.psum(placed, "leaf")
    solution_panels = top_solve(top_rhs - summed, top_inv, top_coupling, levels)
    path_solution = jnp.concatenate([solution_panels[panel] for panel in on_path], 0)
    full_path = lax.all_gather(path_solution, "rhs", axis=1, tiled=True)
    solved = settle_blocks(my_inv, lifted, my_coupling, my_rows, full_path)
    solution_leaf = solved.reshape(per_group * order, full_path.shape[1])
    return (solution_leaf, solution_panels.reshape(panel_count * panel_width, columns))


def solution(mesh):
    placed = (
        P(("leaf", "rhs"), None),
        P(None, "rhs"),
        P("leaf", None, None),
        P("leaf", None, None),
        P("leaf", None),
        P(),
        P(),
    )
    return jax.shard_map(
        per_device,
        mesh=mesh,
        in_specs=placed,
        out_specs=(P(("leaf", "rhs"), None), P(None, "rhs")),
        check_vma=False,
    )
```

profile of v0, /device:TPU:0, one launch (start us, length us, event | category | flops | bytes accessed | tf_op | source)
XLA Modules:
  0.0 172.5 jit_solution(17906159054390275795)
XLA Ops:
  7.2 0.9 fusion.112
  8.1 3.4 %fusion.16 = f32[512,512]{1,0:T(8,128)S(1)} fusion(f32[512,512]{1,0:T(8,128)} %param.7, f32[4,512,512]{2,1,0:T(8,128)} %param.9, s32[]{:T(128)S(6)} %select_n.41), kind=kOutput, calls=%fused_computation.43 | convolution fusion | flops 1610612736 | bytes 3145732 | tf_op jit(solution)/shard_map/bij,bjr->bir/dot_general | solution.py:45
  11.5 1.0 copy-done.1
  12.5 2.3 %fusion.21 = f32[384,512]{1,0:T(8,128)} fusion(f32[512,512]{1,0:T(8,128)S(1)} %fusion.16, f32[4,384,512]{2,1,0:T(8,128)S(1)} %copy-done, s32[]{:T(128)S(6)} %select_n.41), kind=kOutput, calls=%fused_computation.48 | convolution fusion | flops 1207959552 | bytes 2621444 | tf_op jit(solution)/shard_map/bkj,bjr->bkr/dot_general | solution.py:48
  14.8 4.3 %scatter_custom_fusion = f32[384,512]{1,0:T(8,128)} fusion(s32[384]{0:T(512)S(1)} %fusion.112, f32[384,512]{1,0:T(8,128)} %fusion.21, f32[]{:T(128)} %constant.51.clone.1), kind=kCustom, calls=%fused_computation.52 | custom fusion | flops 196608 | bytes 786944 | tf_op jit(solution)/shard_map/scatter-add | solution.py:54
  19.3 26.0 %reduce-scatter.2.cloned.1.call-done = f32[384,128]{1,0:T(8,128)} async-done(((f32[384,512]{1,0:T(8,128)}), f32[384,128]{1,0:T(8,128)}) %reduce-scatter.2.cloned.1.call-update) | async-done | bytes 196624 | tf_op jit(solution)/shard_map/reduce_scatter | solution.py:90
  45.2 0.8 broadcast_in_dim.19
  46.0 1.5 fusion.33
  47.5 1.5 fusion.32
  49.0 1.5 fusion.31
  50.5 0.7 fusion.113
  51.2 71.4 %all-reduce.2.cloned.1.call-done = f32[7,128,128]{2,1,0:T(8,128)} async-done(((f32[7,128,128]{2,1,0:T(8,128)}), f32[7,128,128]{2,1,0:T(8,128)}) %all-reduce.2.cloned.1.call-update) | async-done | bytes 458768 | tf_op jit(solution)/shard_map/psum | solution.py:101
  122.6 1.3 sub.98
  123.9 1.1 fusion.28
  125.0 1.1 fusion.27
  126.2 1.1 fusion.30
  127.3 1.1 fusion.29
  128.4 1.1 fusion.10
  129.5 1.1 fusion.9
  130.7 1.1 fusion.50
  131.8 1.1 fusion.13
  132.9 1.1 fusion.12
  134.0 1.1 fusion.64
  135.1 1.1 fusion.11
  136.2 1.1 fusion.8
  137.3 1.1 fusion.7
  140.4 0.3 bitcast_dynamic-update-slice_fusion.1
  144.6 0.7 copy-done.4
  145.3 9.2 %all_gather.3 = f32[384,512]{1,0:T(8,128)} all-gather(f32[384,128]{1,0:T(8,128)S(1)} %pad_maximum_fusion), channel_id=1, replica_groups=mesh['leaf'=8,'rhs'=4] {'rhs'}, dimensions={1}, use_global_device_ids=true | all-gather | bytes 983040 | tf_op jit(solution)/shard_map/all_gather | solution.py:104
  154.5 3.8 %gather_fusion = f32[384,512]{1,0:T(8,128)} fusion(f32[384,512]{1,0:T(8,128)} %all_gather.3, s32[1024]{0:T(1024)S(1)} %pad_clamp_fusion), kind=kCustom, calls=%fused_computation | custom fusion | bytes 1574400 | tf_op jit(solution)/shard_map/gather | solution.py:60
  158.3 3.3 %convolution_subtract_fusion = f32[512,512]{1,0:T(8,128)S(1)} fusion(f32[512,512]{1,0:T(8,128)} %copy-done.1, f32[384,512]{1,0:T(8,128)} %gather_fusion, f32[4,384,512]{2,1,0:T(8,128)S(1)} %copy-done, s32[]{:T(128)S(6)} %select_n.41), kind=kOutput, calls=%fused_computation.2 | convolution fusion | flops 1208221696 | bytes 3670020 | tf_op jit(solution)/shard_map/bkj,bkr->bjr/dot_general | solution.py:61
  161.6 4.1 %fusion.14 = f32[512,512]{1,0:T(8,128)} fusion(f32[512,512]{1,0:T(8,128)S(1)} %convolution_subtract_fusion, f32[4,512,512]{2,1,0:T(8,128)} %param.9, s32[]{:T(128)S(6)} %select_n.41), kind=kOutput, calls=%fused_computation.41 | convolution fusion | flops 1610612736 | bytes 3145732 | tf_op jit(solution)/shard_map/bji,bjr->bir/dot_general | solution.py:64
  (35 shorter events, 5.8 us)
Async XLA Ops:
  7.2 5.3 %copy-start = (f32[4,384,512]{2,1,0:T(8,128)S(1)}, f32[4,384,512]{2,1,0:T(8,128)}, u32[]{:S(2)}) copy-start(f32[4,384,512]{2,1,0:T(8,128)} %param.10) | copy-start | bytes 9437188
  7.2 38.1 %reduce-scatter.2.cloned.1.call-start = ((), (), s32[]{:S(2)}) async-start(), calls=%async_computation.1 | async-start | bytes 983040 | tf_op jit(solution)/shard_map/reduce_scatter | solution.py:90
  11.5 1.0 copy-start.1
  19.2 103.4 %all-reduce.2.cloned.1.call-start = ((), (), s32[]{:S(2)}) async-start(), calls=%async_computation.2 | async-start | bytes 917504 | tf_op jit(solution)/shard_map/psum | solution.py:101
  122.6 15.9 %copy-start.2 = (f32[10,128,128]{2,1,0:T(8,128)S(1)}, f32[10,128,128]{2,1,0:T(8,128)}, u32[]{:S(2)}) copy-start(f32[10,128,128]{2,1,0:T(8,128)} %param.13) | copy-start | bytes 1966084
  122.6 16.7 %copy-start.3 = (f32[7,128,128]{2,1,0:T(8,128)S(1)}, f32[7,128,128]{2,1,0:T(8,128)}, u32[]{:S(2)}) copy-start(f32[7,128,128]{2,1,0:T(8,128)} %param.12) | copy-start | bytes 1376260
  144.6 0.8 copy-start.4
Sparse Core Ops, SparseCore 0:
  19.3 25.9 reduce-scatter.1
  50.6 71.9 all-reduce.1
where the time goes:
time: 174 us; the launch traced here: 173 us
  waiting for transfers between devices  97.4 us (56%)
  matrix products  33.6 us (19%)
  between operations  14.4 us (8%)
  local copies, waits for them, and re-layouts  10.7 us (6%)
  blocking collectives  9.2 us (5%)
  other arithmetic  7.2 us (4%)
    psum x1, waiting for transfers between devices, per_device(): summed = lax.psum(placed, 'leaf')  71.4 us
    reduce_scatter x1, waiting for transfers between devices, per_device(): lax.psum_scatter(path_terms, 'rhs', scatter_dimension=1, tiled=True)  26 us
    dot_general x34, matrix products, matmul(): jnp.dot(left, right, precision=highest, preferred_element_type=jnp.float32)  20.4 us
    all_gather x1, blocking collectives, per_device(): full_path = lax.all_gather(path_solution, 'rhs', axis=1, tiled=True)  9.2 us
    dynamic_update_slice x3, local copies, waits for them, and re-layouts, per_device(): placed = lax.dynamic_update_slice(placed, piece, (on_path[level], 0, 0))  4.42 us
    scatter-add x1, other arithmetic, lift_blocks(): path_terms = jnp.zeros((path_length, columns), jnp.float32).at[rows.resha...  4.3 us
    dot_general x1, matrix products, settle_blocks(): jnp.einsum('bji,bjr->bir', inverse, lifted - correction, precision=highes...  4.05 us
    gather x1, local copies, waits for them, and re-layouts, settle_blocks(): picked = path_solution[rows]  3.79 us
  transfers between devices with their start and end apart: 2, of which 2 were waited for; matrix products, arithmetic and copies ran while one was open for 0% of the time, Pallas kernels for 0%

commit v1 on v0

v1 whole, which is shorter than its diff:
```python
import jax
import jax.numpy as jnp
from jax import lax
from jax.sharding import PartitionSpec as P

high = lax.Precision.HIGH


def dot(left, right, dims):
    return lax.dot_general(
        left, right, (dims, ((), ())), precision=high, preferred_element_type=jnp.float32
    )


def nn(left, right):
    return dot(left, right, ((1,), (0,)))


def tn(left, right):
    return dot(left, right, ((0,), (0,)))


def swap(value, axis_sizes, partner):
    leaf_count, group_count = axis_sizes
    pairs = []
    for leaf in range(leaf_count):
        for group in range(group_count):
            to_leaf, to_group = partner(leaf, group)
            pairs.append((leaf * group_count + group, to_leaf * group_count + to_group))
    return lax.ppermute(value, ("leaf", "rhs"), pairs)


def per_device(rhs_in, rhs_top, leaf_inv, leaf_coupling, coupling_rows, top_inv, top_coupling):
    block_count, order, _ = leaf_inv.shape
    panel_count, width, _ = top_inv.shape
    levels = (panel_count + 1).bit_length() - 1
    columns = rhs_top.shape[1]
    path_length = coupling_rows.shape[1]
    leaf_count = lax.axis_size("leaf")
    group_count = lax.axis_size("rhs")
    sizes = (leaf_count, group_count)
    leaf = lax.axis_index("leaf")
    group = lax.axis_index("rhs")
    bottoms = 2 ** (levels - 1)
    sharers = leaf_count // bottoms
    place = leaf // sharers
    core, half = group % 2, group // 2
    keep = jnp.where(core == 0, half, leaf % 2)

    def flip_first(lf, gr):
        return (lf, gr ^ 2) if gr % 2 == 0 else (lf ^ 1, gr)

    def flip_second(lf, gr):
        return (lf ^ 1, gr) if gr % 2 == 0 else (lf, gr ^ 2)

    path = [bottoms - 1 + place]
    for level in range(1, levels):
        path.append((path[-1] - 1) // 2)
    first_pair = []
    for level in range(levels):
        depth = levels - 1 - level
        before = sum(d * 2**d for d in range(depth))
        first_pair.append(before + (path[level] - (2**depth - 1)) * depth)
    inv = [lax.dynamic_index_in_dim(top_inv, path[level], 0, False) for level in range(levels)]
    coup = {}
    for below in range(levels):
        for above in range(below + 1, levels):
            coup[below, above] = lax.dynamic_index_in_dim(
                top_coupling, first_pair[below] + above - below - 1, 0, False
            )

    per_group = block_count // group_count
    first = group * per_group
    panels = rhs_top.reshape(panel_count, width, columns)
    total = None
    lifted_all, coupling_all, inv_all = [], [], []
    for block in range(per_group):
        my_inv = lax.dynamic_index_in_dim(leaf_inv, first + block, 0, False)
        my_coupling = lax.dynamic_index_in_dim(leaf_coupling, first + block, 0, False)
        my_rows = lax.dynamic_index_in_dim(coupling_rows, first + block, 0, False)
        chosen = (jnp.arange(path_length)[:, None] == my_rows[None, :]).astype(jnp.float32)
        permuted = nn(chosen, my_coupling)
        lifted = nn(my_inv, rhs_in[block * order : (block + 1) * order])
        terms = nn(permuted, lifted)
        total = terms if total is None else total + terms
        lifted_all.append(lifted)
        coupling_all.append(permuted)
        inv_all.append(my_inv)
    total = total.reshape(path_length, 2, 2, columns)
    other = lax.dynamic_index_in_dim(total, 1 - core, 2, False).transpose(1, 0, 2)
    mine = lax.dynamic_index_in_dim(total, core, 2, False).transpose(1, 0, 2)
    base = []
    for level in range(levels):
        counts = (leaf % (sharers * 2**level)) == 0
        rows = lax.dynamic_index_in_dim(panels, path[level], 0, False)
        base.append(jnp.where(counts, rows, 0.0))
    base = jnp.concatenate(base, 0)
    got = swap(other, sizes, lambda lf, gr: (lf, gr ^ 1))
    number = jnp.arange(2)[:, None, None]
    mine = jnp.where(number == half, base[None], 0.0) - mine - got
    got = swap(lax.dynamic_index_in_dim(mine, 1 - keep, 0, False), sizes, flip_first)
    value = lax.dynamic_index_in_dim(mine, keep, 0, False) + got
    value = value + swap(value, sizes, flip_second)
    bit = 2
    while bit < sharers:
        value = value + swap(value, sizes, lambda lf, gr, bit=bit: (lf ^ bit, gr))
        bit *= 2

    forward = []
    rows = [value[level * width : (level + 1) * width] for level in range(levels)]
    for level in range(levels):
        forward.append(nn(inv[level], rows[level]))
        if level + 1 < levels:
            rest = jnp.concatenate(
                [rows[above] - nn(coup[level, above], forward[level]) for above in range(level + 1, levels)], 0
            )
            bit = sharers * 2**level
            rest = rest + swap(rest, sizes, lambda lf, gr, bit=bit: (lf ^ bit, gr))
            for above in range(level + 1, levels):
                rows[above] = rest[(above - level - 1) * width : (above - level) * width]
    solved = [None] * levels
    for level in reversed(range(levels)):
        accum = forward[level]
        for above in reversed(range(level + 1, levels)):
            accum = accum - tn(coup[level, above], solved[above])
        solved[level] = tn(inv[level], accum)
    solved = jnp.concatenate(solved, 0)

    got = swap(solved, sizes, flip_first)
    pair = jnp.where((number == keep), solved[None], got[None])
    got = swap(pair, sizes, lambda lf, gr: (lf, gr ^ 1))
    core_number = jnp.arange(2)[None, :, None, None]
    full = jnp.where(core_number == core, pair[:, None], got[:, None])
    full = full.transpose(2, 0, 1, 3).reshape(path_length, group_count * columns)
    answers = []
    for block in range(per_group):
        inner = lifted_all[block] - tn(coupling_all[block], full)
        answers.append(tn(inv_all[block], inner))

    own = lax.dynamic_index_in_dim(pair, half, 0, False)
    depths = {levels - 1: own[None, :width]}
    for level in range(1, levels):
        bit = sharers * 2 ** (level - 1)
        sent = jnp.concatenate([depths[d] for d in sorted(depths)], 0)
        came = swap(sent, sizes, lambda lf, gr, bit=bit: (lf ^ bit, gr))
        late = (leaf // bit) % 2
        offset = 0
        for d in sorted(depths):
            count = depths[d].shape[0]
            theirs = came[offset : offset + count]
            offset += count
            depths[d] = jnp.where(
                late == 1,
                jnp.concatenate([theirs, depths[d]], 0),
                jnp.concatenate([depths[d], theirs], 0),
            )
        depths[levels - 1 - level] = own[None, level * width : (level + 1) * width]
    top = jnp.concatenate([depths[d] for d in sorted(depths)], 0)
    return jnp.concatenate(answers, 0), top.reshape(panel_count * width, columns)


def solution(mesh):
    placed = (
        P(("leaf", "rhs"), None),
        P(None, "rhs"),
        P("leaf", None, None),
        P("leaf", None, None),
        P("leaf", None),
        P(),
        P(),
    )
    return jax.shard_map(
        per_device,
        mesh=mesh,
        in_specs=placed,
        out_specs=(P(("leaf", "rhs"), None), P(None, "rhs")),
        check_vma=False,
    )
```

time: 174 us -> 95.2 us (0.55)
  waiting for transfers between devices: 97.4 us -> 21.9 us
  starting transfers between devices: 0.08 us -> 17.6 us
  between operations: 14.4 us -> 0.87 us
  local copies, waits for them, and re-layouts: 10.7 us -> 20.6 us
  matrix products: 33.6 us -> 23.8 us
  blocking collectives: 9.2 us -> 0 us
  other arithmetic: 7.2 us -> 9.22 us
    psum x1 -> x0, waiting for transfers between devices: 71.4 us -> none  [per_device(): summed = lax.psum(placed, 'leaf')]
    reduce_scatter x1 -> x0, waiting for transfers between devices: 26 us -> none  [per_device(): lax.psum_scatter(path_terms, 'rhs', scatter_dimension=1, tiled=True)]
    ppermute x0 -> x9, waiting for transfers between devices: none -> 21.9 us  [swap(): return lax.ppermute(value, ('leaf', 'rhs'), pairs)]
    ppermute x0 -> x9, starting transfers between devices: none -> 17.6 us  [swap(): return lax.ppermute(value, ('leaf', 'rhs'), pairs)]
    dot_general x38 -> x17, matrix products: 33.6 us -> 23.8 us  [dot(): lax.dot_general(left, right, (dims, ((), ())), precision=high, preferred_...]
    all_gather x1 -> x0, blocking collectives: 9.2 us -> none  [per_device(): full_path = lax.all_gather(path_solution, 'rhs', axis=1, tiled=True)]
    broadcast_in_dim x1 -> x7, local copies, waits for them, and re-layouts: 0.8 us -> 9.06 us  [per_device(): full = jnp.where(core_number == core, pair[:, None], got[:, None])]
    dynamic_update_slice x3 -> x0, local copies, waits for them, and re-layouts: 4.42 us -> none  [per_device(): placed = lax.dynamic_update_slice(placed, piece, (on_path[level], 0, 0))]
  transfers between devices with their start and end apart: 2 -> 9, of which waited for: 2 -> 8; matrix products, arithmetic and copies ran while one was open for 0% -> 13% of each run, Pallas kernels for 0% -> 0%
where the time goes in v1:
time: 95.2 us; the launch traced here: 94 us
  matrix products  23.8 us (25%)
  waiting for transfers between devices  21.9 us (23%)
  local copies, waits for them, and re-layouts  20.6 us (22%)
  starting transfers between devices  17.6 us (18%)
  other arithmetic  9.22 us (10%)
    dot_general x17, matrix products, dot(): lax.dot_general(left, right, (dims, ((), ())), precision=high, preferred_...  23.8 us
    ppermute x9, waiting for transfers between devices, swap(): return lax.ppermute(value, ('leaf', 'rhs'), pairs)  21.9 us
    ppermute x9, starting transfers between devices, swap(): return lax.ppermute(value, ('leaf', 'rhs'), pairs)  17.6 us
    broadcast_in_dim x7, local copies, waits for them, and re-layouts, per_device(): full = jnp.where(core_number == core, pair[:, None], got[:, None])  9.06 us
    unnamed x15, local copies, waits for them, and re-layouts  3.53 us
    reshape x1, local copies, waits for them, and re-layouts, per_device(): total = total.reshape(path_length, 2, 2, columns)  2.52 us
    dynamic_slice x1, local copies, waits for them, and re-layouts, per_device(): mine = lax.dynamic_index_in_dim(total, core, 2, False).transpose(1, 0, 2)  2.18 us
  transfers between devices with their start and end apart: 9, of which 8 were waited for; matrix products, arithmetic and copies ran while one was open for 13% of the time, Pallas kernels for 0%

profile of v1, /device:TPU:0, one launch (start us, length us, event | category | flops | bytes accessed | tf_op | source)
XLA Modules:
  0.0 94.0 jit_solution(669826100185571302)
XLA Ops:
  1.5 2.6 %fusion.3 = f32[512,512]{1,0:T(8,128)S(1)} fusion(f32[512,512]{1,0:T(8,128)} %param.7, f32[4,512,512]{2,1,0:T(8,128)} %param.9, s32[]{:T(128)S(6)} %select_n.169), kind=kOutput, calls=%fused_computation.6 | convolution fusion | flops 805306368 | bytes 3145732 | tf_op jit(solution)/shard_map/dot_general | solution.py:10
  6.0 1.7 %fusion.75 = f32[384,512]{1,0:T(8,128)} fusion(f32[384,512]{1,0:T(8,128)S(1)} %fusion.7, f32[512,512]{1,0:T(8,128)S(1)} %fusion.3), kind=kOutput, calls=%fused_computation.102 | convolution fusion | flops 603979776 | bytes 2621440 | tf_op jit(solution)/shard_map/dot_general | solution.py:10
  7.8 2.5 %reshape.53 = f32[384,2,2,128]{3,2,1,0:T(2,128)} reshape(f32[384,512]{1,0:T(8,128)} %fusion.75) | data formatting | bytes 1572864 | tf_op jit(solution)/shard_map/reshape | solution.py:89
  10.3 2.2 %constant_dynamic-slice_fusion.4 = (f32[384,2,1,128]{3,2,1,0:T(1,128)S(1)}, f32[384,2,1,128]{3,2,1,0:T(1,128)S(1)}) fusion(f32[384,2,2,128]{3,2,1,0:T(2,128)} %reshape.53, s32[]{:T(128)S(6)} %select_n.192, s32[]{:T(128)S(6)} %select_n.193), kind=kLoop, calls=%fused_computation.92 | loop fusion | bytes 1572872 | tf_op jit(solution)/shard_map/jit(dynamic_index_in_dim)/dynamic_slice | solution.py:91
  15.4 1.1 %fusion.12 = f32[2,384,128]{2,1,0:T(8,128)S(1)} fusion(f32[2,384,128]{2,1,0:T(8,128)} %collective-permute-done, f32[384,2,1,128]{3,2,1,0:T(1,128)S(1)} %get-tuple-element.2, f32[384,128]{1,0:T(8,128)S(1)} %pad_maximum_fusion.1, pred[2]{0:T(512)(128)(4,1)S(1)} %iota_compare_fusion.2), kind=kLoop, calls=%fused_computation.19 | loop fusion | flops 294912 | bytes 1376258 | tf_op jit(solution)/shard_map/sub | solution.py:100
  17.3 2.9 %collective-permute-start.1 = (f32[384,128]{1,0:T(8,128)S(1)}, f32[384,128]{1,0:T(8,128)S(1)}, u32[]{:S(2)}, u32[]{:S(2)}) collective-permute-start(f32[384,128]{1,0:T(8,128)S(1)} %dynamic-slice_bitcast_fusion), channel_id=1, source_target_pairs={{0,2},{1,5},{2,0},{3,7},{4,6},{5,1},{6,4},{7,3},{8,10},{9,13},{10,... | collective-permute-start | bytes 589832 | tf_op jit(solution)/shard_map/ppermute | solution.py:30
  20.2 3.6 %collective-permute-done.1 = f32[384,128]{1,0:T(8,128)S(1)} collective-permute-done((f32[384,128]{1,0:T(8,128)S(1)}, f32[384,128]{1,0:T(8,128)S(1)}, u32[]{:S(2)}, u32[]{:S(2)}) %collective-permute-start.1) | collective-permute-done | bytes 196640 | tf_op jit(solution)/shard_map/ppermute | solution.py:30
  24.8 2.1 %collective-permute-start.2 = (f32[384,128]{1,0:T(8,128)S(1)}, f32[384,128]{1,0:T(8,128)S(1)}, u32[]{:S(2)}, u32[]{:S(2)}) collective-permute-start(f32[384,128]{1,0:T(8,128)S(1)} %bitcast_add_fusion), channel_id=1, source_target_pairs={{0,4},{1,3},{2,6},{3,1},{4,0},{5,7},{6,2},{7,5},{8,12},{9,11},{10,... | collective-permute-start | bytes 589832 | tf_op jit(solution)/shard_map/ppermute | solution.py:30
  26.9 3.6 %collective-permute-done.2 = f32[384,128]{1,0:T(8,128)S(1)} collective-permute-done((f32[384,128]{1,0:T(8,128)S(1)}, f32[384,128]{1,0:T(8,128)S(1)}, u32[]{:S(2)}, u32[]{:S(2)}) %collective-permute-start.2) | collective-permute-done | bytes 196640 | tf_op jit(solution)/shard_map/ppermute | solution.py:30
  34.3 2.1 %collective-permute-start.3 = (f32[256,128]{1,0:T(8,128)}, f32[256,128]{1,0:T(8,128)S(1)}, u32[]{:S(2)}, u32[]{:S(2)}) collective-permute-start(f32[256,128]{1,0:T(8,128)} %pad_maximum_fusion.4), channel_id=1, source_target_pairs={{0,8},{1,9},{2,10},{3,11},{4,12},{5,13},{6,14},{7,15},{8,0},{9,1},... | collective-permute-start | bytes 393224 | tf_op jit(solution)/shard_map/ppermute | solution.py:30
  36.4 3.2 %collective-permute-done.3 = f32[256,128]{1,0:T(8,128)S(1)} collective-permute-done((f32[256,128]{1,0:T(8,128)}, f32[256,128]{1,0:T(8,128)S(1)}, u32[]{:S(2)}, u32[]{:S(2)}) %collective-permute-start.3) | collective-permute-done | bytes 131104 | tf_op jit(solution)/shard_map/ppermute | solution.py:30
  41.6 3.1 %collective-permute-start.4 = (f32[128,128]{1,0:T(8,128)S(1)}, f32[128,128]{1,0:T(8,128)S(1)}, u32[]{:S(2)}, u32[]{:S(2)}) collective-permute-start(f32[128,128]{1,0:T(8,128)S(1)} %slice_subtract_fusion), channel_id=1, source_target_pairs={{0,16},{1,17},{2,18},{3,19},{4,20},{5,21},{6,22},{7,23},{8,24},{9,... | collective-permute-start | bytes 196616 | tf_op jit(solution)/shard_map/ppermute | solution.py:30
  44.7 2.2 %collective-permute-done.4 = f32[128,128]{1,0:T(8,128)S(1)} collective-permute-done((f32[128,128]{1,0:T(8,128)S(1)}, f32[128,128]{1,0:T(8,128)S(1)}, u32[]{:S(2)}, u32[]{:S(2)}) %collective-permute-start.4) | collective-permute-done | bytes 65568 | tf_op jit(solution)/shard_map/ppermute | solution.py:30
  48.0 1.1 %fusion.33 = f32[128,128]{1,0:T(8,128)S(1)} fusion(f32[128,128]{1,0:T(8,128)S(1)} %fusion.35, f32[7,128,128]{2,1,0:T(8,128)} %param.12, s32[]{:T(128)S(6)} %select_n.188), kind=kOutput, calls=%fused_computation.50 | convolution fusion | flops 12582912 | bytes 196612 | tf_op jit(solution)/shard_map/dot_general | solution.py:10
  49.1 1.1 %convolution_subtract_fusion.1 = f32[128,128]{1,0:T(8,128)S(1)} fusion(f32[128,128]{1,0:T(8,128)S(1)} %fusion.15, f32[128,128]{1,0:T(8,128)S(1)} %fusion.33, f32[10,128,128]{2,1,0:T(8,128)} %param.13, s32[]{:T(128)S(6)} %select_n.198), kind=kOutput, calls=%fused_computation.1 | convolution fusion | flops 12599296 | bytes 262148 | tf_op jit(solution)/shard_map/dot_general | solution.py:10
  52.4 1.1 %fusion = f32[128,128]{1,0:T(8,128)S(1)} fusion(f32[128,128]{1,0:T(8,128)S(1)} %fusion.27, f32[128,128]{1,0:T(8,128)S(1)} %fusion.17, f32[128,128]{1,0:T(8,128)S(1)} %fusion.33, f32[10,128,128]{2,1,0:T(8,128)} %param.13, s32[]{:T(128)S(6)} %select_n.196), kind=kOutput, calls=%fused_computation.3 | convolution fusion | flops 12615680 | bytes 327684 | tf_op jit(solution)/shard_map/dot_general | solution.py:10
  54.6 1.9 %collective-permute-start.5 = (f32[384,128]{1,0:T(8,128)S(1)}, f32[384,128]{1,0:T(8,128)S(1)}, u32[]{:S(2)}, u32[]{:S(2)}) collective-permute-start(f32[384,128]{1,0:T(8,128)S(1)} %pad_maximum_fusion.2), channel_id=1, source_target_pairs={{0,2},{1,5},{2,0},{3,7},{4,6},{5,1},{6,4},{7,3},{8,10},{9,13},{10,... | collective-permute-start | bytes 589832 | tf_op jit(solution)/shard_map/ppermute | solution.py:30
  56.5 3.8 %collective-permute-done.5 = f32[384,128]{1,0:T(8,128)S(1)} collective-permute-done((f32[384,128]{1,0:T(8,128)S(1)}, f32[384,128]{1,0:T(8,128)S(1)}, u32[]{:S(2)}, u32[]{:S(2)}) %collective-permute-start.5) | collective-permute-done | bytes 196640 | tf_op jit(solution)/shard_map/ppermute | solution.py:30
  61.9 1.9 %collective-permute-start.7 = (f32[1,128,128]{2,1,0:T(8,128)}, f32[1,128,128]{2,1,0:T(8,128)}, u32[]{:S(2)}, u32[]{:S(2)}) collective-permute-start(f32[1,128,128]{2,1,0:T(8,128)} %get-tuple-element.9), channel_id=1, source_target_pairs={{0,8},{1,9},{2,10},{3,11},{4,12},{5,13},{6,14},{7,15},{8,0},{9,1},... | collective-permute-start | bytes 196616 | tf_op jit(solution)/shard_map/ppermute | solution.py:30
  63.9 2.5 %collective-permute-done.7 = f32[1,128,128]{2,1,0:T(8,128)} collective-permute-done((f32[1,128,128]{2,1,0:T(8,128)}, f32[1,128,128]{2,1,0:T(8,128)}, u32[]{:S(2)}, u32[]{:S(2)}) %collective-permute-start.7) | collective-permute-done | bytes 65568 | tf_op jit(solution)/shard_map/ppermute | solution.py:30
  67.5 1.5 %pad_maximum_fusion.3 = f32[3,128,128]{2,1,0:T(8,128)} fusion(f32[2,128,128]{2,1,0:T(8,128)S(1)} %maximum_select_fusion.1, f32[1,128,128]{2,1,0:T(8,128)} %get-tuple-element.8), kind=kLoop, calls=%fused_computation.26 | loop fusion | flops 49152 | bytes 393216 | tf_op jit(solution)/shard_map/concatenate | solution.py:144
  69.0 3.1 %collective-permute-start.8 = (f32[3,128,128]{2,1,0:T(8,128)}, f32[3,128,128]{2,1,0:T(8,128)}, u32[]{:S(2)}, u32[]{:S(2)}) collective-permute-start(f32[3,128,128]{2,1,0:T(8,128)} %pad_maximum_fusion.3), channel_id=1, source_target_pairs={{0,16},{1,17},{2,18},{3,19},{4,20},{5,21},{6,22},{7,23},{8,24},{9,... | collective-permute-start | bytes 589832 | tf_op jit(solution)/shard_map/ppermute | solution.py:30
  72.1 1.2 %broadcast_select_fusion = f32[384,2,128]{2,1,0:T(2,128)S(1)} fusion(pred[2]{0:T(512)(128)(4,1)S(1)} %iota_compare_fusion.3, f32[384,128]{1,0:T(8,128)} %copy-done.5, f32[384,128]{1,0:T(8,128)S(1)} %pad_maximum_fusion.2), kind=kLoop, calls=%fused_computation.20 | loop fusion | flops 98304 | bytes 786434 | tf_op jit(solution)/shard_map/jit(_where)/select_n | solution.py:130
  73.2 1.2 %broadcast_in_dim.112 = f32[384,2,2,128]{3,2,1,0:T(2,128)} broadcast(f32[384,2,128]{2,1,0:T(2,128)S(1)} %broadcast_select_fusion), dimensions={0,1,3} | broadcast | bytes 1179648 | tf_op jit(solution)/shard_map/jit(_where)/broadcast_in_dim | solution.py:133
  74.4 2.7 %broadcast_in_dim.113 = f32[384,512]{1,0:T(8,128)} reshape(f32[384,2,2,128]{3,2,1,0:T(2,128)} %broadcast_in_dim.112) | data formatting | bytes 1572864 | tf_op jit(solution)/shard_map/jit(_where)/broadcast_in_dim | solution.py:133
  77.1 2.1 %collective-permute-done.8 = f32[3,128,128]{2,1,0:T(8,128)} collective-permute-done((f32[3,128,128]{2,1,0:T(8,128)}, f32[3,128,128]{2,1,0:T(8,128)}, u32[]{:S(2)}, u32[]{:S(2)}) %collective-permute-start.8) | collective-permute-done | bytes 196640 | tf_op jit(solution)/shard_map/ppermute | solution.py:30
  81.0 1.6 %pad_maximum_fusion = f32[7,128,128]{2,1,0:T(8,128)} fusion(f32[4,128,128]{2,1,0:T(8,128)S(1)} %maximum_select_fusion, f32[2,128,128]{2,1,0:T(8,128)S(1)} %maximum_select_fusion.2, f32[1,128,128]{2,1,0:T(8,128)} %get-tuple-element.7), kind=kLoop, calls=%fused_computation.15 | loop fusion | flops 229376 | bytes 917504 | tf_op jit(solution)/shard_map/concatenate | solution.py:158
  82.6 1.3 %copy.12 = f32[384,2,128]{2,1,0:T(2,128)S(1)} copy(f32[384,2,128]{2,0,1:T(8,128)} %bitcast.18) | data formatting | bytes 786432 | tf_op jit(solution)/shard_map/jit(_where)/broadcast_in_dim | solution.py:133
  83.9 1.2 %broadcast_in_dim.118 = f32[384,2,2,128]{3,2,1,0:T(2,128)} broadcast(f32[384,2,128]{2,1,0:T(2,128)S(1)} %copy.12), dimensions={0,1,3} | broadcast | bytes 1179648 | tf_op jit(solution)/shard_map/jit(_where)/broadcast_in_dim | solution.py:133
  85.1 2.7 %broadcast_in_dim.119 = f32[384,512]{1,0:T(8,128)} reshape(f32[384,2,2,128]{3,2,1,0:T(2,128)} %broadcast_in_dim.118) | data formatting | bytes 1572864 | tf_op jit(solution)/shard_map/jit(_where)/broadcast_in_dim | solution.py:133
  87.8 3.0 %convolution_subtract_fusion = f32[512,512]{1,0:T(8,128)S(1)} fusion(f32[512,512]{1,0:T(8,128)} %copy-done.1, f32[384,512]{1,0:T(8,128)} %copy-done.2, f32[384,512]{1,0:T(8,128)} %broadcast_in_dim.113, f32[384,512]{1,0:T(8,128)} %broadcast_in_dim.119, pred[512]{0:T(512)(128)(4,1)S(1)} %broadcast_in_dim.103), kind=kOutput, calls=%fused_computation | convolution fusion | flops 604438528 | bytes 4456960 | tf_op jit(solution)/shard_map/dot_general | solution.py:10
  90.7 3.2 %fusion.1 = f32[512,512]{1,0:T(8,128)} fusion(f32[512,512]{1,0:T(8,128)S(1)} %convolution_subtract_fusion, f32[4,512,512]{2,1,0:T(8,128)} %param.9, s32[]{:T(128)S(6)} %select_n.169), kind=kOutput, calls=%fused_computation.4 | convolution fusion | flops 805306368 | bytes 3145732 | tf_op jit(solution)/shard_map/dot_general | solution.py:10
  (50 shorter events, 21.9 us)
Async XLA Ops:
  0.6 3.5 %copy-start = (f32[4,384,512]{2,1,0:T(8,128)S(1)}, f32[4,384,512]{2,1,0:T(8,128)}, u32[]{:S(2)}) copy-start(f32[4,384,512]{2,1,0:T(8,128)} %param.10) | copy-start | bytes 9437188
  4.2 1.0 %copy-start.1 = (f32[512,512]{1,0:T(8,128)}, f32[512,512]{1,0:T(8,128)S(1)}, u32[]{:S(2)}) copy-start(f32[512,512]{1,0:T(8,128)S(1)} %fusion.3) | copy-start | bytes 3145732
  5.1 0.9 copy-start.2
  13.2 2.1 %collective-permute-start = (f32[2,384,128]{2,1,0:T(8,128)}, f32[2,384,128]{2,1,0:T(8,128)}, u32[]{:S(2)}, u32[]{:S(2)}) collective-permute-start(f32[2,384,128]{2,1,0:T(8,128)} %bitcast.83), channel_id=1, source_target_pairs={{0,1},{1,0},{2,3},{3,2},{4,5},{5,4},{6,7},{7,6},{8,9},{9,8},{10,11... | collective-permute-start | bytes 1179656 | tf_op jit(solution)/shard_map/ppermute | solution.py:30
  16.5 0.7 copy-start.3
  17.3 6.6 %collective-permute-start.1 = (f32[384,128]{1,0:T(8,128)S(1)}, f32[384,128]{1,0:T(8,128)S(1)}, u32[]{:S(2)}, u32[]{:S(2)}) collective-permute-start(f32[384,128]{1,0:T(8,128)S(1)} %dynamic-slice_bitcast_fusion), channel_id=1, source_target_pairs={{0,2},{1,5},{2,0},{3,7},{4,6},{5,1},{6,4},{7,3},{8,10},{9,13},{10,... | collective-permute-start | bytes 589832 | tf_op jit(solution)/shard_map/ppermute | solution.py:30
  24.8 5.8 %collective-permute-start.2 = (f32[384,128]{1,0:T(8,128)S(1)}, f32[384,128]{1,0:T(8,128)S(1)}, u32[]{:S(2)}, u32[]{:S(2)}) collective-permute-start(f32[384,128]{1,0:T(8,128)S(1)} %bitcast_add_fusion), channel_id=1, source_target_pairs={{0,4},{1,3},{2,6},{3,1},{4,0},{5,7},{6,2},{7,5},{8,12},{9,11},{10,... | collective-permute-start | bytes 589832 | tf_op jit(solution)/shard_map/ppermute | solution.py:30
  34.3 5.2 %collective-permute-start.3 = (f32[256,128]{1,0:T(8,128)}, f32[256,128]{1,0:T(8,128)S(1)}, u32[]{:S(2)}, u32[]{:S(2)}) collective-permute-start(f32[256,128]{1,0:T(8,128)} %pad_maximum_fusion.4), channel_id=1, source_target_pairs={{0,8},{1,9},{2,10},{3,11},{4,12},{5,13},{6,14},{7,15},{8,0},{9,1},... | collective-permute-start | bytes 393224 | tf_op jit(solution)/shard_map/ppermute | solution.py:30
  41.6 5.3 %collective-permute-start.4 = (f32[128,128]{1,0:T(8,128)S(1)}, f32[128,128]{1,0:T(8,128)S(1)}, u32[]{:S(2)}, u32[]{:S(2)}) collective-permute-start(f32[128,128]{1,0:T(8,128)S(1)} %slice_subtract_fusion), channel_id=1, source_target_pairs={{0,16},{1,17},{2,18},{3,19},{4,20},{5,21},{6,22},{7,23},{8,24},{9,... | collective-permute-start | bytes 196616 | tf_op jit(solution)/shard_map/ppermute | solution.py:30
  54.6 5.7 %collective-permute-start.5 = (f32[384,128]{1,0:T(8,128)S(1)}, f32[384,128]{1,0:T(8,128)S(1)}, u32[]{:S(2)}, u32[]{:S(2)}) collective-permute-start(f32[384,128]{1,0:T(8,128)S(1)} %pad_maximum_fusion.2), channel_id=1, source_target_pairs={{0,2},{1,5},{2,0},{3,7},{4,6},{5,1},{6,4},{7,3},{8,10},{9,13},{10,... | collective-permute-start | bytes 589832 | tf_op jit(solution)/shard_map/ppermute | solution.py:30
  60.4 3.6 %copy-start.5 = (f32[384,128]{1,0:T(8,128)}, f32[384,128]{1,0:T(8,128)S(1)}, u32[]{:S(2)}) copy-start(f32[384,128]{1,0:T(8,128)S(1)} %collective-permute-done.5) | copy-start | bytes 589828
  60.5 0.8 copy-start.4
  61.9 4.6 %collective-permute-start.7 = (f32[1,128,128]{2,1,0:T(8,128)}, f32[1,128,128]{2,1,0:T(8,128)}, u32[]{:S(2)}, u32[]{:S(2)}) collective-permute-start(f32[1,128,128]{2,1,0:T(8,128)} %get-tuple-element.9), channel_id=1, source_target_pairs={{0,8},{1,9},{2,10},{3,11},{4,12},{5,13},{6,14},{7,15},{8,0},{9,1},... | collective-permute-start | bytes 196616 | tf_op jit(solution)/shard_map/ppermute | solution.py:30
  63.9 18.7 %collective-permute-start.6 = (f32[2,384,128]{2,1,0:T(8,128)}, f32[2,384,128]{2,1,0:T(8,128)}, u32[]{:S(2)}, u32[]{:S(2)}) collective-permute-start(f32[2,384,128]{2,1,0:T(8,128)} %copy-done.4), channel_id=1, source_target_pairs={{0,1},{1,0},{2,3},{3,2},{4,5},{5,4},{6,7},{7,6},{8,9},{9,8},{10,11... | collective-permute-start | bytes 1179656 | tf_op jit(solution)/shard_map/ppermute | solution.py:30
  66.5 14.5 %copy-start.6 = (f32[1,128,128]{2,1,0:T(8,128)S(1)}, f32[1,128,128]{2,1,0:T(8,128)}, u32[]{:S(2)}) copy-start(f32[1,128,128]{2,1,0:T(8,128)} %get-tuple-element.8) | copy-start | bytes 196612
  69.0 10.2 %collective-permute-start.8 = (f32[3,128,128]{2,1,0:T(8,128)}, f32[3,128,128]{2,1,0:T(8,128)}, u32[]{:S(2)}, u32[]{:S(2)}) collective-permute-start(f32[3,128,128]{2,1,0:T(8,128)} %pad_maximum_fusion.3), channel_id=1, source_target_pairs={{0,16},{1,17},{2,18},{3,19},{4,20},{5,21},{6,22},{7,23},{8,24},{9,... | collective-permute-start | bytes 589832 | tf_op jit(solution)/shard_map/ppermute | solution.py:30

commit v2 on v0

v2 whole, which is shorter than its diff:
```python
import functools

import jax
import jax.numpy as jnp
from jax import lax
from jax.experimental import pallas as pl
from jax.experimental.pallas import tpu as pltpu
from jax.sharding import PartitionSpec as P

F32, BF16 = jnp.float32, jnp.bfloat16
high = lax.Precision.HIGH


def dot(left, right):
    return jnp.dot(left, right, preferred_element_type=F32)


def dot_high(left, right):
    return jnp.dot(left, right, precision=high, preferred_element_type=F32)


def split(value):
    hi = value.astype(BF16)
    return hi, (value - hi.astype(F32)).astype(BF16)


def dot_split(left_hi, left_lo, right):
    hi, lo = split(right)
    return dot(left_hi, hi) + (dot(left_hi, lo) + dot(left_lo, hi))


def lanes(number, width):
    return pl.ds(pl.multiple_of(number * width, width), width)


class Plan:
    def __init__(self, leaf_count, group_count, panel_count, width):
        self.width = width
        self.levels = (panel_count + 1).bit_length() - 1
        self.bottoms = 2 ** (self.levels - 1)
        self.leaf_count, self.group_count = leaf_count, group_count
        self.sharers = leaf_count // self.bottoms

    def here(self):
        leaf, group = lax.axis_index("leaf"), lax.axis_index("rhs")
        return leaf, leaf // self.sharers, group % 2, group // 2

    def panel(self, place, level, flip=0):
        depth = self.levels - 1 - level
        return 2**depth - 1 + ((place >> level) ^ flip)

    def pair(self, place, below, above, flip=0):
        depth = self.levels - 1 - below
        before = sum(d * 2**d for d in range(depth))
        return before + ((place >> below) ^ flip) * depth + (above - below - 1)

    def swap(self, value, partner):
        pairs = []
        for leaf in range(self.leaf_count):
            for group in range(self.group_count):
                to_leaf, to_group = partner(leaf, group)
                pairs.append((leaf * self.group_count + group, to_leaf * self.group_count + to_group))
        return lax.ppermute(value, ("leaf", "rhs"), pairs)

    def swap_rhs(self, value, bit):
        return self.swap(value, lambda leaf, group: (leaf, group ^ bit))

    def swap_leaf(self, value, bit):
        return self.swap(value, lambda leaf, group: (leaf ^ bit, group))


def lift_kernel(plan, order, width, rhs, inv, coupling, rows, sent, rhs_own, lifted, inv_hi, inv_lo,
                perm_hi, perm_lo, rhs_buf, inv_buf, coup_buf, row_buf, sems):
    _, _, core, half = plan.here()
    block = half * 2 + core
    path = coupling.shape[1]
    copies = [
        pltpu.make_async_copy(rows.at[pl.ds(block, 1)], row_buf, sems.at[0]),
        pltpu.make_async_copy(coupling.at[block], coup_buf, sems.at[1]),
    ]
    for number, side in enumerate((1 - half, half)):
        copies.append(pltpu.make_async_copy(
            rhs.at[:, lanes(side * 2 + 1 - core, width)],
            rhs_buf.at[:, pl.ds(number * width, width)], sems.at[2 + number]))
    copies.append(pltpu.make_async_copy(inv.at[block], inv_buf, sems.at[4]))
    for number, side in enumerate((1 - half, half)):
        copies.append(pltpu.make_async_copy(
            rhs.at[:, lanes(side * 2 + core, width)],
            rhs_own.at[:, pl.ds(number * width, width)], sems.at[5 + number]))
    for copy in copies:
        copy.start()
    copies[0].wait()
    chosen = (lax.broadcasted_iota(jnp.int32, (path, path), 0) == row_buf[...]).astype(BF16)
    copies[1].wait()
    coup_hi, coup_lo = split(coup_buf[...])
    perm_hi[...] = dot(chosen, coup_hi).astype(BF16)
    perm_lo[...] = dot(chosen, coup_lo).astype(BF16)
    copies[2].wait()
    copies[3].wait()
    copies[4].wait()
    hi, lo = split(inv_buf[...])
    inv_hi[...] = hi
    inv_lo[...] = lo
    result = dot_split(hi, lo, rhs_buf[...])
    lifted[...] = result
    terms = dot_split(perm_hi[...], perm_lo[...], result)
    sent[0] = -terms[:, :width]
    sent[1] = -terms[:, width:]
    copies[5].wait()
    copies[6].wait()


def own_kernel(plan, width, rhs_own, inv_hi, inv_lo, perm_hi, perm_lo, top, own, lifted):
    leaf, place, _, _ = plan.here()
    result = dot_split(inv_hi[...], inv_lo[...], rhs_own[...])
    lifted[...] = result
    terms = dot_split(perm_hi[...], perm_lo[...], result)
    own[0] = -terms[:, :width]
    for level in range(plan.levels):
        rows = pl.ds(level * plan.width, plan.width)
        panel = plan.panel(place, level)
        share = top[lanes(panel, plan.width), :]
        counts = leaf % (plan.sharers * 2**level) == 0
        share = share * jnp.where(counts, 1.0, 0.0)
        own[1, rows] = share - terms[level * plan.width : (level + 1) * plan.width, width:]


def ready_kernel(top_inv, top_coup, inv, coup, inv_t, coup_t):
    for number in range(top_inv.shape[0]):
        inv[number] = top_inv[number]
        inv_t[number] = top_inv[number].T
    for number in range(top_coup.shape[0]):
        coup[number] = top_coup[number]
        coup_t[number] = top_coup[number].T


def turn_kernel(inv_hi, inv_lo, perm_hi, perm_lo, inv_hi_t, inv_lo_t, perm_hi_t, perm_lo_t):
    inv_hi_t[...] = inv_hi[...].T
    inv_lo_t[...] = inv_lo[...].T
    perm_hi_t[...] = perm_hi[...].T
    perm_lo_t[...] = perm_lo[...].T


def climb_kernel(plan, level, value, came, inv, coup, forward, rest):
    _, place, _, _ = plan.here()
    width = plan.width
    above = plan.levels - 1 - level
    result = dot_high(inv[plan.panel(place, level)], value[:width] + came[:width])
    forward[...] = result
    pairs = coup[pl.ds(plan.pair(place, level, level + 1), above)]
    change = dot_high(pairs.reshape(above * width, width), result)
    rest[...] = value[width:] + came[width:] - change


def descend_kernel(plan, *refs):
    levels, width = plan.levels, plan.width
    value, came, inv, inv_t, coup_t = refs[:5]
    forwards = refs[5 : 5 + levels - 1]
    solved, root = refs[5 + levels - 1 :]
    _, place, _, _ = plan.here()
    top = dot_high(inv[0], value[...] + came[...])
    root[...] = top
    found = [None] * levels
    for level in reversed(range(levels)):
        total = top if level == levels - 1 else forwards[level][...]
        for above in reversed(range(level + 1, levels)):
            total = total - dot_high(coup_t[plan.pair(place, level, above)], found[above])
        found[level] = dot_high(inv_t[plan.panel(place, level)], total)
        solved[pl.ds(level * width, width), :] = found[level]


def settle_kernel(plan, count, sides, fresh, *refs):
    refs = list(refs)
    parts = [refs.pop(0) for _ in range(count)]
    lifted, inv_hi_t, inv_lo_t, perm_hi_t, perm_lo_t = refs[:5]
    refs = refs[5:]
    if not fresh:
        refs = refs[1:]
    out, buffer, sems = refs
    _, _, core, half = plan.here()
    width = buffer.shape[2]
    for number, (part, (far, other)) in enumerate(zip(parts, sides)):
        column = 0 if far else width
        group = (1 - half if far else half) * 2 + (1 - core if other else core)
        inner = lifted[:, column : column + width] - dot_split(perm_hi_t[...], perm_lo_t[...], part[...])
        buffer[number] = dot_split(inv_hi_t[...], inv_lo_t[...], inner)
        pltpu.make_async_copy(buffer.at[number], out.at[:, lanes(group, width)], sems.at[number]).start()
    for number, (far, other) in enumerate(sides):
        group = (1 - half if far else half) * 2 + (1 - core if other else core)
        pltpu.make_async_copy(buffer.at[number], out.at[:, lanes(group, width)], sems.at[number]).wait()


def stack_place(step, level, flip):
    if level == step:
        return 2 ** (step + 1) - 2
    half = 2 ** (step - 1 - level)
    if flip < half:
        return stack_place(step - 1, level, flip)
    return 2**step - 1 + stack_place(step - 1, level, flip - half)


def top_kernel(plan, solved, inv_t, coup_t, *refs):
    levels, width = plan.levels, plan.width
    stacks, out = refs[:-1], refs[-1]
    _, place, _, _ = plan.here()
    found = {}
    for level in reversed(range(levels)):
        for flip in range(2 ** (levels - 1 - level)):
            if flip == 0:
                result = solved[pl.ds(level * width, width), :]
            else:
                step = flip.bit_length() - 1 + level
                offset = stack_place(step, level, flip - 2 ** (step - level))
                total = stacks[step][offset]
                for above in reversed(range(level + 1, levels)):
                    total = total - dot_high(
                        coup_t[plan.pair(place, level, above, flip)], found[above, flip >> (above - level)])
                result = dot_high(inv_t[plan.panel(place, level, flip)], total)
            found[level, flip] = result
            out[lanes(plan.panel(place, level, flip), width), :] = result


VMEM_SPEC = pl.BlockSpec(memory_space=pltpu.VMEM)
HBM_SPEC = pl.BlockSpec(memory_space=pltpu.HBM)
ANY_SPEC = pl.BlockSpec(memory_space=pl.ANY)


def call(kernel, outs, args, flops=0, scratch=(), anys=(), alias=None, name=None, after=(), after_hbm=()):
    size = sum(a.size * a.dtype.itemsize for a in args)
    after_hbm = [pltpu.with_memory_space_constraint(a, pltpu.HBM) for a in after_hbm]
    after_specs = [ANY_SPEC] * len(after) + [HBM_SPEC] * len(after_hbm)
    after = list(after) + after_hbm
    count = len(args)

    def body(*refs):
        kernel(*refs[:count], *refs[count + len(after) :])

    specs = [HBM_SPEC if number in anys else VMEM_SPEC for number in range(count)]
    args = [pltpu.with_memory_space_constraint(a, pltpu.HBM if number in anys else pltpu.VMEM)
            for number, a in enumerate(args)]
    return pl.pallas_call(
        body,
        out_shape=[shape for shape, _ in outs],
        in_specs=specs + after_specs,
        out_specs=[spec for _, spec in outs],
        scratch_shapes=list(scratch),
        input_output_aliases=alias or {},
        compiler_params=pltpu.CompilerParams(vmem_limit_bytes=24 * 2**20),
        cost_estimate=pl.CostEstimate(flops=flops, bytes_accessed=size, transcendentals=0),
        name=name,
    )(*args, *after)


def inside(shape, dtype=F32):
    return (pltpu.VMEM(shape, dtype), VMEM_SPEC)


def per_device(rhs_in, rhs_top, leaf_inv, leaf_coupling, coupling_rows, top_inv, top_coupling):
    block_count, order, _ = leaf_inv.shape
    panel_count, width, _ = top_inv.shape
    columns = rhs_top.shape[1]
    path = coupling_rows.shape[1]
    plan = Plan(lax.axis_size("leaf"), lax.axis_size("rhs"), panel_count, width)
    levels = plan.levels
    assert plan.group_count == 4 and block_count == 4 and plan.sharers >= 2

    sent, rhs_own, lifted_other, inv_hi, inv_lo, perm_hi, perm_lo = call(
        functools.partial(lift_kernel, plan, order, columns),
        [inside((2, path, columns)), inside((order, 2 * columns)), inside((order, 2 * columns)),
         inside((order, order), BF16), inside((order, order), BF16),
         inside((path, order), BF16), inside((path, order), BF16)],
        [rhs_in, leaf_inv, leaf_coupling, coupling_rows],
        flops=3 * 2 * 2 * columns * order * (order + path),
        scratch=[pltpu.VMEM((order, 2 * columns), F32), pltpu.VMEM((order, order), F32),
                 pltpu.VMEM((path, order), F32), pltpu.VMEM((1, path), jnp.int32),
                 pltpu.SemaphoreType.DMA((7,))],
        anys=(0, 1, 2, 3), name="lift")
    came = plan.swap_rhs(sent, 1)
    own, lifted_own = call(
        functools.partial(own_kernel, plan, columns),
        [inside((2, path, columns)), inside((order, 2 * columns))],
        [rhs_own, inv_hi, inv_lo, perm_hi, perm_lo, rhs_top],
        flops=3 * 2 * 2 * columns * order * (order + path), name="own")
    far = own[0] + came[0]
    near = own[1] + came[1]
    inv, coup, inv_t, coup_t = call(
        ready_kernel,
        [inside(top_inv.shape), inside(top_coupling.shape), inside(top_inv.shape), inside(top_coupling.shape)],
        [top_inv, top_coupling], flops=10**9, name="ready", after=[far])
    value = near + plan.swap_rhs(far, 2)
    inv_hi_t, inv_lo_t, perm_hi_t, perm_lo_t = call(
        turn_kernel,
        [inside((order, order), BF16), inside((order, order), BF16),
         inside((order, path), BF16), inside((order, path), BF16)],
        [inv_hi, inv_lo, perm_hi, perm_lo], flops=10**9, name="turn", after=[value])
    bit = 1
    while bit < plan.sharers // 2:
        value = value + plan.swap_leaf(value, bit)
        bit *= 2
    came = plan.swap_leaf(value, bit)

    forwards, stacks = [], []
    known = None
    for level in range(levels - 1):
        forward, value = call(
            functools.partial(climb_kernel, plan, level),
            [inside((width, columns)), inside(((levels - 1 - level) * width, columns))],
            [value, came, inv, coup], flops=10**8, name="climb", after=[] if level else [perm_lo_t])
        bit = plan.sharers * 2**level
        came = plan.swap_leaf(value, bit)
        forwards.append(forward)
        known = forward[None] if known is None else jnp.concatenate([known, stacks[-1], forward[None]], 0)
        stacks.append(plan.swap_leaf(known, bit))
    solved, _ = call(
        functools.partial(descend_kernel, plan),
        [inside((path, columns)), inside((width, columns))],
        [value, came, inv, inv_t, coup_t] + forwards, flops=10**8, name="descend")

    far = plan.swap_rhs(solved, 2)
    cross = plan.swap_rhs(solved, 1)
    out_shape = pltpu.HBM((order, plan.group_count * columns), F32)
    work = 3 * 2 * columns * order * (order + path)

    def settle(parts, sides, lifted, out):
        fresh = out is None
        args = list(parts) + [lifted, inv_hi_t, inv_lo_t, perm_hi_t, perm_lo_t] + ([] if fresh else [out])
        count = len(args)
        return call(
            functools.partial(settle_kernel, plan, len(parts), sides, fresh),
            [(out_shape, HBM_SPEC)], args, flops=work * len(parts),
            scratch=[pltpu.VMEM((len(parts), order, columns), F32), pltpu.SemaphoreType.DMA((len(parts),))],
            anys=() if fresh else (count - 1,), alias={} if fresh else {count - 1: 0}, name="settle")[0]

    out = settle([solved], [(False, False)], lifted_own, None)
    out = settle([cross], [(False, True)], lifted_other, out)
    last = plan.swap_rhs(far, 1)
    out = settle([far], [(True, False)], lifted_own, out)
    out = settle([last], [(True, True)], lifted_other, out)
    top = call(
        functools.partial(top_kernel, plan),
        [(jax.ShapeDtypeStruct((panel_count * width, columns), F32), VMEM_SPEC)],
        [solved, inv_t, coup_t] + stacks, flops=10**8, name="top", after_hbm=[out])[0]
    return out, top


def solution(mesh):
    placed = (
        P(("leaf", "rhs"), None),
        P(None, "rhs"),
        P("leaf", None, None),
        P("leaf", None, None),
        P("leaf", None),
        P(),
        P(),
    )
    return jax.shard_map(
        per_device,
        mesh=mesh,
        in_specs=placed,
        out_specs=(P(("leaf", "rhs"), None), P(None, "rhs")),
        check_vma=False,
    )
```

time: 174 us -> 53.8 us (0.31)
  waiting for transfers between devices: 97.4 us -> 19.6 us
  matrix products: 33.6 us -> 0 us
  Pallas kernels: 0 us -> 18.2 us
  starting transfers between devices: 0.08 us -> 15 us
  between operations: 14.4 us -> 0.77 us
  local copies, waits for them, and re-layouts: 10.7 us -> 0.02 us
  blocking collectives: 9.2 us -> 0 us
  other arithmetic: 7.2 us -> 0.07 us
    psum x1 -> x0, waiting for transfers between devices: 71.4 us -> none  [per_device(): summed = lax.psum(placed, 'leaf')]
    dot_general x38 -> x0, matrix products: 33.6 us -> none  [the longest x34 20.4 us: matmul(): jnp.dot(left, right, precision=highest, preferred_element_type=jnp.float32)]
    reduce_scatter x1 -> x0, waiting for transfers between devices: 26 us -> none  [per_device(): lax.psum_scatter(path_terms, 'rhs', scatter_dimension=1, tiled=True)]
    ppermute x0 -> x10, waiting for transfers between devices: none -> 19.6 us  [swap(): return lax.ppermute(value, ('leaf', 'rhs'), pairs)]
    pallas_call x0 -> x12, Pallas kernels: none -> 18.2 us  [call(): pl.pallas_call(body, out_shape=[shape for shape, _ in outs], in_specs=spe...]
    ppermute x0 -> x10, starting transfers between devices: none -> 15 us  [swap(): return lax.ppermute(value, ('leaf', 'rhs'), pairs)]
    all_gather x1 -> x0, blocking collectives: 9.2 us -> none  [per_device(): full_path = lax.all_gather(path_solution, 'rhs', axis=1, tiled=True)]
    dynamic_update_slice x3 -> x0, local copies, waits for them, and re-layouts: 4.42 us -> none  [per_device(): placed = lax.dynamic_update_slice(placed, piece, (on_path[level], 0, 0))]
  transfers between devices with their start and end apart: 2 -> 10, of which waited for: 2 -> 6; matrix products, arithmetic and copies ran while one was open for 0% -> 0% of each run, Pallas kernels for 0% -> 20%
where the time goes in v2:
time: 53.8 us; the launch traced here: 53.7 us
  waiting for transfers between devices  19.6 us (36%)
  Pallas kernels  18.2 us (34%)
  starting transfers between devices  15 us (28%)
  between operations  0.77 us (1%)
    ppermute x10, waiting for transfers between devices, swap(): return lax.ppermute(value, ('leaf', 'rhs'), pairs)  19.6 us
    pallas_call x12, Pallas kernels, call(): pl.pallas_call(body, out_shape=[shape for shape, _ in outs], in_specs=spe...  18.2 us
    ppermute x10, starting transfers between devices, swap(): return lax.ppermute(value, ('leaf', 'rhs'), pairs)  15 us
  transfers between devices with their start and end apart: 10, of which 6 were waited for; matrix products, arithmetic and copies ran while one was open for 0% of the time, Pallas kernels for 20%

profile of v2, /device:TPU:0, one launch (start us, length us, event | category | flops | bytes accessed | tf_op | source)
XLA Modules:
  0.0 53.7 jit_solution(15550135671065922816)
XLA Ops:
  0.6 3.6 %lift.1 = (f32[2,384,128]{2,1,0:T(8,128)S(1)}, f32[512,256]{1,0:T(8,128)S(1)}, f32[512,256]{1,0:T(8,128)S(1)}, bf16[512,512]{1,0:T(8,128)(2,1)S(1)}, bf16[512,51...) custom-call(f32[512,512]{1,0:T(8,128)} %refs_0_.2, f32[4,512,512]{2,1,0:T(8,128)} %refs_1_.2, ...), custom_call_target="tpu_custom_call" | custom-call | flops 704643072 | bytes 8394752 | tf_op jit(solution)/shard_map/lift/pallas_call | solution.py:241
  4.2 0.0 copy-start.1
  4.2 0.0 copy-start.2
  4.3 0.5 collective-permute-start
  4.8 1.5 %own.1 = (f32[2,384,128]{2,1,0:T(8,128)S(1)}, f32[512,256]{1,0:T(8,128)S(1)}) custom-call(f32[512,256]{1,0:T(8,128)S(1)} %get-tuple-element.24.refs_0_, bf16[512,512]{1,0:T(8,128)(2,1)S(1)} %get-tuple-element.25.refs_1_.refs_0_, bf16[512,512]{1,0:T(8,128)(2,1)S(1)} %get-tuple-element.26.refs_2_.refs_1_, ...), custom_call_target="tpu_custom_call" | custom-call | flops 704643072 | bytes 2818048 | tf_op jit(solution)/shard_map/own/pallas_call | solution.py:241
  6.3 2.7 %collective-permute-start.1 = (f32[384,128]{1,0:T(8,128)S(1)}, f32[384,128]{1,0:T(8,128)S(1)}, u32[]{:S(2)}, u32[]{:S(2)}) collective-permute-start(f32[384,128]{1,0:T(8,128)S(1)} %fusion.refs_2_), channel_id=1, source_target_pairs={{0,2},{1,3},{2,0},{3,1},{4,6},{5,7},{6,4},{7,5},{8,10},{9,11},{10,... | collective-permute-start | bytes 589832 | tf_op jit(solution)/shard_map/ppermute | solution.py:63
  9.1 5.4 %collective-permute-done.1 = f32[384,128]{1,0:T(8,128)S(1)} collective-permute-done((f32[384,128]{1,0:T(8,128)S(1)}, f32[384,128]{1,0:T(8,128)S(1)}, u32[]{:S(2)}, u32[]{:S(2)}) %collective-permute-start.1) | collective-permute-done | bytes 196640 | tf_op jit(solution)/shard_map/ppermute | solution.py:63
  14.5 1.8 %collective-permute-start.2 = (f32[384,128]{1,0:T(8,128)S(1)}, f32[384,128]{1,0:T(8,128)S(1)}, u32[]{:S(2)}, u32[]{:S(2)}) collective-permute-start(f32[384,128]{1,0:T(8,128)S(1)} %fusion.2.refs_4_.refs_0_), channel_id=1, source_target_pairs={{0,4},{1,5},{2,6},{3,7},{4,0},{5,1},{6,2},{7,3},{8,12},{9,13},{10,... | collective-permute-start | bytes 589832 | tf_op jit(solution)/shard_map/ppermute | solution.py:63
  16.3 0.4 ready.1
  16.7 0.5 turn.1
  17.2 4.0 %collective-permute-done.2.refs_1_ = f32[384,128]{1,0:T(8,128)S(1)} collective-permute-done((f32[384,128]{1,0:T(8,128)S(1)}, f32[384,128]{1,0:T(8,128)S(1)}, u32[]{:S(2)}, u32[]{:S(2)}) %collective-permute-start.2) | collective-permute-done | bytes 196640 | tf_op jit(solution)/shard_map/ppermute | solution.py:63
  21.2 0.4 climb.2
  21.6 1.6 %collective-permute-start.3 = (f32[256,128]{1,0:T(8,128)S(1)}, f32[256,128]{1,0:T(8,128)S(1)}, u32[]{:S(2)}, u32[]{:S(2)}) collective-permute-start(f32[256,128]{1,0:T(8,128)S(1)} %get-tuple-element.34.refs_0_), channel_id=1, source_target_pairs={{0,8},{1,9},{2,10},{3,11},{4,12},{5,13},{6,14},{7,15},{8,0},{9,1},... | collective-permute-start | bytes 393224 | tf_op jit(solution)/shard_map/ppermute | solution.py:63
  23.2 3.5 %collective-permute-done.3.refs_1_ = f32[256,128]{1,0:T(8,128)S(1)} collective-permute-done((f32[256,128]{1,0:T(8,128)S(1)}, f32[256,128]{1,0:T(8,128)S(1)}, u32[]{:S(2)}, u32[]{:S(2)}) %collective-permute-start.3) | collective-permute-done | bytes 131104 | tf_op jit(solution)/shard_map/ppermute | solution.py:63
  26.6 0.3 climb.3
  27.0 2.6 %collective-permute-start.4 = (f32[128,128]{1,0:T(8,128)S(1)}, f32[128,128]{1,0:T(8,128)S(1)}, u32[]{:S(2)}, u32[]{:S(2)}) collective-permute-start(f32[128,128]{1,0:T(8,128)S(1)} %get-tuple-element.35.refs_0_), channel_id=1, source_target_pairs={{0,16},{1,17},{2,18},{3,19},{4,20},{5,21},{6,22},{7,23},{8,24},{9,... | collective-permute-start | bytes 196616 | tf_op jit(solution)/shard_map/ppermute | solution.py:63
  29.6 2.6 %collective-permute-done.4.refs_1_ = f32[128,128]{1,0:T(8,128)S(1)} collective-permute-done((f32[128,128]{1,0:T(8,128)S(1)}, f32[128,128]{1,0:T(8,128)S(1)}, u32[]{:S(2)}, u32[]{:S(2)}) %collective-permute-start.4) | collective-permute-done | bytes 65568 | tf_op jit(solution)/shard_map/ppermute | solution.py:63
  32.2 1.5 %descend.1 = (f32[384,128]{1,0:T(8,128)S(1)}, f32[128,128]{1,0:T(8,128)}) custom-call(f32[128,128]{1,0:T(8,128)S(1)} %get-tuple-element.35.refs_0_, f32[128,128]{1,0:T(8,128)S(1)} %collective-permute-done.4.refs_1_, f32[7,128,128]{2,1,0:T(8,128)S(1)} %get-tuple-element.31.refs_2_, f32[7,128,128]{2,1,0:T(8,128)S(1)} %get-tuple-element.36.refs_3_.refs_1_, ...), custom_call_target="tpu_custom_call" | custom-call | flops 100000000 | bytes 1835008 | tf_op jit(solution)/shard_map/descend/pallas_call | solution.py:241
  33.7 1.4 %collective-permute-start.5 = (f32[384,128]{1,0:T(8,128)S(1)}, f32[384,128]{1,0:T(8,128)S(1)}, u32[]{:S(2)}, u32[]{:S(2)}) collective-permute-start(f32[384,128]{1,0:T(8,128)S(1)} %get-tuple-element.40.refs_0_), channel_id=1, source_target_pairs={{0,2},{1,3},{2,0},{3,1},{4,6},{5,7},{6,4},{7,5},{8,10},{9,11},{10,... | collective-permute-start | bytes 589832 | tf_op jit(solution)/shard_map/ppermute | solution.py:63
  35.1 1.6 %collective-permute-start.8 = (f32[1,128,128]{2,1,0:T(8,128)S(1)}, f32[1,128,128]{2,1,0:T(8,128)S(1)}, u32[]{:S(2)}, u32[]{:S(2)}) collective-permute-start(f32[1,128,128]{2,1,0:T(8,128)S(1)} %bitcast.8), channel_id=1, source_target_pairs={{0,8},{1,9},{2,10},{3,11},{4,12},{5,13},{6,14},{7,15},{8,0},{9,1},... | collective-permute-start | bytes 196616 | tf_op jit(solution)/shard_map/ppermute | solution.py:63
  36.7 0.0 collective-permute-start.7
  36.7 2.7 %collective-permute-done.5.refs_0_ = f32[384,128]{1,0:T(8,128)S(1)} collective-permute-done((f32[384,128]{1,0:T(8,128)S(1)}, f32[384,128]{1,0:T(8,128)S(1)}, u32[]{:S(2)}, u32[]{:S(2)}) %collective-permute-start.5) | collective-permute-done | bytes 196640 | tf_op jit(solution)/shard_map/ppermute | solution.py:63
  39.4 0.0 collective-permute-start.6
  39.4 0.0 collective-permute-done.8.refs_3_
  39.4 2.8 %collective-permute-start.9 = (f32[3,128,128]{2,1,0:T(8,128)S(1)}, f32[3,128,128]{2,1,0:T(8,128)S(1)}, u32[]{:S(2)}, u32[]{:S(2)}) collective-permute-start(f32[3,128,128]{2,1,0:T(8,128)S(1)} %pad_maximum_fusion), channel_id=1, source_target_pairs={{0,16},{1,17},{2,18},{3,19},{4,20},{5,21},{6,22},{7,23},{8,24},{9,... | collective-permute-start | bytes 589832 | tf_op jit(solution)/shard_map/ppermute | solution.py:63
  42.2 2.0 %settle.4.refs_6_ = f32[512,512]{1,0:T(8,128)} custom-call(f32[384,128]{1,0:T(8,128)S(1)} %get-tuple-element.40.refs_0_, f32[512,256]{1,0:T(8,128)S(1)} %get-tuple-element.45.refs_1_, bf16[512,512]{1,0:T(8,128)(2,1)S(1)} %get-tuple-element.42.refs_2_, bf16[512,512]{1,0:T(8,128)(2,1)S(1)} %get-tuple-element.43.refs_3_, ...), custom_call_target="tpu_custom_call" | custom-call | flops 352321536 | bytes 2555904 | tf_op jit(solution)/shard_map/settle/pallas_call | solution.py:241
  44.3 0.0 collective-permute-done.7.refs_0_
  44.3 2.0 %settle.5.refs_6_ = f32[512,512]{1,0:T(8,128)} custom-call(f32[384,128]{1,0:T(8,128)S(1)} %collective-permute-done.7.refs_0_, f32[512,256]{1,0:T(8,128)S(1)} %get-tuple-element.41.refs_1_, bf16[512,512]{1,0:T(8,128)(2,1)S(1)} %get-tuple-element.42.refs_2_, bf16[512,512]{1,0:T(8,128)(2,1)S(1)} %get-tuple-element.43.refs_3_, ...), custom_call_target="tpu_custom_call", output_to_operand_aliasing={{}: (6, {})} | custom-call | flops 352321536 | bytes 3604480 | tf_op jit(solution)/shard_map/settle/pallas_call | solution.py:241
  46.3 2.0 %settle.6.refs_6_ = f32[512,512]{1,0:T(8,128)} custom-call(f32[384,128]{1,0:T(8,128)S(1)} %collective-permute-done.5.refs_0_, f32[512,256]{1,0:T(8,128)S(1)} %get-tuple-element.45.refs_1_, bf16[512,512]{1,0:T(8,128)(2,1)S(1)} %get-tuple-element.42.refs_2_, bf16[512,512]{1,0:T(8,128)(2,1)S(1)} %get-tuple-element.43.refs_3_, ...), custom_call_target="tpu_custom_call", output_to_operand_aliasing={{}: (6, {})} | custom-call | flops 352321536 | bytes 3604480 | tf_op jit(solution)/shard_map/settle/pallas_call | solution.py:241
  48.4 2.0 %settle.7.refs_5_ = f32[512,512]{1,0:T(8,128)} custom-call(f32[384,128]{1,0:T(8,128)S(1)} %collective-permute-done.6.refs_0_, f32[512,256]{1,0:T(8,128)S(1)} %get-tuple-element.41.refs_1_, bf16[512,512]{1,0:T(8,128)(2,1)S(1)} %get-tuple-element.42.refs_2_, bf16[512,512]{1,0:T(8,128)(2,1)S(1)} %get-tuple-element.43.refs_3_, ...), custom_call_target="tpu_custom_call", output_to_operand_aliasing={{}: (6, {})} | custom-call | flops 352321536 | bytes 3604480 | tf_op jit(solution)/shard_map/settle/pallas_call | solution.py:241
  50.4 1.4 %collective-permute-done.9.refs_4_ = f32[3,128,128]{2,1,0:T(8,128)S(1)} collective-permute-done((f32[3,128,128]{2,1,0:T(8,128)S(1)}, f32[3,128,128]{2,1,0:T(8,128)S(1)}, u32[]{:S(2)}, u32[]{:S(2)}) %collective-permute-start.9) | collective-permute-done | bytes 196640 | tf_op jit(solution)/shard_map/ppermute | solution.py:63
  51.9 1.8 %top.1 = f32[896,128]{1,0:T(8,128)} custom-call(f32[384,128]{1,0:T(8,128)S(1)} %get-tuple-element.40.refs_0_, f32[7,128,128]{2,1,0:T(8,128)S(1)} %get-tuple-element.36.refs_3_.refs_1_, f32[10,128,128]{2,1,0:T(8,128)S(1)} %get-tuple-element.37.refs_4_.refs_2_, f32[1,128,128]{2,1,0:T(8,128)S(1)} %collective-permute-done.8.refs_3_, ...), custom_call_target="tpu_custom_call" | custom-call | flops 100000000 | bytes 1572864 | tf_op jit(solution)/shard_map/top/pallas_call | solution.py:241
  (9 shorter events, 0.1 us)
Async XLA Ops:
  0.6 4.2 %copy-start = (f32[896,128]{1,0:T(8,128)S(1)}, f32[896,128]{1,0:T(8,128)}, u32[]{:S(2)}) copy-start(f32[896,128]{1,0:T(8,128)} %refs_5_.1) | copy-start | bytes 1376260
  4.2 12.1 %copy-start.1 = (f32[10,128,128]{2,1,0:T(8,128)S(1)}, f32[10,128,128]{2,1,0:T(8,128)}, u32[]{:S(2)}) copy-start(f32[10,128,128]{2,1,0:T(8,128)} %refs_1_.3) | copy-start | bytes 1966084
  4.2 12.1 %copy-start.2 = (f32[7,128,128]{2,1,0:T(8,128)S(1)}, f32[7,128,128]{2,1,0:T(8,128)}, u32[]{:S(2)}) copy-start(f32[7,128,128]{2,1,0:T(8,128)} %refs_0_.3) | copy-start | bytes 1376260
  4.3 2.0 %collective-permute-start = (f32[2,384,128]{2,1,0:T(8,128)S(1)}, f32[2,384,128]{2,1,0:T(8,128)S(1)}, u32[]{:S(2)}, u32[]{:S(2)}) collective-permute-start(f32[2,384,128]{2,1,0:T(8,128)S(1)} %get-tuple-element.30), channel_id=1, source_target_pairs={{0,1},{1,0},{2,3},{3,2},{4,5},{5,4},{6,7},{7,6},{8,9},{9,8},{10,11... | collective-permute-start | bytes 1179656 | tf_op jit(solution)/shard_map/ppermute | solution.py:63
  6.3 8.1 %collective-permute-start.1 = (f32[384,128]{1,0:T(8,128)S(1)}, f32[384,128]{1,0:T(8,128)S(1)}, u32[]{:S(2)}, u32[]{:S(2)}) collective-permute-start(f32[384,128]{1,0:T(8,128)S(1)} %fusion.refs_2_), channel_id=1, source_target_pairs={{0,2},{1,3},{2,0},{3,1},{4,6},{5,7},{6,4},{7,5},{8,10},{9,11},{10,... | collective-permute-start | bytes 589832 | tf_op jit(solution)/shard_map/ppermute | solution.py:63
  14.5 6.7 %collective-permute-start.2 = (f32[384,128]{1,0:T(8,128)S(1)}, f32[384,128]{1,0:T(8,128)S(1)}, u32[]{:S(2)}, u32[]{:S(2)}) collective-permute-start(f32[384,128]{1,0:T(8,128)S(1)} %fusion.2.refs_4_.refs_0_), channel_id=1, source_target_pairs={{0,4},{1,5},{2,6},{3,7},{4,0},{5,1},{6,2},{7,3},{8,12},{9,13},{10,... | collective-permute-start | bytes 589832 | tf_op jit(solution)/shard_map/ppermute | solution.py:63
  21.6 5.0 %collective-permute-start.3 = (f32[256,128]{1,0:T(8,128)S(1)}, f32[256,128]{1,0:T(8,128)S(1)}, u32[]{:S(2)}, u32[]{:S(2)}) collective-permute-start(f32[256,128]{1,0:T(8,128)S(1)} %get-tuple-element.34.refs_0_), channel_id=1, source_target_pairs={{0,8},{1,9},{2,10},{3,11},{4,12},{5,13},{6,14},{7,15},{8,0},{9,1},... | collective-permute-start | bytes 393224 | tf_op jit(solution)/shard_map/ppermute | solution.py:63
  27.0 5.2 %collective-permute-start.4 = (f32[128,128]{1,0:T(8,128)S(1)}, f32[128,128]{1,0:T(8,128)S(1)}, u32[]{:S(2)}, u32[]{:S(2)}) collective-permute-start(f32[128,128]{1,0:T(8,128)S(1)} %get-tuple-element.35.refs_0_), channel_id=1, source_target_pairs={{0,16},{1,17},{2,18},{3,19},{4,20},{5,21},{6,22},{7,23},{8,24},{9,... | collective-permute-start | bytes 196616 | tf_op jit(solution)/shard_map/ppermute | solution.py:63
  33.7 5.7 %collective-permute-start.5 = (f32[384,128]{1,0:T(8,128)S(1)}, f32[384,128]{1,0:T(8,128)S(1)}, u32[]{:S(2)}, u32[]{:S(2)}) collective-permute-start(f32[384,128]{1,0:T(8,128)S(1)} %get-tuple-element.40.refs_0_), channel_id=1, source_target_pairs={{0,2},{1,3},{2,0},{3,1},{4,6},{5,7},{6,4},{7,5},{8,10},{9,11},{10,... | collective-permute-start | bytes 589832 | tf_op jit(solution)/shard_map/ppermute | solution.py:63
  35.1 4.3 %collective-permute-start.8 = (f32[1,128,128]{2,1,0:T(8,128)S(1)}, f32[1,128,128]{2,1,0:T(8,128)S(1)}, u32[]{:S(2)}, u32[]{:S(2)}) collective-permute-start(f32[1,128,128]{2,1,0:T(8,128)S(1)} %bitcast.8), channel_id=1, source_target_pairs={{0,8},{1,9},{2,10},{3,11},{4,12},{5,13},{6,14},{7,15},{8,0},{9,1},... | collective-permute-start | bytes 196616 | tf_op jit(solution)/shard_map/ppermute | solution.py:63
  36.7 7.6 %collective-permute-start.7 = (f32[384,128]{1,0:T(8,128)S(1)}, f32[384,128]{1,0:T(8,128)S(1)}, u32[]{:S(2)}, u32[]{:S(2)}) collective-permute-start(f32[384,128]{1,0:T(8,128)S(1)} %get-tuple-element.40.refs_0_), channel_id=1, source_target_pairs={{0,1},{1,0},{2,3},{3,2},{4,5},{5,4},{6,7},{7,6},{8,9},{9,8},{10,11... | collective-permute-start | bytes 589832 | tf_op jit(solution)/shard_map/ppermute | solution.py:63
  39.4 9.0 %collective-permute-start.6 = (f32[384,128]{1,0:T(8,128)S(1)}, f32[384,128]{1,0:T(8,128)S(1)}, u32[]{:S(2)}, u32[]{:S(2)}) collective-permute-start(f32[384,128]{1,0:T(8,128)S(1)} %collective-permute-done.5.refs_0_), channel_id=1, source_target_pairs={{0,1},{1,0},{2,3},{3,2},{4,5},{5,4},{6,7},{7,6},{8,9},{9,8},{10,11... | collective-permute-start | bytes 589832 | tf_op jit(solution)/shard_map/ppermute | solution.py:63
  39.4 12.5 %collective-permute-start.9 = (f32[3,128,128]{2,1,0:T(8,128)S(1)}, f32[3,128,128]{2,1,0:T(8,128)S(1)}, u32[]{:S(2)}, u32[]{:S(2)}) collective-permute-start(f32[3,128,128]{2,1,0:T(8,128)S(1)} %pad_maximum_fusion), channel_id=1, source_target_pairs={{0,16},{1,17},{2,18},{3,19},{4,20},{5,21},{6,22},{7,23},{8,24},{9,... | collective-permute-start | bytes 589832 | tf_op jit(solution)/shard_map/ppermute | solution.py:63

commit v3 on v2

--- a/solution.py
+++ b/solution.py
@@ -125,20 +125,31 @@
         own[1, rows] = share - terms[level * plan.width : (level + 1) * plan.width, width:]
 
 
-def ready_kernel(top_inv, top_coup, inv, coup, inv_t, coup_t):
+def ready_kernel(levels, top_inv, top_coup, inv, coup, back_hi, back_lo):
+    width = top_inv.shape[1]
+    first = 0
     for number in range(top_inv.shape[0]):
+        depth = (number + 1).bit_length() - 1
         inv[number] = top_inv[number]
-        inv_t[number] = top_inv[number].T
-    for number in range(top_coup.shape[0]):
-        coup[number] = top_coup[number]
-        coup_t[number] = top_coup[number].T
-
-
-def turn_kernel(inv_hi, inv_lo, perm_hi, perm_lo, inv_hi_t, inv_lo_t, perm_hi_t, perm_lo_t):
-    inv_hi_t[...] = inv_hi[...].T
-    inv_lo_t[...] = inv_lo[...].T
-    perm_hi_t[...] = perm_hi[...].T
-    perm_lo_t[...] = perm_lo[...].T
+        turned = top_inv[number].T
+        back_hi[number, :, :width], back_lo[number, :, :width] = split(turned)
+        for step in range(depth):
+            pair = first + step
+            coup[pair] = top_coup[pair]
+            columns = pl.ds((step + 1) * width, width)
+            back_hi[number, :, columns], back_lo[number, :, columns] = split(
+                -dot_high(turned, top_coup[pair].T))
+        first += depth
+
+
+def turn_kernel(inv_hi, inv_lo, perm_hi, perm_lo, lifted_own, lifted_other, base_own, base_other, gain_hi, gain_lo, token):
+    hi, lo = inv_hi[...].T, inv_lo[...].T
+    turned_hi, turned_lo = perm_hi[...].T, perm_lo[...].T
+    gain = dot(hi, turned_hi) + (dot(hi, turned_lo) + dot(lo, turned_hi))
+    gain_hi[...], gain_lo[...] = split(gain)
+    base_own[...] = dot_split(hi, lo, lifted_own[...])
+    base_other[...] = dot_split(hi, lo, lifted_other[...])
+    token[...] = jnp.zeros_like(token)
 
 
 def climb_kernel(plan, level, value, came, inv, coup, forward, rest):
@@ -152,42 +163,51 @@
     rest[...] = value[width:] + came[width:] - change
 
 
+def backward(plan, back_hi, back_lo, panel, level, forward, above):
+    depth = plan.width * (plan.levels - level)
+    known = jnp.concatenate([forward] + above, 0) if above else forward
+    return dot_split(back_hi[panel, :, :depth], back_lo[panel, :, :depth], known)
+
+
 def descend_kernel(plan, *refs):
     levels, width = plan.levels, plan.width
-    value, came, inv, inv_t, coup_t = refs[:5]
+    value, came, inv, back_hi, back_lo = refs[:5]
     forwards = refs[5 : 5 + levels - 1]
-    solved, root = refs[5 + levels - 1 :]
+    solved = refs[5 + levels - 1]
     _, place, _, _ = plan.here()
     top = dot_high(inv[0], value[...] + came[...])
-    root[...] = top
-    found = [None] * levels
+    above = []
     for level in reversed(range(levels)):
-        total = top if level == levels - 1 else forwards[level][...]
-        for above in reversed(range(level + 1, levels)):
-            total = total - dot_high(coup_t[plan.pair(place, level, above)], found[above])
-        found[level] = dot_high(inv_t[plan.panel(place, level)], total)
-        solved[pl.ds(level * width, width), :] = found[level]
-
-
-def settle_kernel(plan, count, sides, fresh, *refs):
-    refs = list(refs)
-    parts = [refs.pop(0) for _ in range(count)]
-    lifted, inv_hi_t, inv_lo_t, perm_hi_t, perm_lo_t = refs[:5]
-    refs = refs[5:]
-    if not fresh:
-        refs = refs[1:]
-    out, buffer, sems = refs
+        forward = top if level == levels - 1 else forwards[level][...]
+        result = backward(plan, back_hi, back_lo, plan.panel(place, level), level, forward, above)
+        solved[pl.ds(level * width, width), :] = result
+        above = [result] + above
+
+
+def settled(base, gain_hi, gain_lo, part, column, width):
+    change = dot_split(gain_hi[...], gain_lo[...], part[...])
+    return base[:, column : column + width] - change
+
+
+def settle_kernel(width, column, part, base, gain_hi, gain_lo, out, token):
+    out[...] = settled(base, gain_hi, gain_lo, part, column, width)
+    token[...] = jnp.zeros_like(token)
+
+
+def last_kernel(plan, width, part, base, gain_hi, gain_lo, own, far, out, buffer, sems):
     _, _, core, half = plan.here()
-    width = buffer.shape[2]
-    for number, (part, (far, other)) in enumerate(zip(parts, sides)):
-        column = 0 if far else width
-        group = (1 - half if far else half) * 2 + (1 - core if other else core)
-        inner = lifted[:, column : column + width] - dot_split(perm_hi_t[...], perm_lo_t[...], part[...])
-        buffer[number] = dot_split(inv_hi_t[...], inv_lo_t[...], inner)
-        pltpu.make_async_copy(buffer.at[number], out.at[:, lanes(group, width)], sems.at[number]).start()
-    for number, (far, other) in enumerate(sides):
-        group = (1 - half if far else half) * 2 + (1 - core if other else core)
-        pltpu.make_async_copy(buffer.at[number], out.at[:, lanes(group, width)], sems.at[number]).wait()
+    groups = ((1 - half) * 2 + core, half * 2 + core, (1 - half) * 2 + 1 - core, half * 2 + 1 - core)
+    copies = [pltpu.make_async_copy(done, out.at[:, lanes(group, width)], sems.at[number])
+              for number, (done, group) in enumerate(zip((
+                  far, own, buffer.at[:, :width], buffer.at[:, width:]), groups))]
+    copies[0].start()
+    copies[1].start()
+    known = jnp.concatenate([part[0], part[1]], 1)
+    buffer[...] = base[...] - dot_split(gain_hi[...], gain_lo[...], known)
+    copies[2].start()
+    copies[3].start()
+    for copy in copies:
+        copy.wait()
 
 
 def stack_place(step, level, flip):
@@ -199,25 +219,23 @@
     return 2**step - 1 + stack_place(step - 1, level, flip - half)
 
 
-def top_kernel(plan, solved, inv_t, coup_t, *refs):
+def top_kernel(plan, solved, back_hi, back_lo, *refs):
     levels, width = plan.levels, plan.width
     stacks, out = refs[:-1], refs[-1]
     _, place, _, _ = plan.here()
     found = {}
     for level in reversed(range(levels)):
         for flip in range(2 ** (levels - 1 - level)):
+            panel = plan.panel(place, level, flip)
             if flip == 0:
                 result = solved[pl.ds(level * width, width), :]
             else:
                 step = flip.bit_length() - 1 + level
-                offset = stack_place(step, level, flip - 2 ** (step - level))
-                total = stacks[step][offset]
-                for above in reversed(range(level + 1, levels)):
-                    total = total - dot_high(
-                        coup_t[plan.pair(place, level, above, flip)], found[above, flip >> (above - level)])
-                result = dot_high(inv_t[plan.panel(place, level, flip)], total)
+                forward = stacks[step][stack_place(step, level, flip - 2 ** (step - level))]
+                above = [found[up, flip >> (up - level)] for up in range(level + 1, levels)]
+                result = backward(plan, back_hi, back_lo, panel, level, forward, above)
             found[level, flip] = result
-            out[lanes(plan.panel(place, level, flip), width), :] = result
+            out[lanes(panel, width), :] = result
 
 
 VMEM_SPEC = pl.BlockSpec(memory_space=pltpu.VMEM)
@@ -225,8 +243,7 @@
 ANY_SPEC = pl.BlockSpec(memory_space=pl.ANY)
 
 
-def call(kernel, outs, args, flops=0, scratch=(), anys=(), alias=None, name=None, after=(), after_hbm=()):
-    size = sum(a.size * a.dtype.itemsize for a in args)
+def call(kernel, outs, args, scratch=(), anys=(), name=None, after=(), after_hbm=(), flops=1000):
     after_hbm = [pltpu.with_memory_space_constraint(a, pltpu.HBM) for a in after_hbm]
     after_specs = [ANY_SPEC] * len(after) + [HBM_SPEC] * len(after_hbm)
     after = list(after) + after_hbm
@@ -244,9 +261,8 @@
         in_specs=specs + after_specs,
         out_specs=[spec for _, spec in outs],
         scratch_shapes=list(scratch),
-        input_output_aliases=alias or {},
         compiler_params=pltpu.CompilerParams(vmem_limit_bytes=24 * 2**20),
-        cost_estimate=pl.CostEstimate(flops=flops, bytes_accessed=size, transcendentals=0),
+        cost_estimate=pl.CostEstimate(flops=flops, bytes_accessed=1000, transcendentals=0),
         name=name,
     )(*args, *after)
 
@@ -270,7 +286,6 @@
          inside((order, order), BF16), inside((order, order), BF16),
          inside((path, order), BF16), inside((path, order), BF16)],
         [rhs_in, leaf_inv, leaf_coupling, coupling_rows],
-        flops=3 * 2 * 2 * columns * order * (order + path),
         scratch=[pltpu.VMEM((order, 2 * columns), F32), pltpu.VMEM((order, order), F32),
                  pltpu.VMEM((path, order), F32), pltpu.VMEM((1, path), jnp.int32),
                  pltpu.SemaphoreType.DMA((7,))],
@@ -279,67 +294,64 @@
     own, lifted_own = call(
         functools.partial(own_kernel, plan, columns),
         [inside((2, path, columns)), inside((order, 2 * columns))],
-        [rhs_own, inv_hi, inv_lo, perm_hi, perm_lo, rhs_top],
-        flops=3 * 2 * 2 * columns * order * (order + path), name="own")
+        [rhs_own, inv_hi, inv_lo, perm_hi, perm_lo, rhs_top], name="own")
     far = own[0] + came[0]
     near = own[1] + came[1]
-    inv, coup, inv_t, coup_t = call(
-        ready_kernel,
-        [inside(top_inv.shape), inside(top_coupling.shape), inside(top_inv.shape), inside(top_coupling.shape)],
-        [top_inv, top_coupling], flops=10**9, name="ready", after=[far])
-    value = near + plan.swap_rhs(far, 2)
-    inv_hi_t, inv_lo_t, perm_hi_t, perm_lo_t = call(
+    base_own, base_other, gain_hi, gain_lo, token = call(
         turn_kernel,
-        [inside((order, order), BF16), inside((order, order), BF16),
-         inside((order, path), BF16), inside((order, path), BF16)],
-        [inv_hi, inv_lo, perm_hi, perm_lo], flops=10**9, name="turn", after=[value])
+        [inside((order, 2 * columns)), inside((order, 2 * columns)),
+         inside((order, path), BF16), inside((order, path), BF16), inside((8, columns))],
+        [inv_hi, inv_lo, perm_hi, perm_lo, lifted_own, lifted_other], name="turn", after=[far])
+    value = near + plan.swap_rhs(far, 2) + token[:1]
+    backs = (panel_count, width, levels * width)
+    inv, coup, back_hi, back_lo = call(
+        functools.partial(ready_kernel, levels),
+        [inside(top_inv.shape), inside(top_coupling.shape), inside(backs, BF16), inside(backs, BF16)],
+        [top_inv, top_coupling], name="ready", after=[value])
     bit = 1
     while bit < plan.sharers // 2:
         value = value + plan.swap_leaf(value, bit)
         bit *= 2
     came = plan.swap_leaf(value, bit)
 
-    forwards, stacks = [], []
-    known = None
+    forwards, stacks, known = [], [], []
     for level in range(levels - 1):
         forward, value = call(
             functools.partial(climb_kernel, plan, level),
             [inside((width, columns)), inside(((levels - 1 - level) * width, columns))],
-            [value, came, inv, coup], flops=10**8, name="climb", after=[] if level else [perm_lo_t])
+            [value, came, inv, coup], name="climb")
         bit = plan.sharers * 2**level
         came = plan.swap_leaf(value, bit)
         forwards.append(forward)
-        known = forward[None] if known is None else jnp.concatenate([known, stacks[-1], forward[None]], 0)
-        stacks.append(plan.swap_leaf(known, bit))
-    solved, _ = call(
+        known = known + stacks[-1:] + [forward[None]]
+        stacks.append(plan.swap_leaf(jnp.concatenate(known, 0), bit))
+    solved = call(
         functools.partial(descend_kernel, plan),
-        [inside((path, columns)), inside((width, columns))],
-        [value, came, inv, inv_t, coup_t] + forwards, flops=10**8, name="descend")
+        [inside((path, columns))],
+        [value, came, inv, back_hi, back_lo] + forwards, name="descend", after=stacks[:-1])[0]
 
     far = plan.swap_rhs(solved, 2)
-    cross = plan.swap_rhs(solved, 1)
-    out_shape = pltpu.HBM((order, plan.group_count * columns), F32)
-    work = 3 * 2 * columns * order * (order + path)
-
-    def settle(parts, sides, lifted, out):
-        fresh = out is None
-        args = list(parts) + [lifted, inv_hi_t, inv_lo_t, perm_hi_t, perm_lo_t] + ([] if fresh else [out])
-        count = len(args)
+
+    def settle(part, base, column):
         return call(
-            functools.partial(settle_kernel, plan, len(parts), sides, fresh),
-            [(out_shape, HBM_SPEC)], args, flops=work * len(parts),
-            scratch=[pltpu.VMEM((len(parts), order, columns), F32), pltpu.SemaphoreType.DMA((len(parts),))],
-            anys=() if fresh else (count - 1,), alias={} if fresh else {count - 1: 0}, name="settle")[0]
-
-    out = settle([solved], [(False, False)], lifted_own, None)
-    out = settle([cross], [(False, True)], lifted_other, out)
-    last = plan.swap_rhs(far, 1)
-    out = settle([far], [(True, False)], lifted_own, out)
-    out = settle([last], [(True, True)], lifted_other, out)
+            functools.partial(settle_kernel, columns, column),
+            [inside((order, columns)), inside((8, columns))],
+            [part, base, gain_hi, gain_lo], name="settle")
+
+    own, token = settle(solved, base_own, columns)
+    pair = jnp.stack([far + token[:1], solved])
+    last = plan.swap_rhs(pair, 1)
+    far, token = settle(far, base_own, 0)
     top = call(
         functools.partial(top_kernel, plan),
         [(jax.ShapeDtypeStruct((panel_count * width, columns), F32), VMEM_SPEC)],
-        [solved, inv_t, coup_t] + stacks, flops=10**8, name="top", after_hbm=[out])[0]
+        [solved, back_hi, back_lo] + stacks, name="top", after=[token], flops=5 * 10**9)[0]
+    out = call(
+        functools.partial(last_kernel, plan, columns),
+        [(pltpu.HBM((order, plan.group_count * columns), F32), HBM_SPEC)],
+        [last, base_other, gain_hi, gain_lo, own, far],
+        scratch=[pltpu.VMEM((order, 2 * columns), F32), pltpu.SemaphoreType.DMA((4,))], name="last",
+        after_hbm=[top])[0]
     return out, top
 
 

time: 53.8 us -> 47.9 us (0.89)
  Pallas kernels: 18.2 us -> 12.9 us
  starting transfers between devices: 15 us -> 12.2 us
  waiting for transfers between devices: 19.6 us -> 21.6 us
    pallas_call x12 -> x11, Pallas kernels: 18.2 us -> 12.9 us  [call(): pl.pallas_call(body, out_shape=[shape for shape, _ in outs], in_specs=spe...]
    ppermute x10 -> x9, starting transfers between devices: 15 us -> 12.2 us  [swap(): return lax.ppermute(value, ('leaf', 'rhs'), pairs)]
    ppermute x10 -> x9, waiting for transfers between devices: 19.6 us -> 21.6 us  [swap(): return lax.ppermute(value, ('leaf', 'rhs'), pairs)]
  transfers between devices with their start and end apart: 10 -> 9, of which waited for: 6 -> 5; matrix products, arithmetic and copies ran while one was open for 0% -> 0% of each run, Pallas kernels for 20% -> 16%
where the time goes in v3:
time: 47.9 us; the launch traced here: 47.7 us
  waiting for transfers between devices  21.6 us (45%)
  Pallas kernels  12.9 us (27%)
  starting transfers between devices  12.2 us (25%)
  between operations  0.78 us (2%)
    ppermute x9, waiting for transfers between devices, swap(): return lax.ppermute(value, ('leaf', 'rhs'), pairs)  21.6 us
    pallas_call x11, Pallas kernels, call(): pl.pallas_call(body, out_shape=[shape for shape, _ in outs], in_specs=spe...  12.9 us
    ppermute x9, starting transfers between devices, swap(): return lax.ppermute(value, ('leaf', 'rhs'), pairs)  12.2 us
  transfers between devices with their start and end apart: 9, of which 5 were waited for; matrix products, arithmetic and copies ran while one was open for 0% of the time, Pallas kernels for 16%

profile of v3, /device:TPU:0, one launch (start us, length us, event | category | flops | bytes accessed | tf_op | source)
XLA Modules:
  0.0 47.7 jit_solution(1193197344009709589)
XLA Ops:
  0.6 0.0 copy-start.2
  0.6 3.6 %lift.1 = (f32[2,384,128]{2,1,0:T(8,128)S(1)}, f32[512,256]{1,0:T(8,128)S(1)}, f32[512,256]{1,0:T(8,128)S(1)}, bf16[512,512]{1,0:T(8,128)(2,1)S(1)}, bf16[512,51...) custom-call(f32[512,512]{1,0:T(8,128)} %refs_0_.2, f32[4,512,512]{2,1,0:T(8,128)} %refs_1_.2, ...), custom_call_target="tpu_custom_call" | custom-call | flops 1000 | bytes 1000 | tf_op jit(solution)/shard_map/lift/pallas_call | solution.py:258
  4.2 0.0 copy-start
  4.3 0.0 copy-start.1
  4.3 0.5 %collective-permute-start = (f32[2,384,128]{2,1,0:T(8,128)S(1)}, f32[2,384,128]{2,1,0:T(8,128)S(1)}, u32[]{:S(2)}, u32[]{:S(2)}) collective-permute-start(f32[2,384,128]{2,1,0:T(8,128)S(1)} %get-tuple-element.34), channel_id=1, source_target_pairs={{0,1},{1,0},{2,3},{3,2},{4,5},{5,4},{6,7},{7,6},{8,9},{9,8},{10,11... | collective-permute-start | bytes 1179656 | tf_op jit(solution)/shard_map/ppermute | solution.py:63
  4.8 1.5 %own.1 = (f32[2,384,128]{2,1,0:T(8,128)S(1)}, f32[512,256]{1,0:T(8,128)S(1)}) custom-call(f32[512,256]{1,0:T(8,128)S(1)} %get-tuple-element.28.refs_0_, bf16[512,512]{1,0:T(8,128)(2,1)S(1)} %get-tuple-element.29.refs_1_.refs_0_, bf16[512,512]{1,0:T(8,128)(2,1)S(1)} %get-tuple-element.30.refs_2_.refs_1_, ...), custom_call_target="tpu_custom_call" | custom-call | flops 1000 | bytes 1000 | tf_op jit(solution)/shard_map/own/pallas_call | solution.py:258
  6.3 0.0 collective-permute-done
  6.4 2.7 %collective-permute-start.1 = (f32[384,128]{1,0:T(8,128)S(1)}, f32[384,128]{1,0:T(8,128)S(1)}, u32[]{:S(2)}, u32[]{:S(2)}) collective-permute-start(f32[384,128]{1,0:T(8,128)S(1)} %fusion.refs_6_), channel_id=1, source_target_pairs={{0,2},{1,3},{2,0},{3,1},{4,6},{5,7},{6,4},{7,5},{8,10},{9,11},{10,... | collective-permute-start | bytes 589832 | tf_op jit(solution)/shard_map/ppermute | solution.py:63
  9.1 1.8 %turn.1 = (f32[512,256]{1,0:T(8,128)S(1)}, f32[512,256]{1,0:T(8,128)S(1)}, bf16[512,384]{1,0:T(8,128)(2,1)S(1)}, bf16[512,384]{1,0:T(8,128)(2,1)S(1)}, f32[8,128]{1,0:T(8,128)S(1)}) custom-call(bf16[512,512]{1,0:T(8,128)(2,1)S(1)} %get-tuple-element.29.refs_1_.refs_0_, bf16[512,512]{1,0:T(8,128)(2,1)S(1)} %get-tuple-element.30.refs_2_.refs_1_, ...), custom_call_target="tpu_custom_call" | custom-call | flops 1000 | bytes 1000 | tf_op jit(solution)/shard_map/turn/pallas_call | solution.py:258
  10.9 3.6 %collective-permute-done.1 = f32[384,128]{1,0:T(8,128)S(1)} collective-permute-done((f32[384,128]{1,0:T(8,128)S(1)}, f32[384,128]{1,0:T(8,128)S(1)}, u32[]{:S(2)}, u32[]{:S(2)}) %collective-permute-start.1) | collective-permute-done | bytes 196640 | tf_op jit(solution)/shard_map/ppermute | solution.py:63
  14.5 1.8 %collective-permute-start.2 = (f32[384,128]{1,0:T(8,128)S(1)}, f32[384,128]{1,0:T(8,128)S(1)}, u32[]{:S(2)}, u32[]{:S(2)}) collective-permute-start(f32[384,128]{1,0:T(8,128)S(1)} %fusion.3.refs_2_.refs_0_), channel_id=1, source_target_pairs={{0,4},{1,5},{2,6},{3,7},{4,0},{5,1},{6,2},{7,3},{8,12},{9,13},{10,... | collective-permute-start | bytes 589832 | tf_op jit(solution)/shard_map/ppermute | solution.py:63
  16.4 0.8 %ready.1 = (f32[7,128,128]{2,1,0:T(8,128)S(1)}, f32[10,128,128]{2,1,0:T(8,128)S(1)}, bf16[7,128,384]{2,1,0:T(8,128)(2,1)S(1)}, bf16[7,128,384]{2,1,0:T(8,128)(2,1)S(1)}) custom-call(f32[7,128,128]{2,1,0:T(8,128)S(1)} %copy-done.1, f32[10,128,128]{2,1,0:T(8,128)S(1)} %copy-done, f32[384,128]{1,0:T(8,128)S(1)} %fusion.3.refs_2_.refs_0_), custom_call_target="tpu_custom_call" | custom-call | flops 1000 | bytes 1000 | tf_op jit(solution)/shard_map/ready/pallas_call | solution.py:258
  17.2 4.0 %collective-permute-done.2.refs_1_ = f32[384,128]{1,0:T(8,128)S(1)} collective-permute-done((f32[384,128]{1,0:T(8,128)S(1)}, f32[384,128]{1,0:T(8,128)S(1)}, u32[]{:S(2)}, u32[]{:S(2)}) %collective-permute-start.2) | collective-permute-done | bytes 196640 | tf_op jit(solution)/shard_map/ppermute | solution.py:63
  21.3 0.4 climb.2
  21.6 1.6 %collective-permute-start.3 = (f32[256,128]{1,0:T(8,128)S(1)}, f32[256,128]{1,0:T(8,128)S(1)}, u32[]{:S(2)}, u32[]{:S(2)}) collective-permute-start(f32[256,128]{1,0:T(8,128)S(1)} %get-tuple-element.40.refs_0_), channel_id=1, source_target_pairs={{0,8},{1,9},{2,10},{3,11},{4,12},{5,13},{6,14},{7,15},{8,0},{9,1},... | collective-permute-start | bytes 393224 | tf_op jit(solution)/shard_map/ppermute | solution.py:63
  23.2 0.5 %collective-permute-start.5 = (f32[1,128,128]{2,1,0:T(8,128)S(1)}, f32[1,128,128]{2,1,0:T(8,128)S(1)}, u32[]{:S(2)}, u32[]{:S(2)}) collective-permute-start(f32[1,128,128]{2,1,0:T(8,128)S(1)} %bitcast.18), channel_id=1, source_target_pairs={{0,8},{1,9},{2,10},{3,11},{4,12},{5,13},{6,14},{7,15},{8,0},{9,1},... | collective-permute-start | bytes 196616 | tf_op jit(solution)/shard_map/ppermute | solution.py:63
  23.7 3.1 %collective-permute-done.3.refs_1_ = f32[256,128]{1,0:T(8,128)S(1)} collective-permute-done((f32[256,128]{1,0:T(8,128)S(1)}, f32[256,128]{1,0:T(8,128)S(1)}, u32[]{:S(2)}, u32[]{:S(2)}) %collective-permute-start.3) | collective-permute-done | bytes 131104 | tf_op jit(solution)/shard_map/ppermute | solution.py:63
  26.8 0.3 climb.3
  27.2 2.5 %collective-permute-start.4 = (f32[128,128]{1,0:T(8,128)S(1)}, f32[128,128]{1,0:T(8,128)S(1)}, u32[]{:S(2)}, u32[]{:S(2)}) collective-permute-start(f32[128,128]{1,0:T(8,128)S(1)} %get-tuple-element.41.refs_0_), channel_id=1, source_target_pairs={{0,16},{1,17},{2,18},{3,19},{4,20},{5,21},{6,22},{7,23},{8,24},{9,... | collective-permute-start | bytes 196616 | tf_op jit(solution)/shard_map/ppermute | solution.py:63
  29.6 0.0 collective-permute-done.5.refs_7_.refs_3_
  29.6 1.0 %collective-permute-start.8 = (f32[3,128,128]{2,1,0:T(8,128)S(1)}, f32[3,128,128]{2,1,0:T(8,128)S(1)}, u32[]{:S(2)}, u32[]{:S(2)}) collective-permute-start(f32[3,128,128]{2,1,0:T(8,128)S(1)} %pad_maximum_fusion.1), channel_id=1, source_target_pairs={{0,16},{1,17},{2,18},{3,19},{4,20},{5,21},{6,22},{7,23},{8,24},{9,... | collective-permute-start | bytes 589832 | tf_op jit(solution)/shard_map/ppermute | solution.py:63
  30.7 7.2 %collective-permute-done.4.refs_1_ = f32[128,128]{1,0:T(8,128)S(1)} collective-permute-done((f32[128,128]{1,0:T(8,128)S(1)}, f32[128,128]{1,0:T(8,128)S(1)}, u32[]{:S(2)}, u32[]{:S(2)}) %collective-permute-start.4) | collective-permute-done | bytes 65568 | tf_op jit(solution)/shard_map/ppermute | solution.py:63
  37.9 0.8 %descend.1.refs_0_ = f32[384,128]{1,0:T(8,128)S(1)} custom-call(f32[128,128]{1,0:T(8,128)S(1)} %get-tuple-element.41.refs_0_, f32[128,128]{1,0:T(8,128)S(1)} %collective-permute-done.4.refs_1_, f32[7,128,128]{2,1,0:T(8,128)S(1)} %get-tuple-element.38.refs_2_, bf16[7,128,384]{2,1,0:T(8,128)(2,1)S(1)} %get-tuple-element.42.refs_3_.refs_1_, ...), custom_call_target="tpu_custom_call" | custom-call | flops 1000 | bytes 1000 | tf_op jit(solution)/shard_map/descend/pallas_call | solution.py:258
  38.6 1.5 %collective-permute-start.6 = (f32[384,128]{1,0:T(8,128)S(1)}, f32[384,128]{1,0:T(8,128)S(1)}, u32[]{:S(2)}, u32[]{:S(2)}) collective-permute-start(f32[384,128]{1,0:T(8,128)S(1)} %descend.1.refs_0_), channel_id=1, source_target_pairs={{0,2},{1,3},{2,0},{3,1},{4,6},{5,7},{6,4},{7,5},{8,10},{9,11},{10,... | collective-permute-start | bytes 589832 | tf_op jit(solution)/shard_map/ppermute | solution.py:63
  40.1 0.5 settle.2
  40.6 3.7 %collective-permute-done.6.refs_0_ = f32[384,128]{1,0:T(8,128)S(1)} collective-permute-done((f32[384,128]{1,0:T(8,128)S(1)}, f32[384,128]{1,0:T(8,128)S(1)}, u32[]{:S(2)}, u32[]{:S(2)}) %collective-permute-start.6) | collective-permute-done | bytes 196640 | tf_op jit(solution)/shard_map/ppermute | solution.py:63
  44.4 0.1 collective-permute-start.7
  44.5 0.5 settle.3
  45.0 0.0 collective-permute-done.8.refs_4_
  45.0 1.3 %top.1.refs_6_ = f32[896,128]{1,0:T(8,128)} custom-call(f32[384,128]{1,0:T(8,128)S(1)} %descend.1.refs_0_, bf16[7,128,384]{2,1,0:T(8,128)(2,1)S(1)} %get-tuple-element.42.refs_3_.refs_1_, bf16[7,128,384]{2,1,0:T(8,128)(2,1)S(1)} %get-tuple-element.43.refs_4_.refs_2_, f32[1,128,128]{2,1,0:T(8,128)S(1)} %collective-permute-done.5.refs_7_.refs_3_, ...), custom_call_target="tpu_custom_call" | custom-call | flops 5000000000 | bytes 1000 | tf_op jit(solution)/shard_map/top/pallas_call | solution.py:258
  46.3 0.0 collective-permute-done.7.refs_0_
  46.3 1.4 %last.1 = f32[512,512]{1,0:T(8,128)} custom-call(f32[2,384,128]{2,1,0:T(8,128)S(1)} %collective-permute-done.7.refs_0_, f32[512,256]{1,0:T(8,128)S(1)} %get-tuple-element.50.refs_1_, bf16[512,384]{1,0:T(8,128)(2,1)S(1)} %get-tuple-element.47.refs_2_, bf16[512,384]{1,0:T(8,128)(2,1)S(1)} %get-tuple-element.48.refs_3_, ...), custom_call_target="tpu_custom_call" | custom-call | flops 1000 | bytes 1000 | tf_op jit(solution)/shard_map/last/pallas_call | solution.py:258
  (10 shorter events, 0.1 us)
Async XLA Ops:
  0.6 4.2 %copy-start.2 = (f32[896,128]{1,0:T(8,128)S(1)}, f32[896,128]{1,0:T(8,128)}, u32[]{:S(2)}) copy-start(f32[896,128]{1,0:T(8,128)} %refs_5_.1) | copy-start | bytes 1376260
  4.2 12.1 %copy-start = (f32[10,128,128]{2,1,0:T(8,128)S(1)}, f32[10,128,128]{2,1,0:T(8,128)}, u32[]{:S(2)}) copy-start(f32[10,128,128]{2,1,0:T(8,128)} %refs_1_.3) | copy-start | bytes 1966084
  4.3 12.1 %copy-start.1 = (f32[7,128,128]{2,1,0:T(8,128)S(1)}, f32[7,128,128]{2,1,0:T(8,128)}, u32[]{:S(2)}) copy-start(f32[7,128,128]{2,1,0:T(8,128)} %refs_0_.3) | copy-start | bytes 1376260
  4.3 2.1 %collective-permute-start = (f32[2,384,128]{2,1,0:T(8,128)S(1)}, f32[2,384,128]{2,1,0:T(8,128)S(1)}, u32[]{:S(2)}, u32[]{:S(2)}) collective-permute-start(f32[2,384,128]{2,1,0:T(8,128)S(1)} %get-tuple-element.34), channel_id=1, source_target_pairs={{0,1},{1,0},{2,3},{3,2},{4,5},{5,4},{6,7},{7,6},{8,9},{9,8},{10,11... | collective-permute-start | bytes 1179656 | tf_op jit(solution)/shard_map/ppermute | solution.py:63
  6.4 8.1 %collective-permute-start.1 = (f32[384,128]{1,0:T(8,128)S(1)}, f32[384,128]{1,0:T(8,128)S(1)}, u32[]{:S(2)}, u32[]{:S(2)}) collective-permute-start(f32[384,128]{1,0:T(8,128)S(1)} %fusion.refs_6_), channel_id=1, source_target_pairs={{0,2},{1,3},{2,0},{3,1},{4,6},{5,7},{6,4},{7,5},{8,10},{9,11},{10,... | collective-permute-start | bytes 589832 | tf_op jit(solution)/shard_map/ppermute | solution.py:63
  14.5 6.7 %collective-permute-start.2 = (f32[384,128]{1,0:T(8,128)S(1)}, f32[384,128]{1,0:T(8,128)S(1)}, u32[]{:S(2)}, u32[]{:S(2)}) collective-permute-start(f32[384,128]{1,0:T(8,128)S(1)} %fusion.3.refs_2_.refs_0_), channel_id=1, source_target_pairs={{0,4},{1,5},{2,6},{3,7},{4,0},{5,1},{6,2},{7,3},{8,12},{9,13},{10,... | collective-permute-start | bytes 589832 | tf_op jit(solution)/shard_map/ppermute | solution.py:63
  21.6 5.1 %collective-permute-start.3 = (f32[256,128]{1,0:T(8,128)S(1)}, f32[256,128]{1,0:T(8,128)S(1)}, u32[]{:S(2)}, u32[]{:S(2)}) collective-permute-start(f32[256,128]{1,0:T(8,128)S(1)} %get-tuple-element.40.refs_0_), channel_id=1, source_target_pairs={{0,8},{1,9},{2,10},{3,11},{4,12},{5,13},{6,14},{7,15},{8,0},{9,1},... | collective-permute-start | bytes 393224 | tf_op jit(solution)/shard_map/ppermute | solution.py:63
  23.2 6.4 %collective-permute-start.5 = (f32[1,128,128]{2,1,0:T(8,128)S(1)}, f32[1,128,128]{2,1,0:T(8,128)S(1)}, u32[]{:S(2)}, u32[]{:S(2)}) collective-permute-start(f32[1,128,128]{2,1,0:T(8,128)S(1)} %bitcast.18), channel_id=1, source_target_pairs={{0,8},{1,9},{2,10},{3,11},{4,12},{5,13},{6,14},{7,15},{8,0},{9,1},... | collective-permute-start | bytes 196616 | tf_op jit(solution)/shard_map/ppermute | solution.py:63
  27.2 10.7 %collective-permute-start.4 = (f32[128,128]{1,0:T(8,128)S(1)}, f32[128,128]{1,0:T(8,128)S(1)}, u32[]{:S(2)}, u32[]{:S(2)}) collective-permute-start(f32[128,128]{1,0:T(8,128)S(1)} %get-tuple-element.41.refs_0_), channel_id=1, source_target_pairs={{0,16},{1,17},{2,18},{3,19},{4,20},{5,21},{6,22},{7,23},{8,24},{9,... | collective-permute-start | bytes 196616 | tf_op jit(solution)/shard_map/ppermute | solution.py:63
  29.6 15.3 %collective-permute-start.8 = (f32[3,128,128]{2,1,0:T(8,128)S(1)}, f32[3,128,128]{2,1,0:T(8,128)S(1)}, u32[]{:S(2)}, u32[]{:S(2)}) collective-permute-start(f32[3,128,128]{2,1,0:T(8,128)S(1)} %pad_maximum_fusion.1), channel_id=1, source_target_pairs={{0,16},{1,17},{2,18},{3,19},{4,20},{5,21},{6,22},{7,23},{8,24},{9,... | collective-permute-start | bytes 589832 | tf_op jit(solution)/shard_map/ppermute | solution.py:63
  38.6 5.7 %collective-permute-start.6 = (f32[384,128]{1,0:T(8,128)S(1)}, f32[384,128]{1,0:T(8,128)S(1)}, u32[]{:S(2)}, u32[]{:S(2)}) collective-permute-start(f32[384,128]{1,0:T(8,128)S(1)} %descend.1.refs_0_), channel_id=1, source_target_pairs={{0,2},{1,3},{2,0},{3,1},{4,6},{5,7},{6,4},{7,5},{8,10},{9,11},{10,... | collective-permute-start | bytes 589832 | tf_op jit(solution)/shard_map/ppermute | solution.py:63
  44.4 1.9 %collective-permute-start.7 = (f32[2,384,128]{2,1,0:T(8,128)S(1)}, f32[2,384,128]{2,1,0:T(8,128)S(1)}, u32[]{:S(2)}, u32[]{:S(2)}) collective-permute-start(f32[2,384,128]{2,1,0:T(8,128)S(1)} %pad_maximum_fusion), channel_id=1, source_target_pairs={{0,1},{1,0},{2,3},{3,2},{4,5},{5,4},{6,7},{7,6},{8,9},{9,8},{10,11... | collective-permute-start | bytes 1179656 | tf_op jit(solution)/shard_map/ppermute | solution.py:63

commit v4 on v3

--- a/solution.py
+++ b/solution.py
@@ -69,8 +69,24 @@
         return self.swap(value, lambda leaf, group: (leaf ^ bit, group))
 
 
+def lift_and_couple(rhs_hi, rhs_lo, inv_hi, inv_lo, perm_hi, perm_lo, lifted, sent, hi_buf, lo_buf, step):
+    width = sent.shape[2]
+    for start in range(0, lifted.shape[0], step):
+        rows = slice(start, start + step)
+        part = dot(inv_hi[rows], rhs_hi) + (dot(inv_hi[rows], rhs_lo) + dot(inv_lo[rows], rhs_hi))
+        lifted[rows] = part
+        hi_buf[rows], lo_buf[rows] = split(part)
+    step = sent.shape[1] // 2
+    for start in range(0, sent.shape[1], step):
+        rows = slice(start, start + step)
+        part = dot(perm_hi[rows], hi_buf[...]) + (
+            dot(perm_hi[rows], lo_buf[...]) + dot(perm_lo[rows], hi_buf[...]))
+        sent[0, rows] = -part[:, :width]
+        sent[1, rows] = -part[:, width:]
+
+
 def lift_kernel(plan, order, width, rhs, inv, coupling, rows, sent, rhs_own, lifted, inv_hi, inv_lo,
-                perm_hi, perm_lo, rhs_buf, inv_buf, coup_buf, row_buf, sems):
+                perm_hi, perm_lo, rhs_buf, inv_buf, coup_buf, row_buf, hi_buf, lo_buf, sems):
     _, _, core, half = plan.here()
     block = half * 2 + core
     path = coupling.shape[1]
@@ -97,32 +113,22 @@
     perm_lo[...] = dot(chosen, coup_lo).astype(BF16)
     copies[2].wait()
     copies[3].wait()
+    rhs_hi, rhs_lo = split(rhs_buf[...])
     copies[4].wait()
-    hi, lo = split(inv_buf[...])
-    inv_hi[...] = hi
-    inv_lo[...] = lo
-    result = dot_split(hi, lo, rhs_buf[...])
-    lifted[...] = result
-    terms = dot_split(perm_hi[...], perm_lo[...], result)
-    sent[0] = -terms[:, :width]
-    sent[1] = -terms[:, width:]
+    inv_hi[...], inv_lo[...] = split(inv_buf[...])
+    lift_and_couple(rhs_hi, rhs_lo, inv_hi, inv_lo, perm_hi, perm_lo, lifted, sent, hi_buf, lo_buf, order // 4)
     copies[5].wait()
     copies[6].wait()
 
 
-def own_kernel(plan, width, rhs_own, inv_hi, inv_lo, perm_hi, perm_lo, top, own, lifted):
+def own_kernel(plan, rhs_own, inv_hi, inv_lo, perm_hi, perm_lo, top, own, lifted, hi_buf, lo_buf):
     leaf, place, _, _ = plan.here()
-    result = dot_split(inv_hi[...], inv_lo[...], rhs_own[...])
-    lifted[...] = result
-    terms = dot_split(perm_hi[...], perm_lo[...], result)
-    own[0] = -terms[:, :width]
+    rhs_hi, rhs_lo = split(rhs_own[...])
+    lift_and_couple(rhs_hi, rhs_lo, inv_hi, inv_lo, perm_hi, perm_lo, lifted, own, hi_buf, lo_buf, lifted.shape[0] // 2)
     for level in range(plan.levels):
-        rows = pl.ds(level * plan.width, plan.width)
-        panel = plan.panel(place, level)
-        share = top[lanes(panel, plan.width), :]
-        counts = leaf % (plan.sharers * 2**level) == 0
-        share = share * jnp.where(counts, 1.0, 0.0)
-        own[1, rows] = share - terms[level * plan.width : (level + 1) * plan.width, width:]
+        @pl.when(leaf % (plan.sharers * 2**level) == 0)
+        def _():
+            own[1, level * plan.width : (level + 1) * plan.width] += top[lanes(plan.panel(place, level), plan.width), :]
 
 
 def ready_kernel(levels, top_inv, top_coup, inv, coup, back_hi, back_lo):
@@ -169,6 +175,15 @@
     return dot_split(back_hi[panel, :, :depth], back_lo[panel, :, :depth], known)
 
 
+def halve_kernel(plan, *refs):
+    leaf, _, _, _ = plan.here()
+    out, number = refs[-1], 0
+    for ref in refs[:-1]:
+        for panel in range(ref.shape[0]):
+            out[number] = ref[panel, lanes(leaf % 2, plan.width // 2), :]
+            number += 1
+
+
 def descend_kernel(plan, *refs):
     levels, width = plan.levels, plan.width
     value, came, inv, back_hi, back_lo = refs[:5]
@@ -222,7 +237,8 @@
 def top_kernel(plan, solved, back_hi, back_lo, *refs):
     levels, width = plan.levels, plan.width
     stacks, out = refs[:-1], refs[-1]
-    _, place, _, _ = plan.here()
+    leaf, place, _, _ = plan.here()
+    second = leaf % 2 == 1
     found = {}
     for level in reversed(range(levels)):
         for flip in range(2 ** (levels - 1 - level)):
@@ -231,7 +247,12 @@
                 result = solved[pl.ds(level * width, width), :]
             else:
                 step = flip.bit_length() - 1 + level
-                forward = stacks[step][stack_place(step, level, flip - 2 ** (step - level))]
+                number = stack_place(step, level, flip - 2 ** (step - level))
+                forward = stacks[step][number]
+                if step == levels - 2:
+                    other = stacks[step + 1][number]
+                    forward = jnp.concatenate(
+                        [jnp.where(second, other, forward), jnp.where(second, forward, other)], 0)
                 above = [found[up, flip >> (up - level)] for up in range(level + 1, levels)]
                 result = backward(plan, back_hi, back_lo, panel, level, forward, above)
             found[level, flip] = result
@@ -261,7 +282,7 @@
         in_specs=specs + after_specs,
         out_specs=[spec for _, spec in outs],
         scratch_shapes=list(scratch),
-        compiler_params=pltpu.CompilerParams(vmem_limit_bytes=24 * 2**20),
+        compiler_params=pltpu.CompilerParams(vmem_limit_bytes=12 * 2**20),
         cost_estimate=pl.CostEstimate(flops=flops, bytes_accessed=1000, transcendentals=0),
         name=name,
     )(*args, *after)
@@ -280,6 +301,7 @@
     levels = plan.levels
     assert plan.group_count == 4 and block_count == 4 and plan.sharers >= 2
 
+    halves = [pltpu.VMEM((order, 2 * columns), BF16)] * 2
     sent, rhs_own, lifted_other, inv_hi, inv_lo, perm_hi, perm_lo = call(
         functools.partial(lift_kernel, plan, order, columns),
         [inside((2, path, columns)), inside((order, 2 * columns)), inside((order, 2 * columns)),
@@ -287,14 +309,14 @@
          inside((path, order), BF16), inside((path, order), BF16)],
         [rhs_in, leaf_inv, leaf_coupling, coupling_rows],
         scratch=[pltpu.VMEM((order, 2 * columns), F32), pltpu.VMEM((order, order), F32),
-                 pltpu.VMEM((path, order), F32), pltpu.VMEM((1, path), jnp.int32),
+                 pltpu.VMEM((path, order), F32), pltpu.VMEM((1, path), jnp.int32), *halves,
                  pltpu.SemaphoreType.DMA((7,))],
         anys=(0, 1, 2, 3), name="lift")
     came = plan.swap_rhs(sent, 1)
     own, lifted_own = call(
-        functools.partial(own_kernel, plan, columns),
+        functools.partial(own_kernel, plan),
         [inside((2, path, columns)), inside((order, 2 * columns))],
-        [rhs_own, inv_hi, inv_lo, perm_hi, perm_lo, rhs_top], name="own")
+        [rhs_own, inv_hi, inv_lo, perm_hi, perm_lo, rhs_top], scratch=halves, name="own")
     far = own[0] + came[0]
     near = own[1] + came[1]
     base_own, base_other, gain_hi, gain_lo, token = call(
@@ -324,7 +346,13 @@
         came = plan.swap_leaf(value, bit)
         forwards.append(forward)
         known = known + stacks[-1:] + [forward[None]]
-        stacks.append(plan.swap_leaf(jnp.concatenate(known, 0), bit))
+        if level == levels - 2:
+            stack = call(
+                functools.partial(halve_kernel, plan),
+                [inside((2 ** (level + 1) - 1, width // 2, columns))], known, name="halve", after=[value])[0]
+        else:
+            stack = jnp.concatenate(known, 0)
+        stacks.append(plan.swap_leaf(stack, bit))
     solved = call(
         functools.partial(descend_kernel, plan),
         [inside((path, columns))],
@@ -339,6 +367,7 @@
             [part, base, gain_hi, gain_lo], name="settle")
 
     own, token = settle(solved, base_own, columns)
+    stacks.append(plan.swap_leaf(stacks[-1] + token[:1], 1))
     pair = jnp.stack([far + token[:1], solved])
     last = plan.swap_rhs(pair, 1)
     far, token = settle(far, base_own, 0)

time: 47.9 us -> 43 us (0.90)
  waiting for transfers between devices: 21.6 us -> 15.7 us
  starting transfers between devices: 12.2 us -> 14.4 us
  Pallas kernels: 12.9 us -> 11.8 us
    ppermute x9 -> x10, waiting for transfers between devices: 21.6 us -> 15.7 us  [swap(): return lax.ppermute(value, ('leaf', 'rhs'), pairs)]
    ppermute x9 -> x10, starting transfers between devices: 12.2 us -> 14.4 us  [swap(): return lax.ppermute(value, ('leaf', 'rhs'), pairs)]
    pallas_call x11 -> x12, Pallas kernels: 12.9 us -> 11.8 us  [call(): pl.pallas_call(body, out_shape=[shape for shape, _ in outs], in_specs=spe...]
  transfers between devices with their start and end apart: 9 -> 10, of which waited for: 5 -> 7; matrix products, arithmetic and copies ran while one was open for 0% -> 0% of each run, Pallas kernels for 16% -> 16%
where the time goes in v4:
time: 43 us; the launch traced here: 42.8 us
  waiting for transfers between devices  15.7 us (37%)
  starting transfers between devices  14.4 us (33%)
  Pallas kernels  11.8 us (27%)
  between operations  0.78 us (2%)
    ppermute x10, waiting for transfers between devices, swap(): return lax.ppermute(value, ('leaf', 'rhs'), pairs)  15.7 us
    ppermute x10, starting transfers between devices, swap(): return lax.ppermute(value, ('leaf', 'rhs'), pairs)  14.4 us
    pallas_call x12, Pallas kernels, call(): pl.pallas_call(body, out_shape=[shape for shape, _ in outs], in_specs=spe...  11.8 us
  transfers between devices with their start and end apart: 10, of which 7 were waited for; matrix products, arithmetic and copies ran while one was open for 0% of the time, Pallas kernels for 16%

profile of v4, /device:TPU:0, one launch (start us, length us, event | category | flops | bytes accessed | tf_op | source)
XLA Modules:
  0.0 42.8 jit_solution(15337108116018850529)
XLA Ops:
  0.6 3.0 %lift.1 = (f32[2,384,128]{2,1,0:T(8,128)S(1)}, f32[512,256]{1,0:T(8,128)S(1)}, f32[512,256]{1,0:T(8,128)S(1)}, bf16[512,512]{1,0:T(8,128)(2,1)S(1)}, bf16[512,51...) custom-call(f32[512,512]{1,0:T(8,128)} %refs_0_.2, f32[4,512,512]{2,1,0:T(8,128)} %refs_1_.2, ...), custom_call_target="tpu_custom_call" | custom-call | flops 1000 | bytes 1000 | tf_op jit(solution)/shard_map/lift/pallas_call | solution.py:279
  3.6 0.0 copy-start
  3.6 0.0 copy-start.1
  3.7 0.5 %collective-permute-start = (f32[2,384,128]{2,1,0:T(8,128)S(1)}, f32[2,384,128]{2,1,0:T(8,128)S(1)}, u32[]{:S(2)}, u32[]{:S(2)}) collective-permute-start(f32[2,384,128]{2,1,0:T(8,128)S(1)} %get-tuple-element.34), channel_id=1, source_target_pairs={{0,1},{1,0},{2,3},{3,2},{4,5},{5,4},{6,7},{7,6},{8,9},{9,8},{10,11... | collective-permute-start | bytes 1179656 | tf_op jit(solution)/shard_map/ppermute | solution.py:63
  4.2 1.1 %own.1 = (f32[2,384,128]{2,1,0:T(8,128)S(1)}, f32[512,256]{1,0:T(8,128)S(1)}) custom-call(f32[512,256]{1,0:T(8,128)S(1)} %get-tuple-element.28.refs_0_, bf16[512,512]{1,0:T(8,128)(2,1)S(1)} %get-tuple-element.29.refs_1_.refs_0_, bf16[512,512]{1,0:T(8,128)(2,1)S(1)} %get-tuple-element.30.refs_2_.refs_1_, ...), custom_call_target="tpu_custom_call" | custom-call | flops 1000 | bytes 1000 | tf_op jit(solution)/shard_map/own/pallas_call | solution.py:279
  5.2 0.3 collective-permute-done
  5.5 2.9 %collective-permute-start.1 = (f32[384,128]{1,0:T(8,128)S(1)}, f32[384,128]{1,0:T(8,128)S(1)}, u32[]{:S(2)}, u32[]{:S(2)}) collective-permute-start(f32[384,128]{1,0:T(8,128)S(1)} %fusion.refs_6_), channel_id=1, source_target_pairs={{0,2},{1,3},{2,0},{3,1},{4,6},{5,7},{6,4},{7,5},{8,10},{9,11},{10,... | collective-permute-start | bytes 589832 | tf_op jit(solution)/shard_map/ppermute | solution.py:63
  8.5 1.8 %turn.1 = (f32[512,256]{1,0:T(8,128)S(1)}, f32[512,256]{1,0:T(8,128)S(1)}, bf16[512,384]{1,0:T(8,128)(2,1)S(1)}, bf16[512,384]{1,0:T(8,128)(2,1)S(1)}, f32[8,128]{1,0:T(8,128)S(1)}) custom-call(bf16[512,512]{1,0:T(8,128)(2,1)S(1)} %get-tuple-element.29.refs_1_.refs_0_, bf16[512,512]{1,0:T(8,128)(2,1)S(1)} %get-tuple-element.30.refs_2_.refs_1_, ...), custom_call_target="tpu_custom_call" | custom-call | flops 1000 | bytes 1000 | tf_op jit(solution)/shard_map/turn/pallas_call | solution.py:279
  10.3 3.4 %collective-permute-done.1 = f32[384,128]{1,0:T(8,128)S(1)} collective-permute-done((f32[384,128]{1,0:T(8,128)S(1)}, f32[384,128]{1,0:T(8,128)S(1)}, u32[]{:S(2)}, u32[]{:S(2)}) %collective-permute-start.1) | collective-permute-done | bytes 196640 | tf_op jit(solution)/shard_map/ppermute | solution.py:63
  13.7 1.8 %collective-permute-start.2 = (f32[384,128]{1,0:T(8,128)S(1)}, f32[384,128]{1,0:T(8,128)S(1)}, u32[]{:S(2)}, u32[]{:S(2)}) collective-permute-start(f32[384,128]{1,0:T(8,128)S(1)} %fusion.3.refs_2_.refs_0_), channel_id=1, source_target_pairs={{0,4},{1,5},{2,6},{3,7},{4,0},{5,1},{6,2},{7,3},{8,12},{9,13},{10,... | collective-permute-start | bytes 589832 | tf_op jit(solution)/shard_map/ppermute | solution.py:63
  15.6 0.8 %ready.1 = (f32[7,128,128]{2,1,0:T(8,128)S(1)}, f32[10,128,128]{2,1,0:T(8,128)S(1)}, bf16[7,128,384]{2,1,0:T(8,128)(2,1)S(1)}, bf16[7,128,384]{2,1,0:T(8,128)(2,1)S(1)}) custom-call(f32[7,128,128]{2,1,0:T(8,128)S(1)} %copy-done.1, f32[10,128,128]{2,1,0:T(8,128)S(1)} %copy-done, f32[384,128]{1,0:T(8,128)S(1)} %fusion.3.refs_2_.refs_0_), custom_call_target="tpu_custom_call" | custom-call | flops 1000 | bytes 1000 | tf_op jit(solution)/shard_map/ready/pallas_call | solution.py:279
  16.4 3.8 %collective-permute-done.2.refs_1_ = f32[384,128]{1,0:T(8,128)S(1)} collective-permute-done((f32[384,128]{1,0:T(8,128)S(1)}, f32[384,128]{1,0:T(8,128)S(1)}, u32[]{:S(2)}, u32[]{:S(2)}) %collective-permute-start.2) | collective-permute-done | bytes 196640 | tf_op jit(solution)/shard_map/ppermute | solution.py:63
  20.2 0.4 climb.2
  20.6 1.6 %collective-permute-start.3 = (f32[256,128]{1,0:T(8,128)S(1)}, f32[256,128]{1,0:T(8,128)S(1)}, u32[]{:S(2)}, u32[]{:S(2)}) collective-permute-start(f32[256,128]{1,0:T(8,128)S(1)} %get-tuple-element.40.refs_0_), channel_id=1, source_target_pairs={{0,8},{1,9},{2,10},{3,11},{4,12},{5,13},{6,14},{7,15},{8,0},{9,1},... | collective-permute-start | bytes 393224 | tf_op jit(solution)/shard_map/ppermute | solution.py:63
  22.2 0.5 %collective-permute-start.5 = (f32[1,128,128]{2,1,0:T(8,128)S(1)}, f32[1,128,128]{2,1,0:T(8,128)S(1)}, u32[]{:S(2)}, u32[]{:S(2)}) collective-permute-start(f32[1,128,128]{2,1,0:T(8,128)S(1)} %bitcast.18), channel_id=1, source_target_pairs={{0,8},{1,9},{2,10},{3,11},{4,12},{5,13},{6,14},{7,15},{8,0},{9,1},... | collective-permute-start | bytes 196616 | tf_op jit(solution)/shard_map/ppermute | solution.py:63
  22.7 2.9 %collective-permute-done.3.refs_1_ = f32[256,128]{1,0:T(8,128)S(1)} collective-permute-done((f32[256,128]{1,0:T(8,128)S(1)}, f32[256,128]{1,0:T(8,128)S(1)}, u32[]{:S(2)}, u32[]{:S(2)}) %collective-permute-start.3) | collective-permute-done | bytes 131104 | tf_op jit(solution)/shard_map/ppermute | solution.py:63
  25.6 0.3 climb.3
  26.0 2.6 %collective-permute-start.4 = (f32[128,128]{1,0:T(8,128)S(1)}, f32[128,128]{1,0:T(8,128)S(1)}, u32[]{:S(2)}, u32[]{:S(2)}) collective-permute-start(f32[128,128]{1,0:T(8,128)S(1)} %get-tuple-element.41.refs_0_.refs_3_), channel_id=1, source_target_pairs={{0,16},{1,17},{2,18},{3,19},{4,20},{5,21},{6,22},{7,23},{8,24},{9,... | collective-permute-start | bytes 196616 | tf_op jit(solution)/shard_map/ppermute | solution.py:63
  28.6 0.0 collective-permute-done.5.refs_7_.refs_1_.refs_3_
  28.6 1.2 %collective-permute-start.8 = (f32[3,64,128]{2,1,0:T(8,128)S(1)}, f32[3,64,128]{2,1,0:T(8,128)S(1)}, u32[]{:S(2)}, u32[]{:S(2)}) collective-permute-start(f32[3,64,128]{2,1,0:T(8,128)S(1)} %halve.1), channel_id=1, source_target_pairs={{0,16},{1,17},{2,18},{3,19},{4,20},{5,21},{6,22},{7,23},{8,24},{9,... | collective-permute-start | bytes 294920 | tf_op jit(solution)/shard_map/ppermute | solution.py:63
  29.8 2.8 %collective-permute-done.4.refs_1_ = f32[128,128]{1,0:T(8,128)S(1)} collective-permute-done((f32[128,128]{1,0:T(8,128)S(1)}, f32[128,128]{1,0:T(8,128)S(1)}, u32[]{:S(2)}, u32[]{:S(2)}) %collective-permute-start.4) | collective-permute-done | bytes 65568 | tf_op jit(solution)/shard_map/ppermute | solution.py:63
  32.6 0.8 %descend.1.refs_0_ = f32[384,128]{1,0:T(8,128)S(1)} custom-call(f32[128,128]{1,0:T(8,128)S(1)} %get-tuple-element.41.refs_0_.refs_3_, f32[128,128]{1,0:T(8,128)S(1)} %collective-permute-done.4.refs_1_, f32[7,128,128]{2,1,0:T(8,128)S(1)} %get-tuple-element.38.refs_2_, bf16[7,128,384]{2,1,0:T(8,128)(2,1)S(1)} %get-tuple-element.42.refs_3_.refs_1_, ...), custom_call_target="tpu_custom_call" | custom-call | flops 1000 | bytes 1000 | tf_op jit(solution)/shard_map/descend/pallas_call | solution.py:279
  33.4 1.6 %collective-permute-start.6 = (f32[384,128]{1,0:T(8,128)S(1)}, f32[384,128]{1,0:T(8,128)S(1)}, u32[]{:S(2)}, u32[]{:S(2)}) collective-permute-start(f32[384,128]{1,0:T(8,128)S(1)} %descend.1.refs_0_), channel_id=1, source_target_pairs={{0,2},{1,3},{2,0},{3,1},{4,6},{5,7},{6,4},{7,5},{8,10},{9,11},{10,... | collective-permute-start | bytes 589832 | tf_op jit(solution)/shard_map/ppermute | solution.py:63
  35.0 0.5 %settle.2 = (f32[512,128]{1,0:T(8,128)S(1)}, f32[8,128]{1,0:T(8,128)S(1)}) custom-call(f32[384,128]{1,0:T(8,128)S(1)} %descend.1.refs_0_, f32[512,256]{1,0:T(8,128)S(1)} %get-tuple-element.46.refs_1_, bf16[512,384]{1,0:T(8,128)(2,1)S(1)} %get-tuple-element.47.refs_2_, bf16[512,384]{1,0:T(8,128)(2,1)S(1)} %get-tuple-element.48.refs_3_), custom_call_target="tpu_custom_call" | custom-call | flops 1000 | bytes 1000 | tf_op jit(solution)/shard_map/settle/pallas_call | solution.py:279
  35.5 1.6 %collective-permute-start.9 = (f32[3,64,128]{2,1,0:T(8,128)S(1)}, f32[3,64,128]{2,1,0:T(8,128)S(1)}, u32[]{:S(2)}, u32[]{:S(2)}) collective-permute-start(f32[3,64,128]{2,1,0:T(8,128)S(1)} %broadcast_add_fusion), channel_id=1, source_target_pairs={{0,4},{1,5},{2,6},{3,7},{4,0},{5,1},{6,2},{7,3},{8,12},{9,13},{10,... | collective-permute-start | bytes 294920 | tf_op jit(solution)/shard_map/ppermute | solution.py:63
  37.0 2.1 %collective-permute-done.6.refs_0_ = f32[384,128]{1,0:T(8,128)S(1)} collective-permute-done((f32[384,128]{1,0:T(8,128)S(1)}, f32[384,128]{1,0:T(8,128)S(1)}, u32[]{:S(2)}, u32[]{:S(2)}) %collective-permute-start.6) | collective-permute-done | bytes 196640 | tf_op jit(solution)/shard_map/ppermute | solution.py:63
  39.2 0.1 collective-permute-start.7
  39.3 0.5 %settle.3 = (f32[512,128]{1,0:T(8,128)S(1)}, f32[8,128]{1,0:T(8,128)S(1)}) custom-call(f32[384,128]{1,0:T(8,128)S(1)} %collective-permute-done.6.refs_0_, f32[512,256]{1,0:T(8,128)S(1)} %get-tuple-element.46.refs_1_, bf16[512,384]{1,0:T(8,128)(2,1)S(1)} %get-tuple-element.47.refs_2_, bf16[512,384]{1,0:T(8,128)(2,1)S(1)} %get-tuple-element.48.refs_3_), custom_call_target="tpu_custom_call" | custom-call | flops 1000 | bytes 1000 | tf_op jit(solution)/shard_map/settle/pallas_call | solution.py:279
  39.7 0.4 collective-permute-done.9.refs_5_
  40.1 1.3 %top.1.refs_6_ = f32[896,128]{1,0:T(8,128)} custom-call(f32[384,128]{1,0:T(8,128)S(1)} %descend.1.refs_0_, bf16[7,128,384]{2,1,0:T(8,128)(2,1)S(1)} %get-tuple-element.42.refs_3_.refs_1_, bf16[7,128,384]{2,1,0:T(8,128)(2,1)S(1)} %get-tuple-element.43.refs_4_.refs_2_, f32[1,128,128]{2,1,0:T(8,128)S(1)} %collective-permute-done.5.refs_7_.refs_1_.refs_3_, ...), custom_call_target="tpu_custom_call" | custom-call | flops 5000000000 | bytes 1000 | tf_op jit(solution)/shard_map/top/pallas_call | solution.py:279
  41.4 0.0 collective-permute-done.7.refs_0_
  41.4 1.4 %last.1 = f32[512,512]{1,0:T(8,128)} custom-call(f32[2,384,128]{2,1,0:T(8,128)S(1)} %collective-permute-done.7.refs_0_, f32[512,256]{1,0:T(8,128)S(1)} %get-tuple-element.50.refs_1_, bf16[512,384]{1,0:T(8,128)(2,1)S(1)} %get-tuple-element.47.refs_2_, bf16[512,384]{1,0:T(8,128)(2,1)S(1)} %get-tuple-element.48.refs_3_, ...), custom_call_target="tpu_custom_call" | custom-call | flops 1000 | bytes 1000 | tf_op jit(solution)/shard_map/last/pallas_call | solution.py:279
  (13 shorter events, 0.1 us)
Async XLA Ops:
  0.6 3.5 %copy-start.2 = (f32[896,128]{1,0:T(8,128)S(1)}, f32[896,128]{1,0:T(8,128)}, u32[]{:S(2)}) copy-start(f32[896,128]{1,0:T(8,128)} %refs_5_.1) | copy-start | bytes 1376260
  3.6 11.9 %copy-start = (f32[10,128,128]{2,1,0:T(8,128)S(1)}, f32[10,128,128]{2,1,0:T(8,128)}, u32[]{:S(2)}) copy-start(f32[10,128,128]{2,1,0:T(8,128)} %refs_1_.3) | copy-start | bytes 1966084
  3.6 11.9 %copy-start.1 = (f32[7,128,128]{2,1,0:T(8,128)S(1)}, f32[7,128,128]{2,1,0:T(8,128)}, u32[]{:S(2)}) copy-start(f32[7,128,128]{2,1,0:T(8,128)} %refs_0_.3) | copy-start | bytes 1376260
  3.7 1.9 %collective-permute-start = (f32[2,384,128]{2,1,0:T(8,128)S(1)}, f32[2,384,128]{2,1,0:T(8,128)S(1)}, u32[]{:S(2)}, u32[]{:S(2)}) collective-permute-start(f32[2,384,128]{2,1,0:T(8,128)S(1)} %get-tuple-element.34), channel_id=1, source_target_pairs={{0,1},{1,0},{2,3},{3,2},{4,5},{5,4},{6,7},{7,6},{8,9},{9,8},{10,11... | collective-permute-start | bytes 1179656 | tf_op jit(solution)/shard_map/ppermute | solution.py:63
  5.5 8.1 %collective-permute-start.1 = (f32[384,128]{1,0:T(8,128)S(1)}, f32[384,128]{1,0:T(8,128)S(1)}, u32[]{:S(2)}, u32[]{:S(2)}) collective-permute-start(f32[384,128]{1,0:T(8,128)S(1)} %fusion.refs_6_), channel_id=1, source_target_pairs={{0,2},{1,3},{2,0},{3,1},{4,6},{5,7},{6,4},{7,5},{8,10},{9,11},{10,... | collective-permute-start | bytes 589832 | tf_op jit(solution)/shard_map/ppermute | solution.py:63
  13.7 6.5 %collective-permute-start.2 = (f32[384,128]{1,0:T(8,128)S(1)}, f32[384,128]{1,0:T(8,128)S(1)}, u32[]{:S(2)}, u32[]{:S(2)}) collective-permute-start(f32[384,128]{1,0:T(8,128)S(1)} %fusion.3.refs_2_.refs_0_), channel_id=1, source_target_pairs={{0,4},{1,5},{2,6},{3,7},{4,0},{5,1},{6,2},{7,3},{8,12},{9,13},{10,... | collective-permute-start | bytes 589832 | tf_op jit(solution)/shard_map/ppermute | solution.py:63
  20.6 5.0 %collective-permute-start.3 = (f32[256,128]{1,0:T(8,128)S(1)}, f32[256,128]{1,0:T(8,128)S(1)}, u32[]{:S(2)}, u32[]{:S(2)}) collective-permute-start(f32[256,128]{1,0:T(8,128)S(1)} %get-tuple-element.40.refs_0_), channel_id=1, source_target_pairs={{0,8},{1,9},{2,10},{3,11},{4,12},{5,13},{6,14},{7,15},{8,0},{9,1},... | collective-permute-start | bytes 393224 | tf_op jit(solution)/shard_map/ppermute | solution.py:63
  22.2 6.4 %collective-permute-start.5 = (f32[1,128,128]{2,1,0:T(8,128)S(1)}, f32[1,128,128]{2,1,0:T(8,128)S(1)}, u32[]{:S(2)}, u32[]{:S(2)}) collective-permute-start(f32[1,128,128]{2,1,0:T(8,128)S(1)} %bitcast.18), channel_id=1, source_target_pairs={{0,8},{1,9},{2,10},{3,11},{4,12},{5,13},{6,14},{7,15},{8,0},{9,1},... | collective-permute-start | bytes 196616 | tf_op jit(solution)/shard_map/ppermute | solution.py:63
  26.0 6.6 %collective-permute-start.4 = (f32[128,128]{1,0:T(8,128)S(1)}, f32[128,128]{1,0:T(8,128)S(1)}, u32[]{:S(2)}, u32[]{:S(2)}) collective-permute-start(f32[128,128]{1,0:T(8,128)S(1)} %get-tuple-element.41.refs_0_.refs_3_), channel_id=1, source_target_pairs={{0,16},{1,17},{2,18},{3,19},{4,20},{5,21},{6,22},{7,23},{8,24},{9,... | collective-permute-start | bytes 196616 | tf_op jit(solution)/shard_map/ppermute | solution.py:63
  28.6 6.8 %collective-permute-start.8 = (f32[3,64,128]{2,1,0:T(8,128)S(1)}, f32[3,64,128]{2,1,0:T(8,128)S(1)}, u32[]{:S(2)}, u32[]{:S(2)}) collective-permute-start(f32[3,64,128]{2,1,0:T(8,128)S(1)} %halve.1), channel_id=1, source_target_pairs={{0,16},{1,17},{2,18},{3,19},{4,20},{5,21},{6,22},{7,23},{8,24},{9,... | collective-permute-start | bytes 294920 | tf_op jit(solution)/shard_map/ppermute | solution.py:63
  33.4 5.7 %collective-permute-start.6 = (f32[384,128]{1,0:T(8,128)S(1)}, f32[384,128]{1,0:T(8,128)S(1)}, u32[]{:S(2)}, u32[]{:S(2)}) collective-permute-start(f32[384,128]{1,0:T(8,128)S(1)} %descend.1.refs_0_), channel_id=1, source_target_pairs={{0,2},{1,3},{2,0},{3,1},{4,6},{5,7},{6,4},{7,5},{8,10},{9,11},{10,... | collective-permute-start | bytes 589832 | tf_op jit(solution)/shard_map/ppermute | solution.py:63
  35.5 4.7 %collective-permute-start.9 = (f32[3,64,128]{2,1,0:T(8,128)S(1)}, f32[3,64,128]{2,1,0:T(8,128)S(1)}, u32[]{:S(2)}, u32[]{:S(2)}) collective-permute-start(f32[3,64,128]{2,1,0:T(8,128)S(1)} %broadcast_add_fusion), channel_id=1, source_target_pairs={{0,4},{1,5},{2,6},{3,7},{4,0},{5,1},{6,2},{7,3},{8,12},{9,13},{10,... | collective-permute-start | bytes 294920 | tf_op jit(solution)/shard_map/ppermute | solution.py:63
  39.2 2.3 %collective-permute-start.7 = (f32[2,384,128]{2,1,0:T(8,128)S(1)}, f32[2,384,128]{2,1,0:T(8,128)S(1)}, u32[]{:S(2)}, u32[]{:S(2)}) collective-permute-start(f32[2,384,128]{2,1,0:T(8,128)S(1)} %pad_maximum_fusion), channel_id=1, source_target_pairs={{0,1},{1,0},{2,3},{3,2},{4,5},{5,4},{6,7},{7,6},{8,9},{9,8},{10,11... | collective-permute-start | bytes 1179656 | tf_op jit(solution)/shard_map/ppermute | solution.py:63

commit v5 on v4

--- a/solution.py
+++ b/solution.py
@@ -69,23 +69,28 @@
         return self.swap(value, lambda leaf, group: (leaf ^ bit, group))
 
 
-def lift_and_couple(rhs_hi, rhs_lo, inv_hi, inv_lo, perm_hi, perm_lo, lifted, sent, hi_buf, lo_buf, step):
-    width = sent.shape[2]
+def lift_and_couple(rhs_hi, rhs_lo, inv_hi, inv_lo, perm_hi, perm_lo, lifted, first, second, hi_buf, lo_buf, step):
+    path, width = perm_hi.shape[0], first.shape[1]
+    cut = first.shape[0]
     for start in range(0, lifted.shape[0], step):
         rows = slice(start, start + step)
         part = dot(inv_hi[rows], rhs_hi) + (dot(inv_hi[rows], rhs_lo) + dot(inv_lo[rows], rhs_hi))
         lifted[rows] = part
         hi_buf[rows], lo_buf[rows] = split(part)
-    step = sent.shape[1] // 2
-    for start in range(0, sent.shape[1], step):
+    step = path // 2
+    for start in range(0, path, step):
         rows = slice(start, start + step)
         part = dot(perm_hi[rows], hi_buf[...]) + (
             dot(perm_hi[rows], lo_buf[...]) + dot(perm_lo[rows], hi_buf[...]))
-        sent[0, rows] = -part[:, :width]
-        sent[1, rows] = -part[:, width:]
-
-
-def lift_kernel(plan, order, width, rhs, inv, coupling, rows, sent, rhs_own, lifted, inv_hi, inv_lo,
+        if start < cut:
+            first[start : min(start + step, cut)] = -part[: min(step, cut - start), :width]
+        if start + step > cut:
+            skip = max(cut - start, 0)
+            second[start + skip - cut : start + step - cut] = -part[skip:, :width]
+        second[path - cut + start : path - cut + start + step] = -part[:, width:]
+
+
+def lift_kernel(plan, order, width, rhs, inv, coupling, rows, first, second, rhs_own, lifted, inv_hi, inv_lo,
                 perm_hi, perm_lo, rhs_buf, inv_buf, coup_buf, row_buf, hi_buf, lo_buf, sems):
     _, _, core, half = plan.here()
     block = half * 2 + core
@@ -116,19 +121,22 @@
     rhs_hi, rhs_lo = split(rhs_buf[...])
     copies[4].wait()
     inv_hi[...], inv_lo[...] = split(inv_buf[...])
-    lift_and_couple(rhs_hi, rhs_lo, inv_hi, inv_lo, perm_hi, perm_lo, lifted, sent, hi_buf, lo_buf, order // 4)
+    lift_and_couple(rhs_hi, rhs_lo, inv_hi, inv_lo, perm_hi, perm_lo, lifted, first, second, hi_buf, lo_buf,
+                    order // 4)
     copies[5].wait()
     copies[6].wait()
 
 
-def own_kernel(plan, rhs_own, inv_hi, inv_lo, perm_hi, perm_lo, top, own, lifted, hi_buf, lo_buf):
+def own_kernel(plan, rhs_own, inv_hi, inv_lo, perm_hi, perm_lo, top, first, second, lifted, hi_buf, lo_buf):
     leaf, place, _, _ = plan.here()
     rhs_hi, rhs_lo = split(rhs_own[...])
-    lift_and_couple(rhs_hi, rhs_lo, inv_hi, inv_lo, perm_hi, perm_lo, lifted, own, hi_buf, lo_buf, lifted.shape[0] // 2)
+    lift_and_couple(rhs_hi, rhs_lo, inv_hi, inv_lo, perm_hi, perm_lo, lifted, first, second, hi_buf, lo_buf,
+                    lifted.shape[0] // 2)
     for level in range(plan.levels):
         @pl.when(leaf % (plan.sharers * 2**level) == 0)
         def _():
-            own[1, level * plan.width : (level + 1) * plan.width] += top[lanes(plan.panel(place, level), plan.width), :]
+            start = perm_hi.shape[0] - first.shape[0] + level * plan.width
+            second[start : start + plan.width] += top[lanes(plan.panel(place, level), plan.width), :]
 
 
 def ready_kernel(levels, top_inv, top_coup, inv, coup, back_hi, back_lo):
@@ -158,15 +166,18 @@
     token[...] = jnp.zeros_like(token)
 
 
-def climb_kernel(plan, level, value, came, inv, coup, forward, rest):
+def climb_kernel(plan, level, count, *refs):
     _, place, _, _ = plan.here()
     width = plan.width
     above = plan.levels - 1 - level
-    result = dot_high(inv[plan.panel(place, level)], value[:width] + came[:width])
+    inv, coup, forward, rest = refs[2 * count :]
+    parts = [value[...] + came[...] for value, came in zip(refs[:count], refs[count : 2 * count])]
+    total = jnp.concatenate(parts, 0) if count > 1 else parts[0]
+    result = dot_high(inv[plan.panel(place, level)], total[:width])
     forward[...] = result
     pairs = coup[pl.ds(plan.pair(place, level, level + 1), above)]
     change = dot_high(pairs.reshape(above * width, width), result)
-    rest[...] = value[width:] + came[width:] - change
+    rest[...] = total[width:] - change
 
 
 def backward(plan, back_hi, back_lo, panel, level, forward, above):
@@ -209,18 +220,25 @@
     token[...] = jnp.zeros_like(token)
 
 
-def last_kernel(plan, width, part, base, gain_hi, gain_lo, own, far, out, buffer, sems):
+def last_kernel(plan, width, part, base, gain_hi, gain_lo, own, far, top, out, out_top, buffer, sems):
     _, _, core, half = plan.here()
     groups = ((1 - half) * 2 + core, half * 2 + core, (1 - half) * 2 + 1 - core, half * 2 + 1 - core)
-    copies = [pltpu.make_async_copy(done, out.at[:, lanes(group, width)], sems.at[number])
-              for number, (done, group) in enumerate(zip((
-                  far, own, buffer.at[:, :width], buffer.at[:, width:]), groups))]
-    copies[0].start()
-    copies[1].start()
-    known = jnp.concatenate([part[0], part[1]], 1)
-    buffer[...] = base[...] - dot_split(gain_hi[...], gain_lo[...], known)
-    copies[2].start()
-    copies[3].start()
+    copies = [pltpu.make_async_copy(top, out_top, sems.at[0])]
+    for done, group in zip((far, own), groups):
+        copies.append(pltpu.make_async_copy(done, out.at[:, lanes(group, width)], sems.at[len(copies)]))
+    for copy in copies:
+        copy.start()
+    known = split(jnp.concatenate([part[0], part[1]], 1))
+    step = buffer.shape[0] // 2
+    for start in range(0, buffer.shape[0], step):
+        rows = slice(start, start + step)
+        change = dot(gain_hi[rows], known[0]) + (dot(gain_hi[rows], known[1]) + dot(gain_lo[rows], known[0]))
+        buffer[rows] = base[rows] - change
+        for number, group in enumerate(groups[2:]):
+            copies.append(pltpu.make_async_copy(
+                buffer.at[pl.ds(start, step), pl.ds(number * width, width)],
+                out.at[pl.ds(start, step), lanes(group, width)], sems.at[len(copies)]))
+            copies[-1].start()
     for copy in copies:
         copy.wait()
 
@@ -302,9 +320,11 @@
     assert plan.group_count == 4 and block_count == 4 and plan.sharers >= 2
 
     halves = [pltpu.VMEM((order, 2 * columns), BF16)] * 2
-    sent, rhs_own, lifted_other, inv_hi, inv_lo, perm_hi, perm_lo = call(
+    cut = path // 2 + 8
+    pieces = [inside((cut, columns)), inside((2 * path - cut, columns))]
+    sent_first, sent_second, rhs_own, lifted_other, inv_hi, inv_lo, perm_hi, perm_lo = call(
         functools.partial(lift_kernel, plan, order, columns),
-        [inside((2, path, columns)), inside((order, 2 * columns)), inside((order, 2 * columns)),
+        pieces + [inside((order, 2 * columns)), inside((order, 2 * columns)),
          inside((order, order), BF16), inside((order, order), BF16),
          inside((path, order), BF16), inside((path, order), BF16)],
         [rhs_in, leaf_inv, leaf_coupling, coupling_rows],
@@ -312,51 +332,53 @@
                  pltpu.VMEM((path, order), F32), pltpu.VMEM((1, path), jnp.int32), *halves,
                  pltpu.SemaphoreType.DMA((7,))],
         anys=(0, 1, 2, 3), name="lift")
-    came = plan.swap_rhs(sent, 1)
-    own, lifted_own = call(
+    came_first, came_second = plan.swap_rhs(sent_first, 1), plan.swap_rhs(sent_second, 1)
+    first, second, lifted_own = call(
         functools.partial(own_kernel, plan),
-        [inside((2, path, columns)), inside((order, 2 * columns))],
+        pieces + [inside((order, 2 * columns))],
         [rhs_own, inv_hi, inv_lo, perm_hi, perm_lo, rhs_top], scratch=halves, name="own")
-    far = own[0] + came[0]
-    near = own[1] + came[1]
+    sent = [first + came_first, second[: path - cut] + came_second[: path - cut]]
+    near = second[path - cut :] + came_second[path - cut :]
     base_own, base_other, gain_hi, gain_lo, token = call(
         turn_kernel,
         [inside((order, 2 * columns)), inside((order, 2 * columns)),
          inside((order, path), BF16), inside((order, path), BF16), inside((8, columns))],
-        [inv_hi, inv_lo, perm_hi, perm_lo, lifted_own, lifted_other], name="turn", after=[far])
-    value = near + plan.swap_rhs(far, 2) + token[:1]
+        [inv_hi, inv_lo, perm_hi, perm_lo, lifted_own, lifted_other], name="turn", after=sent)
+    came = [plan.swap_rhs(part, 2) for part in sent]
+    values = [near[rows] + part + token[:1] for rows, part in zip((slice(0, cut), slice(cut, path)), came)]
     backs = (panel_count, width, levels * width)
     inv, coup, back_hi, back_lo = call(
         functools.partial(ready_kernel, levels),
         [inside(top_inv.shape), inside(top_coupling.shape), inside(backs, BF16), inside(backs, BF16)],
-        [top_inv, top_coupling], name="ready", after=[value])
+        [top_inv, top_coupling], name="ready", after=values[1:])
     bit = 1
     while bit < plan.sharers // 2:
-        value = value + plan.swap_leaf(value, bit)
+        values = [value + plan.swap_leaf(value, bit) for value in values]
         bit *= 2
-    came = plan.swap_leaf(value, bit)
+    came = [plan.swap_leaf(value, bit) for value in values]
+    value, came = values, came
 
     forwards, stacks, known = [], [], []
     for level in range(levels - 1):
-        forward, value = call(
-            functools.partial(climb_kernel, plan, level),
+        forward, rest = call(
+            functools.partial(climb_kernel, plan, level, len(value)),
             [inside((width, columns)), inside(((levels - 1 - level) * width, columns))],
-            [value, came, inv, coup], name="climb")
+            value + came + [inv, coup], name="climb")
         bit = plan.sharers * 2**level
-        came = plan.swap_leaf(value, bit)
+        value, came = [rest], [plan.swap_leaf(rest, bit)]
         forwards.append(forward)
         known = known + stacks[-1:] + [forward[None]]
         if level == levels - 2:
             stack = call(
                 functools.partial(halve_kernel, plan),
-                [inside((2 ** (level + 1) - 1, width // 2, columns))], known, name="halve", after=[value])[0]
+                [inside((2 ** (level + 1) - 1, width // 2, columns))], known, name="halve", after=[rest])[0]
         else:
             stack = jnp.concatenate(known, 0)
         stacks.append(plan.swap_leaf(stack, bit))
     solved = call(
         functools.partial(descend_kernel, plan),
         [inside((path, columns))],
-        [value, came, inv, back_hi, back_lo] + forwards, name="descend", after=stacks[:-1])[0]
+        value + came + [inv, back_hi, back_lo] + forwards, name="descend", after=stacks[:-1])[0]
 
     far = plan.swap_rhs(solved, 2)
 
@@ -373,14 +395,14 @@
     far, token = settle(far, base_own, 0)
     top = call(
         functools.partial(top_kernel, plan),
-        [(jax.ShapeDtypeStruct((panel_count * width, columns), F32), VMEM_SPEC)],
+        [inside((panel_count * width, columns))],
         [solved, back_hi, back_lo] + stacks, name="top", after=[token], flops=5 * 10**9)[0]
-    out = call(
+    out, top = call(
         functools.partial(last_kernel, plan, columns),
-        [(pltpu.HBM((order, plan.group_count * columns), F32), HBM_SPEC)],
-        [last, base_other, gain_hi, gain_lo, own, far],
-        scratch=[pltpu.VMEM((order, 2 * columns), F32), pltpu.SemaphoreType.DMA((4,))], name="last",
-        after_hbm=[top])[0]
+        [(pltpu.HBM((order, plan.group_count * columns), F32), HBM_SPEC),
+         (pltpu.HBM((panel_count * width, columns), F32), HBM_SPEC)],
+        [last, base_other, gain_hi, gain_lo, own, far, top],
+        scratch=[pltpu.VMEM((order, 2 * columns), F32), pltpu.SemaphoreType.DMA((7,))], name="last")
     return out, top
 
 

time: 43 us -> 41.7 us (0.970)
  waiting for transfers between devices: 15.7 us -> 13.7 us
  starting transfers between devices: 14.4 us -> 15.7 us
  Pallas kernels: 11.8 us -> 11.1 us
    ppermute x10 -> x13, waiting for transfers between devices: 15.7 us -> 13.7 us  [swap(): return lax.ppermute(value, ('leaf', 'rhs'), pairs)]
    ppermute x10 -> x13, starting transfers between devices: 14.4 us -> 15.7 us  [swap(): return lax.ppermute(value, ('leaf', 'rhs'), pairs)]
    pallas_call x12, Pallas kernels: 11.8 us -> 11.1 us  [call(): pl.pallas_call(body, out_shape=[shape for shape, _ in outs], in_specs=spe...]
  transfers between devices with their start and end apart: 10 -> 13, of which waited for: 7 -> 9; matrix products, arithmetic and copies ran while one was open for 0% -> 0% of each run, Pallas kernels for 16% -> 15%
where the time goes in v5:
time: 41.7 us; the launch traced here: 41.5 us
  starting transfers between devices  15.7 us (38%)
  waiting for transfers between devices  13.7 us (33%)
  Pallas kernels  11.1 us (27%)
  between operations  0.8 us (2%)
    ppermute x13, starting transfers between devices, swap(): return lax.ppermute(value, ('leaf', 'rhs'), pairs)  15.7 us
    ppermute x13, waiting for transfers between devices, swap(): return lax.ppermute(value, ('leaf', 'rhs'), pairs)  13.7 us
    pallas_call x12, Pallas kernels, call(): pl.pallas_call(body, out_shape=[shape for shape, _ in outs], in_specs=spe...  11.1 us
  transfers between devices with their start and end apart: 13, of which 9 were waited for; matrix products, arithmetic and copies ran while one was open for 0% of the time, Pallas kernels for 15%

profile of v5, /device:TPU:0, one launch (start us, length us, event | category | flops | bytes accessed | tf_op | source)
XLA Modules:
  0.0 41.5 jit_solution(1072837658104904959)
XLA Ops:
  0.6 3.0 %lift.1 = (f32[200,128]{1,0:T(8,128)S(1)}, f32[568,128]{1,0:T(8,128)S(1)}, f32[512,256]{1,0:T(8,128)S(1)}, f32[512,256]{1,0:T(8,128)S(1)}, bf16[512,512]{1,0:T(8...) custom-call(f32[512,512]{1,0:T(8,128)} %refs_0_.2, ...), custom_call_target="tpu_custom_call" | custom-call | flops 1000 | bytes 1000 | tf_op jit(solution)/shard_map/lift/pallas_call | solution.py:297
  3.7 0.5 %collective-permute-start = (f32[568,128]{1,0:T(8,128)S(1)}, f32[568,128]{1,0:T(8,128)S(1)}, u32[]{:S(2)}, u32[]{:S(2)}) collective-permute-start(f32[568,128]{1,0:T(8,128)S(1)} %get-tuple-element.36), channel_id=1, source_target_pairs={{0,1},{1,0},{2,3},{3,2},{4,5},{5,4},{6,7},{7,6},{8,9},{9,8},{10,11... | collective-permute-start | bytes 872456 | tf_op jit(solution)/shard_map/ppermute | solution.py:63
  4.2 0.1 collective-permute-start.1
  4.2 1.1 %own.1 = (f32[200,128]{1,0:T(8,128)S(1)}, f32[568,128]{1,0:T(8,128)S(1)}, f32[512,256]{1,0:T(8,128)S(1)}) custom-call(f32[512,256]{1,0:T(8,128)S(1)} %get-tuple-element.30.refs_0_, bf16[512,512]{1,0:T(8,128)(2,1)S(1)} %get-tuple-element.31.refs_1_.refs_0_, bf16[512,512]{1,0:T(8,128)(2,1)S(1)} %get-tuple-element.32.refs_2_.refs_1_, ...), custom_call_target="tpu_custom_call" | custom-call | flops 1000 | bytes 1000 | tf_op jit(solution)/shard_map/own/pallas_call | solution.py:297
  5.3 0.2 collective-permute-done.1
  5.5 2.9 %collective-permute-start.2 = (f32[200,128]{1,0:T(8,128)S(1)}, f32[200,128]{1,0:T(8,128)S(1)}, u32[]{:S(2)}, u32[]{:S(2)}) collective-permute-start(f32[200,128]{1,0:T(8,128)S(1)} %add.52.refs_6_), channel_id=1, source_target_pairs={{0,2},{1,3},{2,0},{3,1},{4,6},{5,7},{6,4},{7,5},{8,10},{9,11},{10,... | collective-permute-start | bytes 307208 | tf_op jit(solution)/shard_map/ppermute | solution.py:63
  8.5 0.1 collective-permute-start.3
  8.6 1.8 %turn.1 = (f32[512,256]{1,0:T(8,128)S(1)}, f32[512,256]{1,0:T(8,128)S(1)}, bf16[512,384]{1,0:T(8,128)(2,1)S(1)}, bf16[512,384]{1,0:T(8,128)(2,1)S(1)}, f32[8,128]{1,0:T(8,128)S(1)}) custom-call(bf16[512,512]{1,0:T(8,128)(2,1)S(1)} %get-tuple-element.31.refs_1_.refs_0_, bf16[512,512]{1,0:T(8,128)(2,1)S(1)} %get-tuple-element.32.refs_2_.refs_1_, ...), custom_call_target="tpu_custom_call" | custom-call | flops 1000 | bytes 1000 | tf_op jit(solution)/shard_map/turn/pallas_call | solution.py:297
  10.4 1.7 %collective-permute-done.2 = f32[200,128]{1,0:T(8,128)S(1)} collective-permute-done((f32[200,128]{1,0:T(8,128)S(1)}, f32[200,128]{1,0:T(8,128)S(1)}, u32[]{:S(2)}, u32[]{:S(2)}) %collective-permute-start.2) | collective-permute-done | bytes 102432 | tf_op jit(solution)/shard_map/ppermute | solution.py:63
  12.1 2.2 %collective-permute-start.4 = (f32[200,128]{1,0:T(8,128)S(1)}, f32[200,128]{1,0:T(8,128)S(1)}, u32[]{:S(2)}, u32[]{:S(2)}) collective-permute-start(f32[200,128]{1,0:T(8,128)S(1)} %fusion.refs_0_), channel_id=1, source_target_pairs={{0,4},{1,5},{2,6},{3,7},{4,0},{5,1},{6,2},{7,3},{8,12},{9,13},{10,... | collective-permute-start | bytes 307208 | tf_op jit(solution)/shard_map/ppermute | solution.py:63
  14.3 1.2 %collective-permute-start.5 = (f32[184,128]{1,0:T(8,128)S(1)}, f32[184,128]{1,0:T(8,128)S(1)}, u32[]{:S(2)}, u32[]{:S(2)}) collective-permute-start(f32[184,128]{1,0:T(8,128)S(1)} %fusion.1.refs_2_.refs_1_), channel_id=1, source_target_pairs={{0,4},{1,5},{2,6},{3,7},{4,0},{5,1},{6,2},{7,3},{8,12},{9,13},{10,... | collective-permute-start | bytes 282632 | tf_op jit(solution)/shard_map/ppermute | solution.py:63
  15.5 0.8 %ready.1 = (f32[7,128,128]{2,1,0:T(8,128)S(1)}, f32[10,128,128]{2,1,0:T(8,128)S(1)}, bf16[7,128,384]{2,1,0:T(8,128)(2,1)S(1)}, bf16[7,128,384]{2,1,0:T(8,128)(2,1)S(1)}) custom-call(f32[7,128,128]{2,1,0:T(8,128)S(1)} %copy-done.1, f32[10,128,128]{2,1,0:T(8,128)S(1)} %copy-done, f32[184,128]{1,0:T(8,128)S(1)} %fusion.1.refs_2_.refs_1_), custom_call_target="tpu_custom_call" | custom-call | flops 1000 | bytes 1000 | tf_op jit(solution)/shard_map/ready/pallas_call | solution.py:297
  16.4 1.5 %collective-permute-done.4.refs_2_ = f32[200,128]{1,0:T(8,128)S(1)} collective-permute-done((f32[200,128]{1,0:T(8,128)S(1)}, f32[200,128]{1,0:T(8,128)S(1)}, u32[]{:S(2)}, u32[]{:S(2)}) %collective-permute-start.4) | collective-permute-done | bytes 102432 | tf_op jit(solution)/shard_map/ppermute | solution.py:63
  17.9 1.0 %collective-permute-done.5.refs_3_ = f32[184,128]{1,0:T(8,128)S(1)} collective-permute-done((f32[184,128]{1,0:T(8,128)S(1)}, f32[184,128]{1,0:T(8,128)S(1)}, u32[]{:S(2)}, u32[]{:S(2)}) %collective-permute-start.5) | collective-permute-done | bytes 94240 | tf_op jit(solution)/shard_map/ppermute | solution.py:63
  19.0 0.4 climb.2
  19.4 1.7 %collective-permute-start.6 = (f32[256,128]{1,0:T(8,128)S(1)}, f32[256,128]{1,0:T(8,128)S(1)}, u32[]{:S(2)}, u32[]{:S(2)}) collective-permute-start(f32[256,128]{1,0:T(8,128)S(1)} %get-tuple-element.44.refs_0_), channel_id=1, source_target_pairs={{0,8},{1,9},{2,10},{3,11},{4,12},{5,13},{6,14},{7,15},{8,0},{9,1},... | collective-permute-start | bytes 393224 | tf_op jit(solution)/shard_map/ppermute | solution.py:63
  21.1 0.4 collective-permute-start.8
  21.4 3.1 %collective-permute-done.6.refs_1_ = f32[256,128]{1,0:T(8,128)S(1)} collective-permute-done((f32[256,128]{1,0:T(8,128)S(1)}, f32[256,128]{1,0:T(8,128)S(1)}, u32[]{:S(2)}, u32[]{:S(2)}) %collective-permute-start.6) | collective-permute-done | bytes 131104 | tf_op jit(solution)/shard_map/ppermute | solution.py:63
  24.6 0.3 climb.3
  25.0 2.5 %collective-permute-start.7 = (f32[128,128]{1,0:T(8,128)S(1)}, f32[128,128]{1,0:T(8,128)S(1)}, u32[]{:S(2)}, u32[]{:S(2)}) collective-permute-start(f32[128,128]{1,0:T(8,128)S(1)} %get-tuple-element.45.refs_0_.refs_3_), channel_id=1, source_target_pairs={{0,16},{1,17},{2,18},{3,19},{4,20},{5,21},{6,22},{7,23},{8,24},{9,... | collective-permute-start | bytes 196616 | tf_op jit(solution)/shard_map/ppermute | solution.py:63
  27.5 1.0 %collective-permute-start.11 = (f32[3,64,128]{2,1,0:T(8,128)S(1)}, f32[3,64,128]{2,1,0:T(8,128)S(1)}, u32[]{:S(2)}, u32[]{:S(2)}) collective-permute-start(f32[3,64,128]{2,1,0:T(8,128)S(1)} %halve.1), channel_id=1, source_target_pairs={{0,16},{1,17},{2,18},{3,19},{4,20},{5,21},{6,22},{7,23},{8,24},{9,... | collective-permute-start | bytes 294920 | tf_op jit(solution)/shard_map/ppermute | solution.py:63
  28.4 3.3 %collective-permute-done.7.refs_1_ = f32[128,128]{1,0:T(8,128)S(1)} collective-permute-done((f32[128,128]{1,0:T(8,128)S(1)}, f32[128,128]{1,0:T(8,128)S(1)}, u32[]{:S(2)}, u32[]{:S(2)}) %collective-permute-start.7) | collective-permute-done | bytes 65568 | tf_op jit(solution)/shard_map/ppermute | solution.py:63
  31.8 0.8 %descend.1.refs_0_ = f32[384,128]{1,0:T(8,128)S(1)} custom-call(f32[128,128]{1,0:T(8,128)S(1)} %get-tuple-element.45.refs_0_.refs_3_, f32[128,128]{1,0:T(8,128)S(1)} %collective-permute-done.7.refs_1_, f32[7,128,128]{2,1,0:T(8,128)S(1)} %get-tuple-element.42.refs_4_.refs_2_, bf16[7,128,384]{2,1,0:T(8,128)(2,1)S(1)} %get-tuple-element.46.refs_3_.refs_1_, ...), custom_call_target="tpu_custom_call" | custom-call | flops 1000 | bytes 1000 | tf_op jit(solution)/shard_map/descend/pallas_call | solution.py:297
  32.5 1.6 %collective-permute-start.9 = (f32[384,128]{1,0:T(8,128)S(1)}, f32[384,128]{1,0:T(8,128)S(1)}, u32[]{:S(2)}, u32[]{:S(2)}) collective-permute-start(f32[384,128]{1,0:T(8,128)S(1)} %descend.1.refs_0_), channel_id=1, source_target_pairs={{0,2},{1,3},{2,0},{3,1},{4,6},{5,7},{6,4},{7,5},{8,10},{9,11},{10,... | collective-permute-start | bytes 589832 | tf_op jit(solution)/shard_map/ppermute | solution.py:63
  34.1 0.5 %settle.2 = (f32[512,128]{1,0:T(8,128)S(1)}, f32[8,128]{1,0:T(8,128)S(1)}) custom-call(f32[384,128]{1,0:T(8,128)S(1)} %descend.1.refs_0_, f32[512,256]{1,0:T(8,128)S(1)} %get-tuple-element.50.refs_1_, bf16[512,384]{1,0:T(8,128)(2,1)S(1)} %get-tuple-element.51.refs_2_, bf16[512,384]{1,0:T(8,128)(2,1)S(1)} %get-tuple-element.52.refs_3_), custom_call_target="tpu_custom_call" | custom-call | flops 1000 | bytes 1000 | tf_op jit(solution)/shard_map/settle/pallas_call | solution.py:297
  34.6 1.6 %collective-permute-start.12 = (f32[3,64,128]{2,1,0:T(8,128)S(1)}, f32[3,64,128]{2,1,0:T(8,128)S(1)}, u32[]{:S(2)}, u32[]{:S(2)}) collective-permute-start(f32[3,64,128]{2,1,0:T(8,128)S(1)} %broadcast_add_fusion), channel_id=1, source_target_pairs={{0,4},{1,5},{2,6},{3,7},{4,0},{5,1},{6,2},{7,3},{8,12},{9,13},{10,... | collective-permute-start | bytes 294920 | tf_op jit(solution)/shard_map/ppermute | solution.py:63
  36.2 2.1 %collective-permute-done.9.refs_0_ = f32[384,128]{1,0:T(8,128)S(1)} collective-permute-done((f32[384,128]{1,0:T(8,128)S(1)}, f32[384,128]{1,0:T(8,128)S(1)}, u32[]{:S(2)}, u32[]{:S(2)}) %collective-permute-start.9) | collective-permute-done | bytes 196640 | tf_op jit(solution)/shard_map/ppermute | solution.py:63
  38.4 0.5 %settle.3 = (f32[512,128]{1,0:T(8,128)S(1)}, f32[8,128]{1,0:T(8,128)S(1)}) custom-call(f32[384,128]{1,0:T(8,128)S(1)} %collective-permute-done.9.refs_0_, f32[512,256]{1,0:T(8,128)S(1)} %get-tuple-element.50.refs_1_, bf16[512,384]{1,0:T(8,128)(2,1)S(1)} %get-tuple-element.51.refs_2_, bf16[512,384]{1,0:T(8,128)(2,1)S(1)} %get-tuple-element.52.refs_3_), custom_call_target="tpu_custom_call" | custom-call | flops 1000 | bytes 1000 | tf_op jit(solution)/shard_map/settle/pallas_call | solution.py:297
  38.9 0.4 collective-permute-done.12.refs_5_
  39.3 0.5 %top.1.refs_6_ = f32[896,128]{1,0:T(8,128)S(1)} custom-call(f32[384,128]{1,0:T(8,128)S(1)} %descend.1.refs_0_, bf16[7,128,384]{2,1,0:T(8,128)(2,1)S(1)} %get-tuple-element.46.refs_3_.refs_1_, bf16[7,128,384]{2,1,0:T(8,128)(2,1)S(1)} %get-tuple-element.47.refs_4_.refs_2_, f32[1,128,128]{2,1,0:T(8,128)S(1)} %collective-permute-done.8.refs_7_.refs_1_.refs_3_, ...), custom_call_target="tpu_custom_call" | custom-call | flops 5000000000 | bytes 1000 | tf_op jit(solution)/shard_map/top/pallas_call | solution.py:297
  39.8 0.3 collective-permute-done.10.refs_0_
  40.1 1.4 %last.1 = (f32[512,512]{1,0:T(8,128)}, f32[896,128]{1,0:T(8,128)}) custom-call(f32[2,384,128]{2,1,0:T(8,128)S(1)} %collective-permute-done.10.refs_0_, f32[512,256]{1,0:T(8,128)S(1)} %get-tuple-element.54.refs_1_, bf16[512,384]{1,0:T(8,128)(2,1)S(1)} %get-tuple-element.51.refs_2_, bf16[512,384]{1,0:T(8,128)(2,1)S(1)} %get-tuple-element.52.refs_3_, ...), custom_call_target="tpu_custom_call" | custom-call | flops 1000 | bytes 1000 | tf_op jit(solution)/shard_map/last/pallas_call | solution.py:297
  (22 shorter events, 0.3 us)
Async XLA Ops:
  0.6 3.6 %copy-start.2 = (f32[896,128]{1,0:T(8,128)S(1)}, f32[896,128]{1,0:T(8,128)}, u32[]{:S(2)}) copy-start(f32[896,128]{1,0:T(8,128)} %refs_5_.1) | copy-start | bytes 1376260
  3.6 11.9 %copy-start = (f32[10,128,128]{2,1,0:T(8,128)S(1)}, f32[10,128,128]{2,1,0:T(8,128)}, u32[]{:S(2)}) copy-start(f32[10,128,128]{2,1,0:T(8,128)} %refs_1_.3) | copy-start | bytes 1966084
  3.6 11.9 %copy-start.1 = (f32[7,128,128]{2,1,0:T(8,128)S(1)}, f32[7,128,128]{2,1,0:T(8,128)}, u32[]{:S(2)}) copy-start(f32[7,128,128]{2,1,0:T(8,128)} %refs_0_.3) | copy-start | bytes 1376260
  3.7 4.8 %collective-permute-start = (f32[568,128]{1,0:T(8,128)S(1)}, f32[568,128]{1,0:T(8,128)S(1)}, u32[]{:S(2)}, u32[]{:S(2)}) collective-permute-start(f32[568,128]{1,0:T(8,128)S(1)} %get-tuple-element.36), channel_id=1, source_target_pairs={{0,1},{1,0},{2,3},{3,2},{4,5},{5,4},{6,7},{7,6},{8,9},{9,8},{10,11... | collective-permute-start | bytes 872456 | tf_op jit(solution)/shard_map/ppermute | solution.py:63
  4.2 1.3 %collective-permute-start.1 = (f32[200,128]{1,0:T(8,128)S(1)}, f32[200,128]{1,0:T(8,128)S(1)}, u32[]{:S(2)}, u32[]{:S(2)}) collective-permute-start(f32[200,128]{1,0:T(8,128)S(1)} %get-tuple-element.38), channel_id=1, source_target_pairs={{0,1},{1,0},{2,3},{3,2},{4,5},{5,4},{6,7},{7,6},{8,9},{9,8},{10,11... | collective-permute-start | bytes 307208 | tf_op jit(solution)/shard_map/ppermute | solution.py:63
  5.5 6.6 %collective-permute-start.2 = (f32[200,128]{1,0:T(8,128)S(1)}, f32[200,128]{1,0:T(8,128)S(1)}, u32[]{:S(2)}, u32[]{:S(2)}) collective-permute-start(f32[200,128]{1,0:T(8,128)S(1)} %add.52.refs_6_), channel_id=1, source_target_pairs={{0,2},{1,3},{2,0},{3,1},{4,6},{5,7},{6,4},{7,5},{8,10},{9,11},{10,... | collective-permute-start | bytes 307208 | tf_op jit(solution)/shard_map/ppermute | solution.py:63
  8.5 5.8 %collective-permute-start.3 = (f32[184,128]{1,0:T(8,128)S(1)}, f32[184,128]{1,0:T(8,128)S(1)}, u32[]{:S(2)}, u32[]{:S(2)}) collective-permute-start(f32[184,128]{1,0:T(8,128)S(1)} %slice_add_fusion.3.refs_7_), channel_id=1, source_target_pairs={{0,2},{1,3},{2,0},{3,1},{4,6},{5,7},{6,4},{7,5},{8,10},{9,11},{10,... | collective-permute-start | bytes 282632 | tf_op jit(solution)/shard_map/ppermute | solution.py:63
  12.1 5.8 %collective-permute-start.4 = (f32[200,128]{1,0:T(8,128)S(1)}, f32[200,128]{1,0:T(8,128)S(1)}, u32[]{:S(2)}, u32[]{:S(2)}) collective-permute-start(f32[200,128]{1,0:T(8,128)S(1)} %fusion.refs_0_), channel_id=1, source_target_pairs={{0,4},{1,5},{2,6},{3,7},{4,0},{5,1},{6,2},{7,3},{8,12},{9,13},{10,... | collective-permute-start | bytes 307208 | tf_op jit(solution)/shard_map/ppermute | solution.py:63
  14.3 4.6 %collective-permute-start.5 = (f32[184,128]{1,0:T(8,128)S(1)}, f32[184,128]{1,0:T(8,128)S(1)}, u32[]{:S(2)}, u32[]{:S(2)}) collective-permute-start(f32[184,128]{1,0:T(8,128)S(1)} %fusion.1.refs_2_.refs_1_), channel_id=1, source_target_pairs={{0,4},{1,5},{2,6},{3,7},{4,0},{5,1},{6,2},{7,3},{8,12},{9,13},{10,... | collective-permute-start | bytes 282632 | tf_op jit(solution)/shard_map/ppermute | solution.py:63
  19.4 5.2 %collective-permute-start.6 = (f32[256,128]{1,0:T(8,128)S(1)}, f32[256,128]{1,0:T(8,128)S(1)}, u32[]{:S(2)}, u32[]{:S(2)}) collective-permute-start(f32[256,128]{1,0:T(8,128)S(1)} %get-tuple-element.44.refs_0_), channel_id=1, source_target_pairs={{0,8},{1,9},{2,10},{3,11},{4,12},{5,13},{6,14},{7,15},{8,0},{9,1},... | collective-permute-start | bytes 393224 | tf_op jit(solution)/shard_map/ppermute | solution.py:63
  21.1 6.4 %collective-permute-start.8 = (f32[1,128,128]{2,1,0:T(8,128)S(1)}, f32[1,128,128]{2,1,0:T(8,128)S(1)}, u32[]{:S(2)}, u32[]{:S(2)}) collective-permute-start(f32[1,128,128]{2,1,0:T(8,128)S(1)} %bitcast.10), channel_id=1, source_target_pairs={{0,8},{1,9},{2,10},{3,11},{4,12},{5,13},{6,14},{7,15},{8,0},{9,1},... | collective-permute-start | bytes 196616 | tf_op jit(solution)/shard_map/ppermute | solution.py:63
  25.0 6.8 %collective-permute-start.7 = (f32[128,128]{1,0:T(8,128)S(1)}, f32[128,128]{1,0:T(8,128)S(1)}, u32[]{:S(2)}, u32[]{:S(2)}) collective-permute-start(f32[128,128]{1,0:T(8,128)S(1)} %get-tuple-element.45.refs_0_.refs_3_), channel_id=1, source_target_pairs={{0,16},{1,17},{2,18},{3,19},{4,20},{5,21},{6,22},{7,23},{8,24},{9,... | collective-permute-start | bytes 196616 | tf_op jit(solution)/shard_map/ppermute | solution.py:63
  27.5 7.1 %collective-permute-start.11 = (f32[3,64,128]{2,1,0:T(8,128)S(1)}, f32[3,64,128]{2,1,0:T(8,128)S(1)}, u32[]{:S(2)}, u32[]{:S(2)}) collective-permute-start(f32[3,64,128]{2,1,0:T(8,128)S(1)} %halve.1), channel_id=1, source_target_pairs={{0,16},{1,17},{2,18},{3,19},{4,20},{5,21},{6,22},{7,23},{8,24},{9,... | collective-permute-start | bytes 294920 | tf_op jit(solution)/shard_map/ppermute | solution.py:63
  32.5 5.7 %collective-permute-start.9 = (f32[384,128]{1,0:T(8,128)S(1)}, f32[384,128]{1,0:T(8,128)S(1)}, u32[]{:S(2)}, u32[]{:S(2)}) collective-permute-start(f32[384,128]{1,0:T(8,128)S(1)} %descend.1.refs_0_), channel_id=1, source_target_pairs={{0,2},{1,3},{2,0},{3,1},{4,6},{5,7},{6,4},{7,5},{8,10},{9,11},{10,... | collective-permute-start | bytes 589832 | tf_op jit(solution)/shard_map/ppermute | solution.py:63
  34.6 4.7 %collective-permute-start.12 = (f32[3,64,128]{2,1,0:T(8,128)S(1)}, f32[3,64,128]{2,1,0:T(8,128)S(1)}, u32[]{:S(2)}, u32[]{:S(2)}) collective-permute-start(f32[3,64,128]{2,1,0:T(8,128)S(1)} %broadcast_add_fusion), channel_id=1, source_target_pairs={{0,4},{1,5},{2,6},{3,7},{4,0},{5,1},{6,2},{7,3},{8,12},{9,13},{10,... | collective-permute-start | bytes 294920 | tf_op jit(solution)/shard_map/ppermute | solution.py:63
  38.3 1.8 %collective-permute-start.10 = (f32[2,384,128]{2,1,0:T(8,128)S(1)}, f32[2,384,128]{2,1,0:T(8,128)S(1)}, u32[]{:S(2)}, u32[]{:S(2)}) collective-permute-start(f32[2,384,128]{2,1,0:T(8,128)S(1)} %pad_maximum_fusion), channel_id=1, source_target_pairs={{0,1},{1,0},{2,3},{3,2},{4,5},{5,4},{6,7},{7,6},{8,9},{9,8},{10,11... | collective-permute-start | bytes 1179656 | tf_op jit(solution)/shard_map/ppermute | solution.py:63

commit v6 on v5

--- a/solution.py
+++ b/solution.py
@@ -48,11 +48,6 @@
     def panel(self, place, level, flip=0):
         depth = self.levels - 1 - level
         return 2**depth - 1 + ((place >> level) ^ flip)
-
-    def pair(self, place, below, above, flip=0):
-        depth = self.levels - 1 - below
-        before = sum(d * 2**d for d in range(depth))
-        return before + ((place >> below) ^ flip) * depth + (above - below - 1)
 
     def swap(self, value, partner):
         pairs = []
@@ -139,20 +134,20 @@
             second[start : start + plan.width] += top[lanes(plan.panel(place, level), plan.width), :]
 
 
-def ready_kernel(levels, top_inv, top_coup, inv, coup, back_hi, back_lo):
+def ready_kernel(top_inv, top_coup, fore_hi, fore_lo, back_hi, back_lo):
     width = top_inv.shape[1]
     first = 0
     for number in range(top_inv.shape[0]):
         depth = (number + 1).bit_length() - 1
-        inv[number] = top_inv[number]
-        turned = top_inv[number].T
+        inv = top_inv[number]
+        turned = inv.T
+        fore_hi[number, :width], fore_lo[number, :width] = split(inv)
         back_hi[number, :, :width], back_lo[number, :, :width] = split(turned)
         for step in range(depth):
-            pair = first + step
-            coup[pair] = top_coup[pair]
-            columns = pl.ds((step + 1) * width, width)
-            back_hi[number, :, columns], back_lo[number, :, columns] = split(
-                -dot_high(turned, top_coup[pair].T))
+            change = dot_high(top_coup[first + step], inv)
+            place = pl.ds((step + 1) * width, width)
+            fore_hi[number, place], fore_lo[number, place] = split(change)
+            back_hi[number, :, place], back_lo[number, :, place] = split(-change.T)
         first += depth
 
 
@@ -170,14 +165,14 @@
     _, place, _, _ = plan.here()
     width = plan.width
     above = plan.levels - 1 - level
-    inv, coup, forward, rest = refs[2 * count :]
+    fore_hi, fore_lo, forward, rest = refs[2 * count :]
     parts = [value[...] + came[...] for value, came in zip(refs[:count], refs[count : 2 * count])]
     total = jnp.concatenate(parts, 0) if count > 1 else parts[0]
-    result = dot_high(inv[plan.panel(place, level)], total[:width])
-    forward[...] = result
-    pairs = coup[pl.ds(plan.pair(place, level, level + 1), above)]
-    change = dot_high(pairs.reshape(above * width, width), result)
-    rest[...] = total[width:] - change
+    panel = plan.panel(place, level)
+    result = dot_split(
+        fore_hi[panel, : (above + 1) * width], fore_lo[panel, : (above + 1) * width], total[:width])
+    forward[...] = result[:width]
+    rest[...] = total[width:] - result[width:]
 
 
 def backward(plan, back_hi, back_lo, panel, level, forward, above):
@@ -197,11 +192,11 @@
 
 def descend_kernel(plan, *refs):
     levels, width = plan.levels, plan.width
-    value, came, inv, back_hi, back_lo = refs[:5]
-    forwards = refs[5 : 5 + levels - 1]
-    solved = refs[5 + levels - 1]
+    value, came, fore_hi, fore_lo, back_hi, back_lo = refs[:6]
+    forwards = refs[6 : 6 + levels - 1]
+    solved = refs[6 + levels - 1]
     _, place, _, _ = plan.here()
-    top = dot_high(inv[0], value[...] + came[...])
+    top = dot_split(fore_hi[0, :width], fore_lo[0, :width], value[...] + came[...])
     above = []
     for level in reversed(range(levels)):
         forward = top if level == levels - 1 else forwards[level][...]
@@ -346,10 +341,10 @@
         [inv_hi, inv_lo, perm_hi, perm_lo, lifted_own, lifted_other], name="turn", after=sent)
     came = [plan.swap_rhs(part, 2) for part in sent]
     values = [near[rows] + part + token[:1] for rows, part in zip((slice(0, cut), slice(cut, path)), came)]
-    backs = (panel_count, width, levels * width)
-    inv, coup, back_hi, back_lo = call(
-        functools.partial(ready_kernel, levels),
-        [inside(top_inv.shape), inside(top_coupling.shape), inside(backs, BF16), inside(backs, BF16)],
+    fores, backs = (panel_count, levels * width, width), (panel_count, width, levels * width)
+    fore_hi, fore_lo, back_hi, back_lo = call(
+        ready_kernel,
+        [inside(fores, BF16), inside(fores, BF16), inside(backs, BF16), inside(backs, BF16)],
         [top_inv, top_coupling], name="ready", after=values[1:])
     bit = 1
     while bit < plan.sharers // 2:
@@ -363,7 +358,7 @@
         forward, rest = call(
             functools.partial(climb_kernel, plan, level, len(value)),
             [inside((width, columns)), inside(((levels - 1 - level) * width, columns))],
-            value + came + [inv, coup], name="climb")
+            value + came + [fore_hi, fore_lo], name="climb")
         bit = plan.sharers * 2**level
         value, came = [rest], [plan.swap_leaf(rest, bit)]
         forwards.append(forward)
@@ -378,7 +373,7 @@
     solved = call(
         functools.partial(descend_kernel, plan),
         [inside((path, columns))],
-        value + came + [inv, back_hi, back_lo] + forwards, name="descend", after=stacks[:-1])[0]
+        value + came + [fore_hi, fore_lo, back_hi, back_lo] + forwards, name="descend", after=stacks[:-1])[0]
 
     far = plan.swap_rhs(solved, 2)
 

time: 41.7 us -> 41.4 us (level)
  Pallas kernels: 11.1 us -> 10.5 us
    pallas_call x12, Pallas kernels: 11.1 us -> 10.5 us  [call(): pl.pallas_call(body, out_shape=[shape for shape, _ in outs], in_specs=spe...]
  transfers between devices with their start and end apart: 13 -> 13, of which waited for: 9 -> 9; matrix products, arithmetic and copies ran while one was open for 0% -> 0% of each run, Pallas kernels for 15% -> 14%
where the time goes in v6:
time: 41.4 us; the launch traced here: 41.2 us
  starting transfers between devices  16 us (39%)
  waiting for transfers between devices  13.7 us (33%)
  Pallas kernels  10.5 us (25%)
  between operations  0.81 us (2%)
    ppermute x13, starting transfers between devices, swap(): return lax.ppermute(value, ('leaf', 'rhs'), pairs)  16 us
    ppermute x13, waiting for transfers between devices, swap(): return lax.ppermute(value, ('leaf', 'rhs'), pairs)  13.7 us
    pallas_call x12, Pallas kernels, call(): pl.pallas_call(body, out_shape=[shape for shape, _ in outs], in_specs=spe...  10.5 us
  transfers between devices with their start and end apart: 13, of which 9 were waited for; matrix products, arithmetic and copies ran while one was open for 0% of the time, Pallas kernels for 14%

profile of v6, /device:TPU:0, one launch (start us, length us, event | category | flops | bytes accessed | tf_op | source)
XLA Modules:
  0.0 41.2 jit_solution(13674566840740544486)
XLA Ops:
  0.6 3.0 %lift.1 = (f32[200,128]{1,0:T(8,128)S(1)}, f32[568,128]{1,0:T(8,128)S(1)}, f32[512,256]{1,0:T(8,128)S(1)}, f32[512,256]{1,0:T(8,128)S(1)}, bf16[512,512]{1,0:T(8...) custom-call(f32[512,512]{1,0:T(8,128)} %refs_0_.2, ...), custom_call_target="tpu_custom_call" | custom-call | flops 1000 | bytes 1000 | tf_op jit(solution)/shard_map/lift/pallas_call | solution.py:292
  3.7 0.5 %collective-permute-start = (f32[568,128]{1,0:T(8,128)S(1)}, f32[568,128]{1,0:T(8,128)S(1)}, u32[]{:S(2)}, u32[]{:S(2)}) collective-permute-start(f32[568,128]{1,0:T(8,128)S(1)} %get-tuple-element.36), channel_id=1, source_target_pairs={{0,1},{1,0},{2,3},{3,2},{4,5},{5,4},{6,7},{7,6},{8,9},{9,8},{10,11... | collective-permute-start | bytes 872456 | tf_op jit(solution)/shard_map/ppermute | solution.py:58
  4.2 0.1 collective-permute-start.1
  4.2 1.1 %own.1 = (f32[200,128]{1,0:T(8,128)S(1)}, f32[568,128]{1,0:T(8,128)S(1)}, f32[512,256]{1,0:T(8,128)S(1)}) custom-call(f32[512,256]{1,0:T(8,128)S(1)} %get-tuple-element.30.refs_0_, bf16[512,512]{1,0:T(8,128)(2,1)S(1)} %get-tuple-element.31.refs_1_.refs_0_, bf16[512,512]{1,0:T(8,128)(2,1)S(1)} %get-tuple-element.32.refs_2_.refs_1_, ...), custom_call_target="tpu_custom_call" | custom-call | flops 1000 | bytes 1000 | tf_op jit(solution)/shard_map/own/pallas_call | solution.py:292
  5.3 0.2 collective-permute-done.1
  5.5 2.9 %collective-permute-start.2 = (f32[200,128]{1,0:T(8,128)S(1)}, f32[200,128]{1,0:T(8,128)S(1)}, u32[]{:S(2)}, u32[]{:S(2)}) collective-permute-start(f32[200,128]{1,0:T(8,128)S(1)} %add.52.refs_6_), channel_id=1, source_target_pairs={{0,2},{1,3},{2,0},{3,1},{4,6},{5,7},{6,4},{7,5},{8,10},{9,11},{10,... | collective-permute-start | bytes 307208 | tf_op jit(solution)/shard_map/ppermute | solution.py:58
  8.5 0.1 collective-permute-start.3
  8.6 1.8 %turn.1 = (f32[512,256]{1,0:T(8,128)S(1)}, f32[512,256]{1,0:T(8,128)S(1)}, bf16[512,384]{1,0:T(8,128)(2,1)S(1)}, bf16[512,384]{1,0:T(8,128)(2,1)S(1)}, f32[8,128]{1,0:T(8,128)S(1)}) custom-call(bf16[512,512]{1,0:T(8,128)(2,1)S(1)} %get-tuple-element.31.refs_1_.refs_0_, bf16[512,512]{1,0:T(8,128)(2,1)S(1)} %get-tuple-element.32.refs_2_.refs_1_, ...), custom_call_target="tpu_custom_call" | custom-call | flops 1000 | bytes 1000 | tf_op jit(solution)/shard_map/turn/pallas_call | solution.py:292
  10.5 1.7 %collective-permute-done.2 = f32[200,128]{1,0:T(8,128)S(1)} collective-permute-done((f32[200,128]{1,0:T(8,128)S(1)}, f32[200,128]{1,0:T(8,128)S(1)}, u32[]{:S(2)}, u32[]{:S(2)}) %collective-permute-start.2) | collective-permute-done | bytes 102432 | tf_op jit(solution)/shard_map/ppermute | solution.py:58
  12.1 2.2 %collective-permute-start.4 = (f32[200,128]{1,0:T(8,128)S(1)}, f32[200,128]{1,0:T(8,128)S(1)}, u32[]{:S(2)}, u32[]{:S(2)}) collective-permute-start(f32[200,128]{1,0:T(8,128)S(1)} %fusion.refs_0_), channel_id=1, source_target_pairs={{0,4},{1,5},{2,6},{3,7},{4,0},{5,1},{6,2},{7,3},{8,12},{9,13},{10,... | collective-permute-start | bytes 307208 | tf_op jit(solution)/shard_map/ppermute | solution.py:58
  14.3 1.2 %collective-permute-start.5 = (f32[184,128]{1,0:T(8,128)S(1)}, f32[184,128]{1,0:T(8,128)S(1)}, u32[]{:S(2)}, u32[]{:S(2)}) collective-permute-start(f32[184,128]{1,0:T(8,128)S(1)} %fusion.1.refs_2_.refs_1_), channel_id=1, source_target_pairs={{0,4},{1,5},{2,6},{3,7},{4,0},{5,1},{6,2},{7,3},{8,12},{9,13},{10,... | collective-permute-start | bytes 282632 | tf_op jit(solution)/shard_map/ppermute | solution.py:58
  15.5 0.6 %ready.1 = (bf16[7,384,128]{2,1,0:T(8,128)(2,1)S(1)}, bf16[7,384,128]{2,1,0:T(8,128)(2,1)S(1)}, bf16[7,128,384]{2,1,0:T(8,128)(2,1)S(1)}, bf16[7,128,384]{2,1,0:T(8,128)(2,1)S(1)}) custom-call(f32[7,128,128]{2,1,0:T(8,128)S(1)} %copy-done.1, f32[10,128,128]{2,1,0:T(8,128)S(1)} %copy-done, f32[184,128]{1,0:T(8,128)S(1)} %fusion.1.refs_2_.refs_1_), custom_call_target="tpu_custom_call" | custom-call | flops 1000 | bytes 1000 | tf_op jit(solution)/shard_map/ready/pallas_call | solution.py:292
  16.1 1.8 %collective-permute-done.4.refs_2_ = f32[200,128]{1,0:T(8,128)S(1)} collective-permute-done((f32[200,128]{1,0:T(8,128)S(1)}, f32[200,128]{1,0:T(8,128)S(1)}, u32[]{:S(2)}, u32[]{:S(2)}) %collective-permute-start.4) | collective-permute-done | bytes 102432 | tf_op jit(solution)/shard_map/ppermute | solution.py:58
  17.9 1.0 %collective-permute-done.5.refs_3_ = f32[184,128]{1,0:T(8,128)S(1)} collective-permute-done((f32[184,128]{1,0:T(8,128)S(1)}, f32[184,128]{1,0:T(8,128)S(1)}, u32[]{:S(2)}, u32[]{:S(2)}) %collective-permute-start.5) | collective-permute-done | bytes 94240 | tf_op jit(solution)/shard_map/ppermute | solution.py:58
  19.0 0.2 climb.2
  19.2 1.7 %collective-permute-start.6 = (f32[256,128]{1,0:T(8,128)S(1)}, f32[256,128]{1,0:T(8,128)S(1)}, u32[]{:S(2)}, u32[]{:S(2)}) collective-permute-start(f32[256,128]{1,0:T(8,128)S(1)} %get-tuple-element.44.refs_0_), channel_id=1, source_target_pairs={{0,8},{1,9},{2,10},{3,11},{4,12},{5,13},{6,14},{7,15},{8,0},{9,1},... | collective-permute-start | bytes 393224 | tf_op jit(solution)/shard_map/ppermute | solution.py:58
  20.9 0.4 collective-permute-start.8
  21.3 3.2 %collective-permute-done.6.refs_1_ = f32[256,128]{1,0:T(8,128)S(1)} collective-permute-done((f32[256,128]{1,0:T(8,128)S(1)}, f32[256,128]{1,0:T(8,128)S(1)}, u32[]{:S(2)}, u32[]{:S(2)}) %collective-permute-start.6) | collective-permute-done | bytes 131104 | tf_op jit(solution)/shard_map/ppermute | solution.py:58
  24.4 0.2 climb.3
  24.7 2.5 %collective-permute-start.7 = (f32[128,128]{1,0:T(8,128)S(1)}, f32[128,128]{1,0:T(8,128)S(1)}, u32[]{:S(2)}, u32[]{:S(2)}) collective-permute-start(f32[128,128]{1,0:T(8,128)S(1)} %get-tuple-element.45.refs_0_.refs_3_), channel_id=1, source_target_pairs={{0,16},{1,17},{2,18},{3,19},{4,20},{5,21},{6,22},{7,23},{8,24},{9,... | collective-permute-start | bytes 196616 | tf_op jit(solution)/shard_map/ppermute | solution.py:58
  27.2 1.3 %collective-permute-start.11 = (f32[3,64,128]{2,1,0:T(8,128)S(1)}, f32[3,64,128]{2,1,0:T(8,128)S(1)}, u32[]{:S(2)}, u32[]{:S(2)}) collective-permute-start(f32[3,64,128]{2,1,0:T(8,128)S(1)} %halve.1), channel_id=1, source_target_pairs={{0,16},{1,17},{2,18},{3,19},{4,20},{5,21},{6,22},{7,23},{8,24},{9,... | collective-permute-start | bytes 294920 | tf_op jit(solution)/shard_map/ppermute | solution.py:58
  28.4 3.0 %collective-permute-done.7.refs_1_ = f32[128,128]{1,0:T(8,128)S(1)} collective-permute-done((f32[128,128]{1,0:T(8,128)S(1)}, f32[128,128]{1,0:T(8,128)S(1)}, u32[]{:S(2)}, u32[]{:S(2)}) %collective-permute-start.7) | collective-permute-done | bytes 65568 | tf_op jit(solution)/shard_map/ppermute | solution.py:58
  31.5 0.8 %descend.1.refs_0_ = f32[384,128]{1,0:T(8,128)S(1)} custom-call(f32[128,128]{1,0:T(8,128)S(1)} %get-tuple-element.45.refs_0_.refs_3_, f32[128,128]{1,0:T(8,128)S(1)} %collective-permute-done.7.refs_1_, bf16[7,384,128]{2,1,0:T(8,128)(2,1)S(1)} %get-tuple-element.42.refs_4_.refs_2_, bf16[7,384,128]{2,1,0:T(8,128)(2,1)S(1)} %get-tuple-element.43.refs_5_.refs_3_, ...), custom_call_target="tpu_custom_call" | custom-call | flops 1000 | bytes 1000 | tf_op jit(solution)/shard_map/descend/pallas_call | solution.py:292
  32.2 1.6 %collective-permute-start.9 = (f32[384,128]{1,0:T(8,128)S(1)}, f32[384,128]{1,0:T(8,128)S(1)}, u32[]{:S(2)}, u32[]{:S(2)}) collective-permute-start(f32[384,128]{1,0:T(8,128)S(1)} %descend.1.refs_0_), channel_id=1, source_target_pairs={{0,2},{1,3},{2,0},{3,1},{4,6},{5,7},{6,4},{7,5},{8,10},{9,11},{10,... | collective-permute-start | bytes 589832 | tf_op jit(solution)/shard_map/ppermute | solution.py:58
  33.8 0.5 %settle.2 = (f32[512,128]{1,0:T(8,128)S(1)}, f32[8,128]{1,0:T(8,128)S(1)}) custom-call(f32[384,128]{1,0:T(8,128)S(1)} %descend.1.refs_0_, f32[512,256]{1,0:T(8,128)S(1)} %get-tuple-element.50.refs_1_, bf16[512,384]{1,0:T(8,128)(2,1)S(1)} %get-tuple-element.51.refs_2_, bf16[512,384]{1,0:T(8,128)(2,1)S(1)} %get-tuple-element.52.refs_3_), custom_call_target="tpu_custom_call" | custom-call | flops 1000 | bytes 1000 | tf_op jit(solution)/shard_map/settle/pallas_call | solution.py:292
  34.3 1.6 %collective-permute-start.12 = (f32[3,64,128]{2,1,0:T(8,128)S(1)}, f32[3,64,128]{2,1,0:T(8,128)S(1)}, u32[]{:S(2)}, u32[]{:S(2)}) collective-permute-start(f32[3,64,128]{2,1,0:T(8,128)S(1)} %broadcast_add_fusion), channel_id=1, source_target_pairs={{0,4},{1,5},{2,6},{3,7},{4,0},{5,1},{6,2},{7,3},{8,12},{9,13},{10,... | collective-permute-start | bytes 294920 | tf_op jit(solution)/shard_map/ppermute | solution.py:58
  35.9 2.1 %collective-permute-done.9.refs_0_ = f32[384,128]{1,0:T(8,128)S(1)} collective-permute-done((f32[384,128]{1,0:T(8,128)S(1)}, f32[384,128]{1,0:T(8,128)S(1)}, u32[]{:S(2)}, u32[]{:S(2)}) %collective-permute-start.9) | collective-permute-done | bytes 196640 | tf_op jit(solution)/shard_map/ppermute | solution.py:58
  38.1 0.5 %settle.3 = (f32[512,128]{1,0:T(8,128)S(1)}, f32[8,128]{1,0:T(8,128)S(1)}) custom-call(f32[384,128]{1,0:T(8,128)S(1)} %collective-permute-done.9.refs_0_, f32[512,256]{1,0:T(8,128)S(1)} %get-tuple-element.50.refs_1_, bf16[512,384]{1,0:T(8,128)(2,1)S(1)} %get-tuple-element.51.refs_2_, bf16[512,384]{1,0:T(8,128)(2,1)S(1)} %get-tuple-element.52.refs_3_), custom_call_target="tpu_custom_call" | custom-call | flops 1000 | bytes 1000 | tf_op jit(solution)/shard_map/settle/pallas_call | solution.py:292
  38.6 0.4 %collective-permute-done.12.refs_5_ = f32[3,64,128]{2,1,0:T(8,128)S(1)} collective-permute-done((f32[3,64,128]{2,1,0:T(8,128)S(1)}, f32[3,64,128]{2,1,0:T(8,128)S(1)}, u32[]{:S(2)}, u32[]{:S(2)}) %collective-permute-start.12) | collective-permute-done | bytes 98336 | tf_op jit(solution)/shard_map/ppermute | solution.py:58
  39.0 0.5 %top.1.refs_6_ = f32[896,128]{1,0:T(8,128)S(1)} custom-call(f32[384,128]{1,0:T(8,128)S(1)} %descend.1.refs_0_, bf16[7,128,384]{2,1,0:T(8,128)(2,1)S(1)} %get-tuple-element.46.refs_4_.refs_1_, bf16[7,128,384]{2,1,0:T(8,128)(2,1)S(1)} %get-tuple-element.47.refs_5_.refs_2_, f32[1,128,128]{2,1,0:T(8,128)S(1)} %collective-permute-done.8.refs_8_.refs_1_.refs_3_, ...), custom_call_target="tpu_custom_call" | custom-call | flops 5000000000 | bytes 1000 | tf_op jit(solution)/shard_map/top/pallas_call | solution.py:292
  39.5 0.3 collective-permute-done.10.refs_0_
  39.8 1.4 %last.1 = (f32[512,512]{1,0:T(8,128)}, f32[896,128]{1,0:T(8,128)}) custom-call(f32[2,384,128]{2,1,0:T(8,128)S(1)} %collective-permute-done.10.refs_0_, f32[512,256]{1,0:T(8,128)S(1)} %get-tuple-element.54.refs_1_, bf16[512,384]{1,0:T(8,128)(2,1)S(1)} %get-tuple-element.51.refs_2_, bf16[512,384]{1,0:T(8,128)(2,1)S(1)} %get-tuple-element.52.refs_3_, ...), custom_call_target="tpu_custom_call" | custom-call | flops 1000 | bytes 1000 | tf_op jit(solution)/shard_map/last/pallas_call | solution.py:292
  (22 shorter events, 0.3 us)
Async XLA Ops:
  0.6 3.6 %copy-start.2 = (f32[896,128]{1,0:T(8,128)S(1)}, f32[896,128]{1,0:T(8,128)}, u32[]{:S(2)}) copy-start(f32[896,128]{1,0:T(8,128)} %refs_5_.1) | copy-start | bytes 1376260
  3.6 11.9 %copy-start = (f32[10,128,128]{2,1,0:T(8,128)S(1)}, f32[10,128,128]{2,1,0:T(8,128)}, u32[]{:S(2)}) copy-start(f32[10,128,128]{2,1,0:T(8,128)} %refs_1_.3) | copy-start | bytes 1966084
  3.6 11.9 %copy-start.1 = (f32[7,128,128]{2,1,0:T(8,128)S(1)}, f32[7,128,128]{2,1,0:T(8,128)}, u32[]{:S(2)}) copy-start(f32[7,128,128]{2,1,0:T(8,128)} %refs_0_.3) | copy-start | bytes 1376260
  3.7 4.8 %collective-permute-start = (f32[568,128]{1,0:T(8,128)S(1)}, f32[568,128]{1,0:T(8,128)S(1)}, u32[]{:S(2)}, u32[]{:S(2)}) collective-permute-start(f32[568,128]{1,0:T(8,128)S(1)} %get-tuple-element.36), channel_id=1, source_target_pairs={{0,1},{1,0},{2,3},{3,2},{4,5},{5,4},{6,7},{7,6},{8,9},{9,8},{10,11... | collective-permute-start | bytes 872456 | tf_op jit(solution)/shard_map/ppermute | solution.py:58
  4.2 1.3 %collective-permute-start.1 = (f32[200,128]{1,0:T(8,128)S(1)}, f32[200,128]{1,0:T(8,128)S(1)}, u32[]{:S(2)}, u32[]{:S(2)}) collective-permute-start(f32[200,128]{1,0:T(8,128)S(1)} %get-tuple-element.38), channel_id=1, source_target_pairs={{0,1},{1,0},{2,3},{3,2},{4,5},{5,4},{6,7},{7,6},{8,9},{9,8},{10,11... | collective-permute-start | bytes 307208 | tf_op jit(solution)/shard_map/ppermute | solution.py:58
  5.5 6.6 %collective-permute-start.2 = (f32[200,128]{1,0:T(8,128)S(1)}, f32[200,128]{1,0:T(8,128)S(1)}, u32[]{:S(2)}, u32[]{:S(2)}) collective-permute-start(f32[200,128]{1,0:T(8,128)S(1)} %add.52.refs_6_), channel_id=1, source_target_pairs={{0,2},{1,3},{2,0},{3,1},{4,6},{5,7},{6,4},{7,5},{8,10},{9,11},{10,... | collective-permute-start | bytes 307208 | tf_op jit(solution)/shard_map/ppermute | solution.py:58
  8.5 5.8 %collective-permute-start.3 = (f32[184,128]{1,0:T(8,128)S(1)}, f32[184,128]{1,0:T(8,128)S(1)}, u32[]{:S(2)}, u32[]{:S(2)}) collective-permute-start(f32[184,128]{1,0:T(8,128)S(1)} %slice_add_fusion.3.refs_7_), channel_id=1, source_target_pairs={{0,2},{1,3},{2,0},{3,1},{4,6},{5,7},{6,4},{7,5},{8,10},{9,11},{10,... | collective-permute-start | bytes 282632 | tf_op jit(solution)/shard_map/ppermute | solution.py:58
  12.1 5.8 %collective-permute-start.4 = (f32[200,128]{1,0:T(8,128)S(1)}, f32[200,128]{1,0:T(8,128)S(1)}, u32[]{:S(2)}, u32[]{:S(2)}) collective-permute-start(f32[200,128]{1,0:T(8,128)S(1)} %fusion.refs_0_), channel_id=1, source_target_pairs={{0,4},{1,5},{2,6},{3,7},{4,0},{5,1},{6,2},{7,3},{8,12},{9,13},{10,... | collective-permute-start | bytes 307208 | tf_op jit(solution)/shard_map/ppermute | solution.py:58
  14.3 4.6 %collective-permute-start.5 = (f32[184,128]{1,0:T(8,128)S(1)}, f32[184,128]{1,0:T(8,128)S(1)}, u32[]{:S(2)}, u32[]{:S(2)}) collective-permute-start(f32[184,128]{1,0:T(8,128)S(1)} %fusion.1.refs_2_.refs_1_), channel_id=1, source_target_pairs={{0,4},{1,5},{2,6},{3,7},{4,0},{5,1},{6,2},{7,3},{8,12},{9,13},{10,... | collective-permute-start | bytes 282632 | tf_op jit(solution)/shard_map/ppermute | solution.py:58
  19.2 5.2 %collective-permute-start.6 = (f32[256,128]{1,0:T(8,128)S(1)}, f32[256,128]{1,0:T(8,128)S(1)}, u32[]{:S(2)}, u32[]{:S(2)}) collective-permute-start(f32[256,128]{1,0:T(8,128)S(1)} %get-tuple-element.44.refs_0_), channel_id=1, source_target_pairs={{0,8},{1,9},{2,10},{3,11},{4,12},{5,13},{6,14},{7,15},{8,0},{9,1},... | collective-permute-start | bytes 393224 | tf_op jit(solution)/shard_map/ppermute | solution.py:58
  20.9 6.3 %collective-permute-start.8 = (f32[1,128,128]{2,1,0:T(8,128)S(1)}, f32[1,128,128]{2,1,0:T(8,128)S(1)}, u32[]{:S(2)}, u32[]{:S(2)}) collective-permute-start(f32[1,128,128]{2,1,0:T(8,128)S(1)} %bitcast.10), channel_id=1, source_target_pairs={{0,8},{1,9},{2,10},{3,11},{4,12},{5,13},{6,14},{7,15},{8,0},{9,1},... | collective-permute-start | bytes 196616 | tf_op jit(solution)/shard_map/ppermute | solution.py:58
  24.7 6.8 %collective-permute-start.7 = (f32[128,128]{1,0:T(8,128)S(1)}, f32[128,128]{1,0:T(8,128)S(1)}, u32[]{:S(2)}, u32[]{:S(2)}) collective-permute-start(f32[128,128]{1,0:T(8,128)S(1)} %get-tuple-element.45.refs_0_.refs_3_), channel_id=1, source_target_pairs={{0,16},{1,17},{2,18},{3,19},{4,20},{5,21},{6,22},{7,23},{8,24},{9,... | collective-permute-start | bytes 196616 | tf_op jit(solution)/shard_map/ppermute | solution.py:58
  27.2 7.1 %collective-permute-start.11 = (f32[3,64,128]{2,1,0:T(8,128)S(1)}, f32[3,64,128]{2,1,0:T(8,128)S(1)}, u32[]{:S(2)}, u32[]{:S(2)}) collective-permute-start(f32[3,64,128]{2,1,0:T(8,128)S(1)} %halve.1), channel_id=1, source_target_pairs={{0,16},{1,17},{2,18},{3,19},{4,20},{5,21},{6,22},{7,23},{8,24},{9,... | collective-permute-start | bytes 294920 | tf_op jit(solution)/shard_map/ppermute | solution.py:58
  32.2 5.7 %collective-permute-start.9 = (f32[384,128]{1,0:T(8,128)S(1)}, f32[384,128]{1,0:T(8,128)S(1)}, u32[]{:S(2)}, u32[]{:S(2)}) collective-permute-start(f32[384,128]{1,0:T(8,128)S(1)} %descend.1.refs_0_), channel_id=1, source_target_pairs={{0,2},{1,3},{2,0},{3,1},{4,6},{5,7},{6,4},{7,5},{8,10},{9,11},{10,... | collective-permute-start | bytes 589832 | tf_op jit(solution)/shard_map/ppermute | solution.py:58
  34.3 4.7 %collective-permute-start.12 = (f32[3,64,128]{2,1,0:T(8,128)S(1)}, f32[3,64,128]{2,1,0:T(8,128)S(1)}, u32[]{:S(2)}, u32[]{:S(2)}) collective-permute-start(f32[3,64,128]{2,1,0:T(8,128)S(1)} %broadcast_add_fusion), channel_id=1, source_target_pairs={{0,4},{1,5},{2,6},{3,7},{4,0},{5,1},{6,2},{7,3},{8,12},{9,13},{10,... | collective-permute-start | bytes 294920 | tf_op jit(solution)/shard_map/ppermute | solution.py:58
  38.0 1.8 %collective-permute-start.10 = (f32[2,384,128]{2,1,0:T(8,128)S(1)}, f32[2,384,128]{2,1,0:T(8,128)S(1)}, u32[]{:S(2)}, u32[]{:S(2)}) collective-permute-start(f32[2,384,128]{2,1,0:T(8,128)S(1)} %pad_maximum_fusion), channel_id=1, source_target_pairs={{0,1},{1,0},{2,3},{3,2},{4,5},{5,4},{6,7},{7,6},{8,9},{9,8},{10,11... | collective-permute-start | bytes 1179656 | tf_op jit(solution)/shard_map/ppermute | solution.py:58

commit v7 on v6

--- a/solution.py
+++ b/solution.py
@@ -215,25 +215,24 @@
     token[...] = jnp.zeros_like(token)
 
 
-def last_kernel(plan, width, part, base, gain_hi, gain_lo, own, far, top, out, out_top, buffer, sems):
+def last_kernel(plan, width, part, base, gain_hi, gain_lo, far, own, cross, top, out, out_top, buffer, sems):
     _, _, core, half = plan.here()
-    groups = ((1 - half) * 2 + core, half * 2 + core, (1 - half) * 2 + 1 - core, half * 2 + 1 - core)
+    groups = ((1 - half) * 2 + core, half * 2 + core, half * 2 + 1 - core, (1 - half) * 2 + 1 - core)
     copies = [pltpu.make_async_copy(top, out_top, sems.at[0])]
-    for done, group in zip((far, own), groups):
+    for done, group in zip((far, own, cross), groups):
         copies.append(pltpu.make_async_copy(done, out.at[:, lanes(group, width)], sems.at[len(copies)]))
     for copy in copies:
         copy.start()
-    known = split(jnp.concatenate([part[0], part[1]], 1))
+    known = split(part[...])
     step = buffer.shape[0] // 2
     for start in range(0, buffer.shape[0], step):
         rows = slice(start, start + step)
         change = dot(gain_hi[rows], known[0]) + (dot(gain_hi[rows], known[1]) + dot(gain_lo[rows], known[0]))
-        buffer[rows] = base[rows] - change
-        for number, group in enumerate(groups[2:]):
-            copies.append(pltpu.make_async_copy(
-                buffer.at[pl.ds(start, step), pl.ds(number * width, width)],
-                out.at[pl.ds(start, step), lanes(group, width)], sems.at[len(copies)]))
-            copies[-1].start()
+        buffer[rows] = base[rows, :width] - change
+        copies.append(pltpu.make_async_copy(
+            buffer.at[pl.ds(start, step)], out.at[pl.ds(start, step), lanes(groups[3], width)],
+            sems.at[len(copies)]))
+        copies[-1].start()
     for copy in copies:
         copy.wait()
 
@@ -315,7 +314,7 @@
     assert plan.group_count == 4 and block_count == 4 and plan.sharers >= 2
 
     halves = [pltpu.VMEM((order, 2 * columns), BF16)] * 2
-    cut = path // 2 + 8
+    cut = path // 2 + 32
     pieces = [inside((cut, columns)), inside((2 * path - cut, columns))]
     sent_first, sent_second, rhs_own, lifted_other, inv_hi, inv_lo, perm_hi, perm_lo = call(
         functools.partial(lift_kernel, plan, order, columns),
@@ -384,9 +383,11 @@
             [part, base, gain_hi, gain_lo], name="settle")
 
     own, token = settle(solved, base_own, columns)
+    cross = plan.swap_rhs(solved + token[:1], 1)
     stacks.append(plan.swap_leaf(stacks[-1] + token[:1], 1))
-    pair = jnp.stack([far + token[:1], solved])
-    last = plan.swap_rhs(pair, 1)
+    cross, token = settle(cross, base_other, columns)
+    far = far + token[:1]
+    last = plan.swap_rhs(far, 1)
     far, token = settle(far, base_own, 0)
     top = call(
         functools.partial(top_kernel, plan),
@@ -396,8 +397,8 @@
         functools.partial(last_kernel, plan, columns),
         [(pltpu.HBM((order, plan.group_count * columns), F32), HBM_SPEC),
          (pltpu.HBM((panel_count * width, columns), F32), HBM_SPEC)],
-        [last, base_other, gain_hi, gain_lo, own, far, top],
-        scratch=[pltpu.VMEM((order, 2 * columns), F32), pltpu.SemaphoreType.DMA((7,))], name="last")
+        [last, base_other, gain_hi, gain_lo, far, own, cross, top],
+        scratch=[pltpu.VMEM((order, columns), F32), pltpu.SemaphoreType.DMA((6,))], name="last")
     return out, top
 
 

time: 41.4 us -> 41 us (level)
  starting transfers between devices: 16 us -> 15.5 us
    ppermute x13 -> x14, starting transfers between devices: 16 us -> 15.5 us  [swap(): return lax.ppermute(value, ('leaf', 'rhs'), pairs)]
    pallas_call x12 -> x13, Pallas kernels: 10.5 us -> 10.9 us  [call(): pl.pallas_call(body, out_shape=[shape for shape, _ in outs], in_specs=spe...]
    ppermute x13 -> x14, waiting for transfers between devices: 13.7 us -> 13.5 us  [swap(): return lax.ppermute(value, ('leaf', 'rhs'), pairs)]
  transfers between devices with their start and end apart: 13 -> 14, of which waited for: 9 -> 9; matrix products, arithmetic and copies ran while one was open for 0% -> 0% of each run, Pallas kernels for 14% -> 16%
where the time goes in v7:
time: 41 us; the launch traced here: 40.8 us
  starting transfers between devices  15.5 us (38%)
  waiting for transfers between devices  13.5 us (33%)
  Pallas kernels  10.9 us (27%)
  between operations  0.84 us (2%)
    ppermute x14, starting transfers between devices, swap(): return lax.ppermute(value, ('leaf', 'rhs'), pairs)  15.5 us
    ppermute x14, waiting for transfers between devices, swap(): return lax.ppermute(value, ('leaf', 'rhs'), pairs)  13.5 us
    pallas_call x13, Pallas kernels, call(): pl.pallas_call(body, out_shape=[shape for shape, _ in outs], in_specs=spe...  10.9 us
  transfers between devices with their start and end apart: 14, of which 9 were waited for; matrix products, arithmetic and copies ran while one was open for 0% of the time, Pallas kernels for 16%

profile of v7, /device:TPU:0, one launch (start us, length us, event | category | flops | bytes accessed | tf_op | source)
XLA Modules:
  0.0 40.8 jit_solution(1821133997150959339)
XLA Ops:
  0.6 3.0 %lift.1 = (f32[224,128]{1,0:T(8,128)S(1)}, f32[544,128]{1,0:T(8,128)S(1)}, f32[512,256]{1,0:T(8,128)S(1)}, f32[512,256]{1,0:T(8,128)S(1)}, bf16[512,512]{1,0:T(8...) custom-call(f32[512,512]{1,0:T(8,128)} %refs_0_.2, ...), custom_call_target="tpu_custom_call" | custom-call | flops 1000 | bytes 1000 | tf_op jit(solution)/shard_map/lift/pallas_call | solution.py:291
  3.7 0.5 %collective-permute-start = (f32[544,128]{1,0:T(8,128)S(1)}, f32[544,128]{1,0:T(8,128)S(1)}, u32[]{:S(2)}, u32[]{:S(2)}) collective-permute-start(f32[544,128]{1,0:T(8,128)S(1)} %get-tuple-element.38), channel_id=1, source_target_pairs={{0,1},{1,0},{2,3},{3,2},{4,5},{5,4},{6,7},{7,6},{8,9},{9,8},{10,11... | collective-permute-start | bytes 835592 | tf_op jit(solution)/shard_map/ppermute | solution.py:58
  4.2 1.1 %own.1 = (f32[224,128]{1,0:T(8,128)S(1)}, f32[544,128]{1,0:T(8,128)S(1)}, f32[512,256]{1,0:T(8,128)S(1)}) custom-call(f32[512,256]{1,0:T(8,128)S(1)} %get-tuple-element.32.refs_0_, bf16[512,512]{1,0:T(8,128)(2,1)S(1)} %get-tuple-element.33.refs_1_.refs_0_, bf16[512,512]{1,0:T(8,128)(2,1)S(1)} %get-tuple-element.34.refs_2_.refs_1_, ...), custom_call_target="tpu_custom_call" | custom-call | flops 1000 | bytes 1000 | tf_op jit(solution)/shard_map/own/pallas_call | solution.py:291
  5.3 0.2 collective-permute-done.1
  5.5 2.9 %collective-permute-start.2 = (f32[224,128]{1,0:T(8,128)S(1)}, f32[224,128]{1,0:T(8,128)S(1)}, u32[]{:S(2)}, u32[]{:S(2)}) collective-permute-start(f32[224,128]{1,0:T(8,128)S(1)} %add.62.refs_6_), channel_id=1, source_target_pairs={{0,2},{1,3},{2,0},{3,1},{4,6},{5,7},{6,4},{7,5},{8,10},{9,11},{10,... | collective-permute-start | bytes 344072 | tf_op jit(solution)/shard_map/ppermute | solution.py:58
  8.5 0.1 collective-permute-start.3
  8.6 1.8 %turn.1 = (f32[512,256]{1,0:T(8,128)S(1)}, f32[512,256]{1,0:T(8,128)S(1)}, bf16[512,384]{1,0:T(8,128)(2,1)S(1)}, bf16[512,384]{1,0:T(8,128)(2,1)S(1)}, f32[8,128]{1,0:T(8,128)S(1)}) custom-call(bf16[512,512]{1,0:T(8,128)(2,1)S(1)} %get-tuple-element.33.refs_1_.refs_0_, bf16[512,512]{1,0:T(8,128)(2,1)S(1)} %get-tuple-element.34.refs_2_.refs_1_, ...), custom_call_target="tpu_custom_call" | custom-call | flops 1000 | bytes 1000 | tf_op jit(solution)/shard_map/turn/pallas_call | solution.py:291
  10.4 1.9 %collective-permute-done.2 = f32[224,128]{1,0:T(8,128)S(1)} collective-permute-done((f32[224,128]{1,0:T(8,128)S(1)}, f32[224,128]{1,0:T(8,128)S(1)}, u32[]{:S(2)}, u32[]{:S(2)}) %collective-permute-start.2) | collective-permute-done | bytes 114720 | tf_op jit(solution)/shard_map/ppermute | solution.py:58
  12.4 2.2 %collective-permute-start.4 = (f32[224,128]{1,0:T(8,128)S(1)}, f32[224,128]{1,0:T(8,128)S(1)}, u32[]{:S(2)}, u32[]{:S(2)}) collective-permute-start(f32[224,128]{1,0:T(8,128)S(1)} %fusion.refs_0_), channel_id=1, source_target_pairs={{0,4},{1,5},{2,6},{3,7},{4,0},{5,1},{6,2},{7,3},{8,12},{9,13},{10,... | collective-permute-start | bytes 344072 | tf_op jit(solution)/shard_map/ppermute | solution.py:58
  14.6 0.9 %collective-permute-start.5 = (f32[160,128]{1,0:T(8,128)S(1)}, f32[160,128]{1,0:T(8,128)S(1)}, u32[]{:S(2)}, u32[]{:S(2)}) collective-permute-start(f32[160,128]{1,0:T(8,128)S(1)} %fusion.1.refs_2_.refs_1_), channel_id=1, source_target_pairs={{0,4},{1,5},{2,6},{3,7},{4,0},{5,1},{6,2},{7,3},{8,12},{9,13},{10,... | collective-permute-start | bytes 245768 | tf_op jit(solution)/shard_map/ppermute | solution.py:58
  15.5 0.6 %ready.1 = (bf16[7,384,128]{2,1,0:T(8,128)(2,1)S(1)}, bf16[7,384,128]{2,1,0:T(8,128)(2,1)S(1)}, bf16[7,128,384]{2,1,0:T(8,128)(2,1)S(1)}, bf16[7,128,384]{2,1,0:T(8,128)(2,1)S(1)}) custom-call(f32[7,128,128]{2,1,0:T(8,128)S(1)} %copy-done.1, f32[10,128,128]{2,1,0:T(8,128)S(1)} %copy-done, f32[160,128]{1,0:T(8,128)S(1)} %fusion.1.refs_2_.refs_1_), custom_call_target="tpu_custom_call" | custom-call | flops 1000 | bytes 1000 | tf_op jit(solution)/shard_map/ready/pallas_call | solution.py:291
  16.1 2.0 %collective-permute-done.4.refs_2_ = f32[224,128]{1,0:T(8,128)S(1)} collective-permute-done((f32[224,128]{1,0:T(8,128)S(1)}, f32[224,128]{1,0:T(8,128)S(1)}, u32[]{:S(2)}, u32[]{:S(2)}) %collective-permute-start.4) | collective-permute-done | bytes 114720 | tf_op jit(solution)/shard_map/ppermute | solution.py:58
  18.1 1.0 %collective-permute-done.5.refs_3_ = f32[160,128]{1,0:T(8,128)S(1)} collective-permute-done((f32[160,128]{1,0:T(8,128)S(1)}, f32[160,128]{1,0:T(8,128)S(1)}, u32[]{:S(2)}, u32[]{:S(2)}) %collective-permute-start.5) | collective-permute-done | bytes 81952 | tf_op jit(solution)/shard_map/ppermute | solution.py:58
  19.1 0.2 climb.2
  19.3 1.6 %collective-permute-start.6 = (f32[256,128]{1,0:T(8,128)S(1)}, f32[256,128]{1,0:T(8,128)S(1)}, u32[]{:S(2)}, u32[]{:S(2)}) collective-permute-start(f32[256,128]{1,0:T(8,128)S(1)} %get-tuple-element.46.refs_0_), channel_id=1, source_target_pairs={{0,8},{1,9},{2,10},{3,11},{4,12},{5,13},{6,14},{7,15},{8,0},{9,1},... | collective-permute-start | bytes 393224 | tf_op jit(solution)/shard_map/ppermute | solution.py:58
  21.0 0.5 %collective-permute-start.8 = (f32[1,128,128]{2,1,0:T(8,128)S(1)}, f32[1,128,128]{2,1,0:T(8,128)S(1)}, u32[]{:S(2)}, u32[]{:S(2)}) collective-permute-start(f32[1,128,128]{2,1,0:T(8,128)S(1)} %bitcast.8), channel_id=1, source_target_pairs={{0,8},{1,9},{2,10},{3,11},{4,12},{5,13},{6,14},{7,15},{8,0},{9,1},... | collective-permute-start | bytes 196616 | tf_op jit(solution)/shard_map/ppermute | solution.py:58
  21.4 2.9 %collective-permute-done.6.refs_1_ = f32[256,128]{1,0:T(8,128)S(1)} collective-permute-done((f32[256,128]{1,0:T(8,128)S(1)}, f32[256,128]{1,0:T(8,128)S(1)}, u32[]{:S(2)}, u32[]{:S(2)}) %collective-permute-start.6) | collective-permute-done | bytes 131104 | tf_op jit(solution)/shard_map/ppermute | solution.py:58
  24.4 0.2 climb.3
  24.6 3.0 %collective-permute-start.7 = (f32[128,128]{1,0:T(8,128)S(1)}, f32[128,128]{1,0:T(8,128)S(1)}, u32[]{:S(2)}, u32[]{:S(2)}) collective-permute-start(f32[128,128]{1,0:T(8,128)S(1)} %get-tuple-element.47.refs_0_.refs_3_), channel_id=1, source_target_pairs={{0,16},{1,17},{2,18},{3,19},{4,20},{5,21},{6,22},{7,23},{8,24},{9,... | collective-permute-start | bytes 196616 | tf_op jit(solution)/shard_map/ppermute | solution.py:58
  27.6 0.8 %collective-permute-start.12 = (f32[3,64,128]{2,1,0:T(8,128)S(1)}, f32[3,64,128]{2,1,0:T(8,128)S(1)}, u32[]{:S(2)}, u32[]{:S(2)}) collective-permute-start(f32[3,64,128]{2,1,0:T(8,128)S(1)} %halve.1), channel_id=1, source_target_pairs={{0,16},{1,17},{2,18},{3,19},{4,20},{5,21},{6,22},{7,23},{8,24},{9,... | collective-permute-start | bytes 294920 | tf_op jit(solution)/shard_map/ppermute | solution.py:58
  28.4 1.8 %collective-permute-done.7.refs_1_ = f32[128,128]{1,0:T(8,128)S(1)} collective-permute-done((f32[128,128]{1,0:T(8,128)S(1)}, f32[128,128]{1,0:T(8,128)S(1)}, u32[]{:S(2)}, u32[]{:S(2)}) %collective-permute-start.7) | collective-permute-done | bytes 65568 | tf_op jit(solution)/shard_map/ppermute | solution.py:58
  30.2 0.8 %descend.1.refs_0_ = f32[384,128]{1,0:T(8,128)S(1)} custom-call(f32[128,128]{1,0:T(8,128)S(1)} %get-tuple-element.47.refs_0_.refs_3_, f32[128,128]{1,0:T(8,128)S(1)} %collective-permute-done.7.refs_1_, bf16[7,384,128]{2,1,0:T(8,128)(2,1)S(1)} %get-tuple-element.44.refs_4_.refs_2_, bf16[7,384,128]{2,1,0:T(8,128)(2,1)S(1)} %get-tuple-element.45.refs_5_.refs_3_, ...), custom_call_target="tpu_custom_call" | custom-call | flops 1000 | bytes 1000 | tf_op jit(solution)/shard_map/descend/pallas_call | solution.py:291
  31.0 1.6 %collective-permute-start.9 = (f32[384,128]{1,0:T(8,128)S(1)}, f32[384,128]{1,0:T(8,128)S(1)}, u32[]{:S(2)}, u32[]{:S(2)}) collective-permute-start(f32[384,128]{1,0:T(8,128)S(1)} %descend.1.refs_0_), channel_id=1, source_target_pairs={{0,2},{1,3},{2,0},{3,1},{4,6},{5,7},{6,4},{7,5},{8,10},{9,11},{10,... | collective-permute-start | bytes 589832 | tf_op jit(solution)/shard_map/ppermute | solution.py:58
  32.5 0.5 %settle.3 = (f32[512,128]{1,0:T(8,128)S(1)}, f32[8,128]{1,0:T(8,128)S(1)}) custom-call(f32[384,128]{1,0:T(8,128)S(1)} %descend.1.refs_0_, f32[512,256]{1,0:T(8,128)S(1)} %get-tuple-element.52.refs_1_, bf16[512,384]{1,0:T(8,128)(2,1)S(1)} %get-tuple-element.53.refs_2_, bf16[512,384]{1,0:T(8,128)(2,1)S(1)} %get-tuple-element.54.refs_3_), custom_call_target="tpu_custom_call" | custom-call | flops 1000 | bytes 1000 | tf_op jit(solution)/shard_map/settle/pallas_call | solution.py:291
  33.1 1.1 %collective-permute-done.12.refs_4_ = f32[3,64,128]{2,1,0:T(8,128)S(1)} collective-permute-done((f32[3,64,128]{2,1,0:T(8,128)S(1)}, f32[3,64,128]{2,1,0:T(8,128)S(1)}, u32[]{:S(2)}, u32[]{:S(2)}) %collective-permute-start.12) | collective-permute-done | bytes 98336 | tf_op jit(solution)/shard_map/ppermute | solution.py:58
  34.3 1.2 %collective-permute-start.13 = (f32[3,64,128]{2,1,0:T(8,128)S(1)}, f32[3,64,128]{2,1,0:T(8,128)S(1)}, u32[]{:S(2)}, u32[]{:S(2)}) collective-permute-start(f32[3,64,128]{2,1,0:T(8,128)S(1)} %broadcast_add_fusion.2), channel_id=1, source_target_pairs={{0,4},{1,5},{2,6},{3,7},{4,0},{5,1},{6,2},{7,3},{8,12},{9,13},{10,... | collective-permute-start | bytes 294920 | tf_op jit(solution)/shard_map/ppermute | solution.py:58
  35.4 0.5 %settle.4 = (f32[512,128]{1,0:T(8,128)S(1)}, f32[8,128]{1,0:T(8,128)S(1)}) custom-call(f32[384,128]{1,0:T(8,128)S(1)} %collective-permute-done.10.refs_0_, f32[512,256]{1,0:T(8,128)S(1)} %get-tuple-element.56.refs_1_, bf16[512,384]{1,0:T(8,128)(2,1)S(1)} %get-tuple-element.53.refs_2_, bf16[512,384]{1,0:T(8,128)(2,1)S(1)} %get-tuple-element.54.refs_3_), custom_call_target="tpu_custom_call" | custom-call | flops 1000 | bytes 1000 | tf_op jit(solution)/shard_map/settle/pallas_call | solution.py:291
  35.9 0.8 %collective-permute-done.9 = f32[384,128]{1,0:T(8,128)S(1)} collective-permute-done((f32[384,128]{1,0:T(8,128)S(1)}, f32[384,128]{1,0:T(8,128)S(1)}, u32[]{:S(2)}, u32[]{:S(2)}) %collective-permute-start.9) | collective-permute-done | bytes 196640 | tf_op jit(solution)/shard_map/ppermute | solution.py:58
  36.8 0.5 %settle.5 = (f32[512,128]{1,0:T(8,128)S(1)}, f32[8,128]{1,0:T(8,128)S(1)}) custom-call(f32[384,128]{1,0:T(8,128)S(1)} %broadcast_add_fusion.refs_0_, f32[512,256]{1,0:T(8,128)S(1)} %get-tuple-element.52.refs_1_, bf16[512,384]{1,0:T(8,128)(2,1)S(1)} %get-tuple-element.53.refs_2_, bf16[512,384]{1,0:T(8,128)(2,1)S(1)} %get-tuple-element.54.refs_3_), custom_call_target="tpu_custom_call" | custom-call | flops 1000 | bytes 1000 | tf_op jit(solution)/shard_map/settle/pallas_call | solution.py:291
  37.3 1.7 %collective-permute-done.13.refs_5_ = f32[3,64,128]{2,1,0:T(8,128)S(1)} collective-permute-done((f32[3,64,128]{2,1,0:T(8,128)S(1)}, f32[3,64,128]{2,1,0:T(8,128)S(1)}, u32[]{:S(2)}, u32[]{:S(2)}) %collective-permute-start.13) | collective-permute-done | bytes 98336 | tf_op jit(solution)/shard_map/ppermute | solution.py:58
  38.9 0.5 %top.1.refs_7_ = f32[896,128]{1,0:T(8,128)S(1)} custom-call(f32[384,128]{1,0:T(8,128)S(1)} %descend.1.refs_0_, bf16[7,128,384]{2,1,0:T(8,128)(2,1)S(1)} %get-tuple-element.48.refs_4_.refs_1_, bf16[7,128,384]{2,1,0:T(8,128)(2,1)S(1)} %get-tuple-element.49.refs_5_.refs_2_, f32[1,128,128]{2,1,0:T(8,128)S(1)} %collective-permute-done.8.refs_8_.refs_1_.refs_3_, ...), custom_call_target="tpu_custom_call" | custom-call | flops 5000000000 | bytes 1000 | tf_op jit(solution)/shard_map/top/pallas_call | solution.py:291
  39.5 1.3 %last.1 = (f32[512,512]{1,0:T(8,128)}, f32[896,128]{1,0:T(8,128)}) custom-call(f32[384,128]{1,0:T(8,128)S(1)} %collective-permute-done.11.refs_0_, f32[512,256]{1,0:T(8,128)S(1)} %get-tuple-element.56.refs_1_, bf16[512,384]{1,0:T(8,128)(2,1)S(1)} %get-tuple-element.53.refs_2_, bf16[512,384]{1,0:T(8,128)(2,1)S(1)} %get-tuple-element.54.refs_3_, ...), custom_call_target="tpu_custom_call" | custom-call | flops 1000 | bytes 1000 | tf_op jit(solution)/shard_map/last/pallas_call | solution.py:291
  (26 shorter events, 0.4 us)
Async XLA Ops:
  0.6 3.6 %copy-start.2 = (f32[896,128]{1,0:T(8,128)S(1)}, f32[896,128]{1,0:T(8,128)}, u32[]{:S(2)}) copy-start(f32[896,128]{1,0:T(8,128)} %refs_5_.1) | copy-start | bytes 1376260
  3.6 11.9 %copy-start = (f32[10,128,128]{2,1,0:T(8,128)S(1)}, f32[10,128,128]{2,1,0:T(8,128)}, u32[]{:S(2)}) copy-start(f32[10,128,128]{2,1,0:T(8,128)} %refs_1_.3) | copy-start | bytes 1966084
  3.6 11.9 %copy-start.1 = (f32[7,128,128]{2,1,0:T(8,128)S(1)}, f32[7,128,128]{2,1,0:T(8,128)}, u32[]{:S(2)}) copy-start(f32[7,128,128]{2,1,0:T(8,128)} %refs_0_.3) | copy-start | bytes 1376260
  3.7 4.8 %collective-permute-start = (f32[544,128]{1,0:T(8,128)S(1)}, f32[544,128]{1,0:T(8,128)S(1)}, u32[]{:S(2)}, u32[]{:S(2)}) collective-permute-start(f32[544,128]{1,0:T(8,128)S(1)} %get-tuple-element.38), channel_id=1, source_target_pairs={{0,1},{1,0},{2,3},{3,2},{4,5},{5,4},{6,7},{7,6},{8,9},{9,8},{10,11... | collective-permute-start | bytes 835592 | tf_op jit(solution)/shard_map/ppermute | solution.py:58
  4.2 1.3 %collective-permute-start.1 = (f32[224,128]{1,0:T(8,128)S(1)}, f32[224,128]{1,0:T(8,128)S(1)}, u32[]{:S(2)}, u32[]{:S(2)}) collective-permute-start(f32[224,128]{1,0:T(8,128)S(1)} %get-tuple-element.40), channel_id=1, source_target_pairs={{0,1},{1,0},{2,3},{3,2},{4,5},{5,4},{6,7},{7,6},{8,9},{9,8},{10,11... | collective-permute-start | bytes 344072 | tf_op jit(solution)/shard_map/ppermute | solution.py:58
  5.5 6.9 %collective-permute-start.2 = (f32[224,128]{1,0:T(8,128)S(1)}, f32[224,128]{1,0:T(8,128)S(1)}, u32[]{:S(2)}, u32[]{:S(2)}) collective-permute-start(f32[224,128]{1,0:T(8,128)S(1)} %add.62.refs_6_), channel_id=1, source_target_pairs={{0,2},{1,3},{2,0},{3,1},{4,6},{5,7},{6,4},{7,5},{8,10},{9,11},{10,... | collective-permute-start | bytes 344072 | tf_op jit(solution)/shard_map/ppermute | solution.py:58
  8.5 6.1 %collective-permute-start.3 = (f32[160,128]{1,0:T(8,128)S(1)}, f32[160,128]{1,0:T(8,128)S(1)}, u32[]{:S(2)}, u32[]{:S(2)}) collective-permute-start(f32[160,128]{1,0:T(8,128)S(1)} %slice_add_fusion.3.refs_7_), channel_id=1, source_target_pairs={{0,2},{1,3},{2,0},{3,1},{4,6},{5,7},{6,4},{7,5},{8,10},{9,11},{10,... | collective-permute-start | bytes 245768 | tf_op jit(solution)/shard_map/ppermute | solution.py:58
  12.4 5.7 %collective-permute-start.4 = (f32[224,128]{1,0:T(8,128)S(1)}, f32[224,128]{1,0:T(8,128)S(1)}, u32[]{:S(2)}, u32[]{:S(2)}) collective-permute-start(f32[224,128]{1,0:T(8,128)S(1)} %fusion.refs_0_), channel_id=1, source_target_pairs={{0,4},{1,5},{2,6},{3,7},{4,0},{5,1},{6,2},{7,3},{8,12},{9,13},{10,... | collective-permute-start | bytes 344072 | tf_op jit(solution)/shard_map/ppermute | solution.py:58
  14.6 4.5 %collective-permute-start.5 = (f32[160,128]{1,0:T(8,128)S(1)}, f32[160,128]{1,0:T(8,128)S(1)}, u32[]{:S(2)}, u32[]{:S(2)}) collective-permute-start(f32[160,128]{1,0:T(8,128)S(1)} %fusion.1.refs_2_.refs_1_), channel_id=1, source_target_pairs={{0,4},{1,5},{2,6},{3,7},{4,0},{5,1},{6,2},{7,3},{8,12},{9,13},{10,... | collective-permute-start | bytes 245768 | tf_op jit(solution)/shard_map/ppermute | solution.py:58
  19.3 5.0 %collective-permute-start.6 = (f32[256,128]{1,0:T(8,128)S(1)}, f32[256,128]{1,0:T(8,128)S(1)}, u32[]{:S(2)}, u32[]{:S(2)}) collective-permute-start(f32[256,128]{1,0:T(8,128)S(1)} %get-tuple-element.46.refs_0_), channel_id=1, source_target_pairs={{0,8},{1,9},{2,10},{3,11},{4,12},{5,13},{6,14},{7,15},{8,0},{9,1},... | collective-permute-start | bytes 393224 | tf_op jit(solution)/shard_map/ppermute | solution.py:58
  21.0 6.6 %collective-permute-start.8 = (f32[1,128,128]{2,1,0:T(8,128)S(1)}, f32[1,128,128]{2,1,0:T(8,128)S(1)}, u32[]{:S(2)}, u32[]{:S(2)}) collective-permute-start(f32[1,128,128]{2,1,0:T(8,128)S(1)} %bitcast.8), channel_id=1, source_target_pairs={{0,8},{1,9},{2,10},{3,11},{4,12},{5,13},{6,14},{7,15},{8,0},{9,1},... | collective-permute-start | bytes 196616 | tf_op jit(solution)/shard_map/ppermute | solution.py:58
  24.6 5.6 %collective-permute-start.7 = (f32[128,128]{1,0:T(8,128)S(1)}, f32[128,128]{1,0:T(8,128)S(1)}, u32[]{:S(2)}, u32[]{:S(2)}) collective-permute-start(f32[128,128]{1,0:T(8,128)S(1)} %get-tuple-element.47.refs_0_.refs_3_), channel_id=1, source_target_pairs={{0,16},{1,17},{2,18},{3,19},{4,20},{5,21},{6,22},{7,23},{8,24},{9,... | collective-permute-start | bytes 196616 | tf_op jit(solution)/shard_map/ppermute | solution.py:58
  27.6 6.6 %collective-permute-start.12 = (f32[3,64,128]{2,1,0:T(8,128)S(1)}, f32[3,64,128]{2,1,0:T(8,128)S(1)}, u32[]{:S(2)}, u32[]{:S(2)}) collective-permute-start(f32[3,64,128]{2,1,0:T(8,128)S(1)} %halve.1), channel_id=1, source_target_pairs={{0,16},{1,17},{2,18},{3,19},{4,20},{5,21},{6,22},{7,23},{8,24},{9,... | collective-permute-start | bytes 294920 | tf_op jit(solution)/shard_map/ppermute | solution.py:58
  31.0 5.7 %collective-permute-start.9 = (f32[384,128]{1,0:T(8,128)S(1)}, f32[384,128]{1,0:T(8,128)S(1)}, u32[]{:S(2)}, u32[]{:S(2)}) collective-permute-start(f32[384,128]{1,0:T(8,128)S(1)} %descend.1.refs_0_), channel_id=1, source_target_pairs={{0,2},{1,3},{2,0},{3,1},{4,6},{5,7},{6,4},{7,5},{8,10},{9,11},{10,... | collective-permute-start | bytes 589832 | tf_op jit(solution)/shard_map/ppermute | solution.py:58
  33.0 2.4 %collective-permute-start.10 = (f32[384,128]{1,0:T(8,128)S(1)}, f32[384,128]{1,0:T(8,128)S(1)}, u32[]{:S(2)}, u32[]{:S(2)}) collective-permute-start(f32[384,128]{1,0:T(8,128)S(1)} %broadcast_add_fusion.1), channel_id=1, source_target_pairs={{0,1},{1,0},{2,3},{3,2},{4,5},{5,4},{6,7},{7,6},{8,9},{9,8},{10,11... | collective-permute-start | bytes 589832 | tf_op jit(solution)/shard_map/ppermute | solution.py:58
  34.3 4.7 %collective-permute-start.13 = (f32[3,64,128]{2,1,0:T(8,128)S(1)}, f32[3,64,128]{2,1,0:T(8,128)S(1)}, u32[]{:S(2)}, u32[]{:S(2)}) collective-permute-start(f32[3,64,128]{2,1,0:T(8,128)S(1)} %broadcast_add_fusion.2), channel_id=1, source_target_pairs={{0,4},{1,5},{2,6},{3,7},{4,0},{5,1},{6,2},{7,3},{8,12},{9,13},{10,... | collective-permute-start | bytes 294920 | tf_op jit(solution)/shard_map/ppermute | solution.py:58
  36.7 2.8 %collective-permute-start.11 = (f32[384,128]{1,0:T(8,128)S(1)}, f32[384,128]{1,0:T(8,128)S(1)}, u32[]{:S(2)}, u32[]{:S(2)}) collective-permute-start(f32[384,128]{1,0:T(8,128)S(1)} %broadcast_add_fusion.refs_0_), channel_id=1, source_target_pairs={{0,1},{1,0},{2,3},{3,2},{4,5},{5,4},{6,7},{7,6},{8,9},{9,8},{10,11... | collective-permute-start | bytes 589832 | tf_op jit(solution)/shard_map/ppermute | solution.py:58

commit v8 on v7

--- a/solution.py
+++ b/solution.py
@@ -215,11 +215,23 @@
     token[...] = jnp.zeros_like(token)
 
 
-def last_kernel(plan, width, part, base, gain_hi, gain_lo, far, own, cross, top, out, out_top, buffer, sems):
+def cross_kernel(plan, width, column, part, base, gain_hi, gain_lo, own, out, token, buffer, sems):
     _, _, core, half = plan.here()
-    groups = ((1 - half) * 2 + core, half * 2 + core, half * 2 + 1 - core, (1 - half) * 2 + 1 - core)
+    copies = [pltpu.make_async_copy(own, out.at[:, lanes(half * 2 + core, width)], sems.at[0]),
+              pltpu.make_async_copy(buffer, out.at[:, lanes(half * 2 + 1 - core, width)], sems.at[1])]
+    copies[0].start()
+    buffer[...] = settled(base, gain_hi, gain_lo, part, column, width)
+    copies[1].start()
+    token[...] = jnp.zeros_like(token)
+    for copy in copies:
+        copy.wait()
+
+
+def last_kernel(plan, width, part, base, gain_hi, gain_lo, far, top, begun, out, out_top, buffer, sems):
+    _, _, core, half = plan.here()
+    groups = ((1 - half) * 2 + core, (1 - half) * 2 + 1 - core)
     copies = [pltpu.make_async_copy(top, out_top, sems.at[0])]
-    for done, group in zip((far, own, cross), groups):
+    for done, group in zip((far,), groups):
         copies.append(pltpu.make_async_copy(done, out.at[:, lanes(group, width)], sems.at[len(copies)]))
     for copy in copies:
         copy.start()
@@ -230,7 +242,7 @@
         change = dot(gain_hi[rows], known[0]) + (dot(gain_hi[rows], known[1]) + dot(gain_lo[rows], known[0]))
         buffer[rows] = base[rows, :width] - change
         copies.append(pltpu.make_async_copy(
-            buffer.at[pl.ds(start, step)], out.at[pl.ds(start, step), lanes(groups[3], width)],
+            buffer.at[pl.ds(start, step)], out.at[pl.ds(start, step), lanes(groups[1], width)],
             sems.at[len(copies)]))
         copies[-1].start()
     for copy in copies:
@@ -276,7 +288,7 @@
 ANY_SPEC = pl.BlockSpec(memory_space=pl.ANY)
 
 
-def call(kernel, outs, args, scratch=(), anys=(), name=None, after=(), after_hbm=(), flops=1000):
+def call(kernel, outs, args, scratch=(), anys=(), name=None, after=(), after_hbm=(), flops=1000, alias=None):
     after_hbm = [pltpu.with_memory_space_constraint(a, pltpu.HBM) for a in after_hbm]
     after_specs = [ANY_SPEC] * len(after) + [HBM_SPEC] * len(after_hbm)
     after = list(after) + after_hbm
@@ -294,6 +306,7 @@
         in_specs=specs + after_specs,
         out_specs=[spec for _, spec in outs],
         scratch_shapes=list(scratch),
+        input_output_aliases=alias or {},
         compiler_params=pltpu.CompilerParams(vmem_limit_bytes=12 * 2**20),
         cost_estimate=pl.CostEstimate(flops=flops, bytes_accessed=1000, transcendentals=0),
         name=name,
@@ -385,7 +398,12 @@
     own, token = settle(solved, base_own, columns)
     cross = plan.swap_rhs(solved + token[:1], 1)
     stacks.append(plan.swap_leaf(stacks[-1] + token[:1], 1))
-    cross, token = settle(cross, base_other, columns)
+    whole = (order, plan.group_count * columns)
+    out, token = call(
+        functools.partial(cross_kernel, plan, columns, columns),
+        [(pltpu.HBM(whole, F32), HBM_SPEC), inside((8, columns))],
+        [cross, base_other, gain_hi, gain_lo, own],
+        scratch=[pltpu.VMEM((order, columns), F32), pltpu.SemaphoreType.DMA((2,))], name="cross")
     far = far + token[:1]
     last = plan.swap_rhs(far, 1)
     far, token = settle(far, base_own, 0)
@@ -395,10 +413,10 @@
         [solved, back_hi, back_lo] + stacks, name="top", after=[token], flops=5 * 10**9)[0]
     out, top = call(
         functools.partial(last_kernel, plan, columns),
-        [(pltpu.HBM((order, plan.group_count * columns), F32), HBM_SPEC),
+        [(pltpu.HBM(whole, F32), HBM_SPEC),
          (pltpu.HBM((panel_count * width, columns), F32), HBM_SPEC)],
-        [last, base_other, gain_hi, gain_lo, far, own, cross, top],
-        scratch=[pltpu.VMEM((order, columns), F32), pltpu.SemaphoreType.DMA((6,))], name="last")
+        [last, base_other, gain_hi, gain_lo, far, top, out], anys=(6,), alias={6: 0},
+        scratch=[pltpu.VMEM((order, columns), F32), pltpu.SemaphoreType.DMA((4,))], name="last")
     return out, top
 
 

time: 41 us -> 40.8 us (level)
  waiting for transfers between devices: 13.5 us -> 12.6 us
  Pallas kernels: 10.9 us -> 11.4 us
    ppermute x14, waiting for transfers between devices: 13.5 us -> 12.6 us  [swap(): return lax.ppermute(value, ('leaf', 'rhs'), pairs)]
    pallas_call x13, Pallas kernels: 10.9 us -> 11.4 us  [call(): pl.pallas_call(body, out_shape=[shape for shape, _ in outs], in_specs=spe...]
  transfers between devices with their start and end apart: 14 -> 14, of which waited for: 9 -> 9; matrix products, arithmetic and copies ran while one was open for 0% -> 0% of each run, Pallas kernels for 16% -> 17%
where the time goes in v8:
time: 40.8 us; the launch traced here: 40.7 us
  starting transfers between devices  15.6 us (38%)
  waiting for transfers between devices  12.6 us (31%)
  Pallas kernels  11.4 us (28%)
  between operations  0.83 us (2%)
    ppermute x14, starting transfers between devices, swap(): return lax.ppermute(value, ('leaf', 'rhs'), pairs)  15.6 us
    ppermute x14, waiting for transfers between devices, swap(): return lax.ppermute(value, ('leaf', 'rhs'), pairs)  12.6 us
    pallas_call x13, Pallas kernels, call(): pl.pallas_call(body, out_shape=[shape for shape, _ in outs], in_specs=spe...  11.4 us
  transfers between devices with their start and end apart: 14, of which 9 were waited for; matrix products, arithmetic and copies ran while one was open for 0% of the time, Pallas kernels for 17%

profile of v8, /device:TPU:0, one launch (start us, length us, event | category | flops | bytes accessed | tf_op | source)
XLA Modules:
  0.0 40.7 jit_solution(15989583489463220793)
XLA Ops:
  0.6 3.0 %lift.1 = (f32[224,128]{1,0:T(8,128)S(1)}, f32[544,128]{1,0:T(8,128)S(1)}, f32[512,256]{1,0:T(8,128)S(1)}, f32[512,256]{1,0:T(8,128)S(1)}, bf16[512,512]{1,0:T(8...) custom-call(f32[512,512]{1,0:T(8,128)} %refs_0_.2, ...), custom_call_target="tpu_custom_call" | custom-call | flops 1000 | bytes 1000 | tf_op jit(solution)/shard_map/lift/pallas_call | solution.py:303
  3.7 0.5 %collective-permute-start = (f32[544,128]{1,0:T(8,128)S(1)}, f32[544,128]{1,0:T(8,128)S(1)}, u32[]{:S(2)}, u32[]{:S(2)}) collective-permute-start(f32[544,128]{1,0:T(8,128)S(1)} %get-tuple-element.38), channel_id=1, source_target_pairs={{0,1},{1,0},{2,3},{3,2},{4,5},{5,4},{6,7},{7,6},{8,9},{9,8},{10,11... | collective-permute-start | bytes 835592 | tf_op jit(solution)/shard_map/ppermute | solution.py:58
  4.2 1.1 %own.1 = (f32[224,128]{1,0:T(8,128)S(1)}, f32[544,128]{1,0:T(8,128)S(1)}, f32[512,256]{1,0:T(8,128)S(1)}) custom-call(f32[512,256]{1,0:T(8,128)S(1)} %get-tuple-element.32.refs_0_, bf16[512,512]{1,0:T(8,128)(2,1)S(1)} %get-tuple-element.33.refs_1_.refs_0_, bf16[512,512]{1,0:T(8,128)(2,1)S(1)} %get-tuple-element.34.refs_2_.refs_1_, ...), custom_call_target="tpu_custom_call" | custom-call | flops 1000 | bytes 1000 | tf_op jit(solution)/shard_map/own/pallas_call | solution.py:303
  5.3 0.2 collective-permute-done.1
  5.5 2.9 %collective-permute-start.2 = (f32[224,128]{1,0:T(8,128)S(1)}, f32[224,128]{1,0:T(8,128)S(1)}, u32[]{:S(2)}, u32[]{:S(2)}) collective-permute-start(f32[224,128]{1,0:T(8,128)S(1)} %add.62.refs_6_), channel_id=1, source_target_pairs={{0,2},{1,3},{2,0},{3,1},{4,6},{5,7},{6,4},{7,5},{8,10},{9,11},{10,... | collective-permute-start | bytes 344072 | tf_op jit(solution)/shard_map/ppermute | solution.py:58
  8.5 0.1 collective-permute-start.3
  8.6 1.8 %turn.1 = (f32[512,256]{1,0:T(8,128)S(1)}, f32[512,256]{1,0:T(8,128)S(1)}, bf16[512,384]{1,0:T(8,128)(2,1)S(1)}, bf16[512,384]{1,0:T(8,128)(2,1)S(1)}, f32[8,128]{1,0:T(8,128)S(1)}) custom-call(bf16[512,512]{1,0:T(8,128)(2,1)S(1)} %get-tuple-element.33.refs_1_.refs_0_, bf16[512,512]{1,0:T(8,128)(2,1)S(1)} %get-tuple-element.34.refs_2_.refs_1_, ...), custom_call_target="tpu_custom_call" | custom-call | flops 1000 | bytes 1000 | tf_op jit(solution)/shard_map/turn/pallas_call | solution.py:303
  10.4 1.9 %collective-permute-done.2 = f32[224,128]{1,0:T(8,128)S(1)} collective-permute-done((f32[224,128]{1,0:T(8,128)S(1)}, f32[224,128]{1,0:T(8,128)S(1)}, u32[]{:S(2)}, u32[]{:S(2)}) %collective-permute-start.2) | collective-permute-done | bytes 114720 | tf_op jit(solution)/shard_map/ppermute | solution.py:58
  12.4 2.2 %collective-permute-start.4 = (f32[224,128]{1,0:T(8,128)S(1)}, f32[224,128]{1,0:T(8,128)S(1)}, u32[]{:S(2)}, u32[]{:S(2)}) collective-permute-start(f32[224,128]{1,0:T(8,128)S(1)} %fusion.refs_0_), channel_id=1, source_target_pairs={{0,4},{1,5},{2,6},{3,7},{4,0},{5,1},{6,2},{7,3},{8,12},{9,13},{10,... | collective-permute-start | bytes 344072 | tf_op jit(solution)/shard_map/ppermute | solution.py:58
  14.6 0.9 %collective-permute-start.5 = (f32[160,128]{1,0:T(8,128)S(1)}, f32[160,128]{1,0:T(8,128)S(1)}, u32[]{:S(2)}, u32[]{:S(2)}) collective-permute-start(f32[160,128]{1,0:T(8,128)S(1)} %fusion.1.refs_2_.refs_1_), channel_id=1, source_target_pairs={{0,4},{1,5},{2,6},{3,7},{4,0},{5,1},{6,2},{7,3},{8,12},{9,13},{10,... | collective-permute-start | bytes 245768 | tf_op jit(solution)/shard_map/ppermute | solution.py:58
  15.5 0.6 %ready.1 = (bf16[7,384,128]{2,1,0:T(8,128)(2,1)S(1)}, bf16[7,384,128]{2,1,0:T(8,128)(2,1)S(1)}, bf16[7,128,384]{2,1,0:T(8,128)(2,1)S(1)}, bf16[7,128,384]{2,1,0:T(8,128)(2,1)S(1)}) custom-call(f32[7,128,128]{2,1,0:T(8,128)S(1)} %copy-done.1, f32[10,128,128]{2,1,0:T(8,128)S(1)} %copy-done, f32[160,128]{1,0:T(8,128)S(1)} %fusion.1.refs_2_.refs_1_), custom_call_target="tpu_custom_call" | custom-call | flops 1000 | bytes 1000 | tf_op jit(solution)/shard_map/ready/pallas_call | solution.py:303
  16.1 2.0 %collective-permute-done.4.refs_2_ = f32[224,128]{1,0:T(8,128)S(1)} collective-permute-done((f32[224,128]{1,0:T(8,128)S(1)}, f32[224,128]{1,0:T(8,128)S(1)}, u32[]{:S(2)}, u32[]{:S(2)}) %collective-permute-start.4) | collective-permute-done | bytes 114720 | tf_op jit(solution)/shard_map/ppermute | solution.py:58
  18.1 1.0 %collective-permute-done.5.refs_3_ = f32[160,128]{1,0:T(8,128)S(1)} collective-permute-done((f32[160,128]{1,0:T(8,128)S(1)}, f32[160,128]{1,0:T(8,128)S(1)}, u32[]{:S(2)}, u32[]{:S(2)}) %collective-permute-start.5) | collective-permute-done | bytes 81952 | tf_op jit(solution)/shard_map/ppermute | solution.py:58
  19.1 0.2 climb.2
  19.3 1.6 %collective-permute-start.6 = (f32[256,128]{1,0:T(8,128)S(1)}, f32[256,128]{1,0:T(8,128)S(1)}, u32[]{:S(2)}, u32[]{:S(2)}) collective-permute-start(f32[256,128]{1,0:T(8,128)S(1)} %get-tuple-element.46.refs_0_), channel_id=1, source_target_pairs={{0,8},{1,9},{2,10},{3,11},{4,12},{5,13},{6,14},{7,15},{8,0},{9,1},... | collective-permute-start | bytes 393224 | tf_op jit(solution)/shard_map/ppermute | solution.py:58
  21.0 0.5 %collective-permute-start.8 = (f32[1,128,128]{2,1,0:T(8,128)S(1)}, f32[1,128,128]{2,1,0:T(8,128)S(1)}, u32[]{:S(2)}, u32[]{:S(2)}) collective-permute-start(f32[1,128,128]{2,1,0:T(8,128)S(1)} %bitcast.8), channel_id=1, source_target_pairs={{0,8},{1,9},{2,10},{3,11},{4,12},{5,13},{6,14},{7,15},{8,0},{9,1},... | collective-permute-start | bytes 196616 | tf_op jit(solution)/shard_map/ppermute | solution.py:58
  21.4 2.9 %collective-permute-done.6.refs_1_ = f32[256,128]{1,0:T(8,128)S(1)} collective-permute-done((f32[256,128]{1,0:T(8,128)S(1)}, f32[256,128]{1,0:T(8,128)S(1)}, u32[]{:S(2)}, u32[]{:S(2)}) %collective-permute-start.6) | collective-permute-done | bytes 131104 | tf_op jit(solution)/shard_map/ppermute | solution.py:58
  24.4 0.2 climb.3
  24.6 3.0 %collective-permute-start.7 = (f32[128,128]{1,0:T(8,128)S(1)}, f32[128,128]{1,0:T(8,128)S(1)}, u32[]{:S(2)}, u32[]{:S(2)}) collective-permute-start(f32[128,128]{1,0:T(8,128)S(1)} %get-tuple-element.47.refs_0_.refs_3_), channel_id=1, source_target_pairs={{0,16},{1,17},{2,18},{3,19},{4,20},{5,21},{6,22},{7,23},{8,24},{9,... | collective-permute-start | bytes 196616 | tf_op jit(solution)/shard_map/ppermute | solution.py:58
  27.6 0.8 %collective-permute-start.12 = (f32[3,64,128]{2,1,0:T(8,128)S(1)}, f32[3,64,128]{2,1,0:T(8,128)S(1)}, u32[]{:S(2)}, u32[]{:S(2)}) collective-permute-start(f32[3,64,128]{2,1,0:T(8,128)S(1)} %halve.1), channel_id=1, source_target_pairs={{0,16},{1,17},{2,18},{3,19},{4,20},{5,21},{6,22},{7,23},{8,24},{9,... | collective-permute-start | bytes 294920 | tf_op jit(solution)/shard_map/ppermute | solution.py:58
  28.4 1.8 %collective-permute-done.7.refs_1_ = f32[128,128]{1,0:T(8,128)S(1)} collective-permute-done((f32[128,128]{1,0:T(8,128)S(1)}, f32[128,128]{1,0:T(8,128)S(1)}, u32[]{:S(2)}, u32[]{:S(2)}) %collective-permute-start.7) | collective-permute-done | bytes 65568 | tf_op jit(solution)/shard_map/ppermute | solution.py:58
  30.2 0.8 %descend.1.refs_0_ = f32[384,128]{1,0:T(8,128)S(1)} custom-call(f32[128,128]{1,0:T(8,128)S(1)} %get-tuple-element.47.refs_0_.refs_3_, f32[128,128]{1,0:T(8,128)S(1)} %collective-permute-done.7.refs_1_, bf16[7,384,128]{2,1,0:T(8,128)(2,1)S(1)} %get-tuple-element.44.refs_4_.refs_2_, bf16[7,384,128]{2,1,0:T(8,128)(2,1)S(1)} %get-tuple-element.45.refs_5_.refs_3_, ...), custom_call_target="tpu_custom_call" | custom-call | flops 1000 | bytes 1000 | tf_op jit(solution)/shard_map/descend/pallas_call | solution.py:303
  31.0 1.6 %collective-permute-start.9 = (f32[384,128]{1,0:T(8,128)S(1)}, f32[384,128]{1,0:T(8,128)S(1)}, u32[]{:S(2)}, u32[]{:S(2)}) collective-permute-start(f32[384,128]{1,0:T(8,128)S(1)} %descend.1.refs_0_), channel_id=1, source_target_pairs={{0,2},{1,3},{2,0},{3,1},{4,6},{5,7},{6,4},{7,5},{8,10},{9,11},{10,... | collective-permute-start | bytes 589832 | tf_op jit(solution)/shard_map/ppermute | solution.py:58
  32.5 0.5 %settle.2 = (f32[512,128]{1,0:T(8,128)S(1)}, f32[8,128]{1,0:T(8,128)S(1)}) custom-call(f32[384,128]{1,0:T(8,128)S(1)} %descend.1.refs_0_, f32[512,256]{1,0:T(8,128)S(1)} %get-tuple-element.52.refs_1_, bf16[512,384]{1,0:T(8,128)(2,1)S(1)} %get-tuple-element.53.refs_2_, bf16[512,384]{1,0:T(8,128)(2,1)S(1)} %get-tuple-element.54.refs_3_), custom_call_target="tpu_custom_call" | custom-call | flops 1000 | bytes 1000 | tf_op jit(solution)/shard_map/settle/pallas_call | solution.py:303
  33.1 1.1 %collective-permute-done.12.refs_4_ = f32[3,64,128]{2,1,0:T(8,128)S(1)} collective-permute-done((f32[3,64,128]{2,1,0:T(8,128)S(1)}, f32[3,64,128]{2,1,0:T(8,128)S(1)}, u32[]{:S(2)}, u32[]{:S(2)}) %collective-permute-start.12) | collective-permute-done | bytes 98336 | tf_op jit(solution)/shard_map/ppermute | solution.py:58
  34.3 1.2 %collective-permute-start.13 = (f32[3,64,128]{2,1,0:T(8,128)S(1)}, f32[3,64,128]{2,1,0:T(8,128)S(1)}, u32[]{:S(2)}, u32[]{:S(2)}) collective-permute-start(f32[3,64,128]{2,1,0:T(8,128)S(1)} %broadcast_add_fusion.2), channel_id=1, source_target_pairs={{0,4},{1,5},{2,6},{3,7},{4,0},{5,1},{6,2},{7,3},{8,12},{9,13},{10,... | collective-permute-start | bytes 294920 | tf_op jit(solution)/shard_map/ppermute | solution.py:58
  35.4 1.2 %cross.1 = (f32[512,512]{1,0:T(8,128)}, f32[8,128]{1,0:T(8,128)S(1)}) custom-call(f32[384,128]{1,0:T(8,128)S(1)} %collective-permute-done.10.refs_0_, f32[512,256]{1,0:T(8,128)S(1)} %get-tuple-element.56.refs_1_, bf16[512,384]{1,0:T(8,128)(2,1)S(1)} %get-tuple-element.53.refs_2_, bf16[512,384]{1,0:T(8,128)(2,1)S(1)} %get-tuple-element.54.refs_3_, ...), custom_call_target="tpu_custom_call" | custom-call | flops 1000 | bytes 1000 | tf_op jit(solution)/shard_map/cross/pallas_call | solution.py:303
  36.7 0.2 collective-permute-start.11
  36.9 0.5 %settle.3 = (f32[512,128]{1,0:T(8,128)S(1)}, f32[8,128]{1,0:T(8,128)S(1)}) custom-call(f32[384,128]{1,0:T(8,128)S(1)} %broadcast_add_fusion.refs_0_, f32[512,256]{1,0:T(8,128)S(1)} %get-tuple-element.52.refs_1_, bf16[512,384]{1,0:T(8,128)(2,1)S(1)} %get-tuple-element.53.refs_2_, bf16[512,384]{1,0:T(8,128)(2,1)S(1)} %get-tuple-element.54.refs_3_), custom_call_target="tpu_custom_call" | custom-call | flops 1000 | bytes 1000 | tf_op jit(solution)/shard_map/settle/pallas_call | solution.py:303
  37.4 1.6 %collective-permute-done.13.refs_5_ = f32[3,64,128]{2,1,0:T(8,128)S(1)} collective-permute-done((f32[3,64,128]{2,1,0:T(8,128)S(1)}, f32[3,64,128]{2,1,0:T(8,128)S(1)}, u32[]{:S(2)}, u32[]{:S(2)}) %collective-permute-start.13) | collective-permute-done | bytes 98336 | tf_op jit(solution)/shard_map/ppermute | solution.py:58
  38.9 0.5 %top.1.refs_5_ = f32[896,128]{1,0:T(8,128)S(1)} custom-call(f32[384,128]{1,0:T(8,128)S(1)} %descend.1.refs_0_, bf16[7,128,384]{2,1,0:T(8,128)(2,1)S(1)} %get-tuple-element.48.refs_4_.refs_1_, bf16[7,128,384]{2,1,0:T(8,128)(2,1)S(1)} %get-tuple-element.49.refs_5_.refs_2_, f32[1,128,128]{2,1,0:T(8,128)S(1)} %collective-permute-done.8.refs_8_.refs_1_.refs_3_, ...), custom_call_target="tpu_custom_call" | custom-call | flops 5000000000 | bytes 1000 | tf_op jit(solution)/shard_map/top/pallas_call | solution.py:303
  39.5 1.2 %last.1 = (f32[512,512]{1,0:T(8,128)}, f32[896,128]{1,0:T(8,128)}) custom-call(f32[384,128]{1,0:T(8,128)S(1)} %collective-permute-done.11.refs_0_, f32[512,256]{1,0:T(8,128)S(1)} %get-tuple-element.56.refs_1_, bf16[512,384]{1,0:T(8,128)(2,1)S(1)} %get-tuple-element.53.refs_2_, ...), custom_call_target="tpu_custom_call", output_to_operand_aliasing={{0}: (6, {})} | custom-call | flops 1000 | bytes 1000 | tf_op jit(solution)/shard_map/last/pallas_call | solution.py:303
  (26 shorter events, 0.4 us)
Async XLA Ops:
  0.6 3.6 %copy-start.2 = (f32[896,128]{1,0:T(8,128)S(1)}, f32[896,128]{1,0:T(8,128)}, u32[]{:S(2)}) copy-start(f32[896,128]{1,0:T(8,128)} %refs_5_.1) | copy-start | bytes 1376260
  3.6 11.9 %copy-start = (f32[10,128,128]{2,1,0:T(8,128)S(1)}, f32[10,128,128]{2,1,0:T(8,128)}, u32[]{:S(2)}) copy-start(f32[10,128,128]{2,1,0:T(8,128)} %refs_1_.3) | copy-start | bytes 1966084
  3.6 11.9 %copy-start.1 = (f32[7,128,128]{2,1,0:T(8,128)S(1)}, f32[7,128,128]{2,1,0:T(8,128)}, u32[]{:S(2)}) copy-start(f32[7,128,128]{2,1,0:T(8,128)} %refs_0_.3) | copy-start | bytes 1376260
  3.7 4.8 %collective-permute-start = (f32[544,128]{1,0:T(8,128)S(1)}, f32[544,128]{1,0:T(8,128)S(1)}, u32[]{:S(2)}, u32[]{:S(2)}) collective-permute-start(f32[544,128]{1,0:T(8,128)S(1)} %get-tuple-element.38), channel_id=1, source_target_pairs={{0,1},{1,0},{2,3},{3,2},{4,5},{5,4},{6,7},{7,6},{8,9},{9,8},{10,11... | collective-permute-start | bytes 835592 | tf_op jit(solution)/shard_map/ppermute | solution.py:58
  4.2 1.3 %collective-permute-start.1 = (f32[224,128]{1,0:T(8,128)S(1)}, f32[224,128]{1,0:T(8,128)S(1)}, u32[]{:S(2)}, u32[]{:S(2)}) collective-permute-start(f32[224,128]{1,0:T(8,128)S(1)} %get-tuple-element.40), channel_id=1, source_target_pairs={{0,1},{1,0},{2,3},{3,2},{4,5},{5,4},{6,7},{7,6},{8,9},{9,8},{10,11... | collective-permute-start | bytes 344072 | tf_op jit(solution)/shard_map/ppermute | solution.py:58
  5.5 6.9 %collective-permute-start.2 = (f32[224,128]{1,0:T(8,128)S(1)}, f32[224,128]{1,0:T(8,128)S(1)}, u32[]{:S(2)}, u32[]{:S(2)}) collective-permute-start(f32[224,128]{1,0:T(8,128)S(1)} %add.62.refs_6_), channel_id=1, source_target_pairs={{0,2},{1,3},{2,0},{3,1},{4,6},{5,7},{6,4},{7,5},{8,10},{9,11},{10,... | collective-permute-start | bytes 344072 | tf_op jit(solution)/shard_map/ppermute | solution.py:58
  8.5 6.1 %collective-permute-start.3 = (f32[160,128]{1,0:T(8,128)S(1)}, f32[160,128]{1,0:T(8,128)S(1)}, u32[]{:S(2)}, u32[]{:S(2)}) collective-permute-start(f32[160,128]{1,0:T(8,128)S(1)} %slice_add_fusion.3.refs_7_), channel_id=1, source_target_pairs={{0,2},{1,3},{2,0},{3,1},{4,6},{5,7},{6,4},{7,5},{8,10},{9,11},{10,... | collective-permute-start | bytes 245768 | tf_op jit(solution)/shard_map/ppermute | solution.py:58
  12.4 5.7 %collective-permute-start.4 = (f32[224,128]{1,0:T(8,128)S(1)}, f32[224,128]{1,0:T(8,128)S(1)}, u32[]{:S(2)}, u32[]{:S(2)}) collective-permute-start(f32[224,128]{1,0:T(8,128)S(1)} %fusion.refs_0_), channel_id=1, source_target_pairs={{0,4},{1,5},{2,6},{3,7},{4,0},{5,1},{6,2},{7,3},{8,12},{9,13},{10,... | collective-permute-start | bytes 344072 | tf_op jit(solution)/shard_map/ppermute | solution.py:58
  14.6 4.5 %collective-permute-start.5 = (f32[160,128]{1,0:T(8,128)S(1)}, f32[160,128]{1,0:T(8,128)S(1)}, u32[]{:S(2)}, u32[]{:S(2)}) collective-permute-start(f32[160,128]{1,0:T(8,128)S(1)} %fusion.1.refs_2_.refs_1_), channel_id=1, source_target_pairs={{0,4},{1,5},{2,6},{3,7},{4,0},{5,1},{6,2},{7,3},{8,12},{9,13},{10,... | collective-permute-start | bytes 245768 | tf_op jit(solution)/shard_map/ppermute | solution.py:58
  19.3 5.0 %collective-permute-start.6 = (f32[256,128]{1,0:T(8,128)S(1)}, f32[256,128]{1,0:T(8,128)S(1)}, u32[]{:S(2)}, u32[]{:S(2)}) collective-permute-start(f32[256,128]{1,0:T(8,128)S(1)} %get-tuple-element.46.refs_0_), channel_id=1, source_target_pairs={{0,8},{1,9},{2,10},{3,11},{4,12},{5,13},{6,14},{7,15},{8,0},{9,1},... | collective-permute-start | bytes 393224 | tf_op jit(solution)/shard_map/ppermute | solution.py:58
  21.0 6.6 %collective-permute-start.8 = (f32[1,128,128]{2,1,0:T(8,128)S(1)}, f32[1,128,128]{2,1,0:T(8,128)S(1)}, u32[]{:S(2)}, u32[]{:S(2)}) collective-permute-start(f32[1,128,128]{2,1,0:T(8,128)S(1)} %bitcast.8), channel_id=1, source_target_pairs={{0,8},{1,9},{2,10},{3,11},{4,12},{5,13},{6,14},{7,15},{8,0},{9,1},... | collective-permute-start | bytes 196616 | tf_op jit(solution)/shard_map/ppermute | solution.py:58
  24.6 5.6 %collective-permute-start.7 = (f32[128,128]{1,0:T(8,128)S(1)}, f32[128,128]{1,0:T(8,128)S(1)}, u32[]{:S(2)}, u32[]{:S(2)}) collective-permute-start(f32[128,128]{1,0:T(8,128)S(1)} %get-tuple-element.47.refs_0_.refs_3_), channel_id=1, source_target_pairs={{0,16},{1,17},{2,18},{3,19},{4,20},{5,21},{6,22},{7,23},{8,24},{9,... | collective-permute-start | bytes 196616 | tf_op jit(solution)/shard_map/ppermute | solution.py:58
  27.6 6.6 %collective-permute-start.12 = (f32[3,64,128]{2,1,0:T(8,128)S(1)}, f32[3,64,128]{2,1,0:T(8,128)S(1)}, u32[]{:S(2)}, u32[]{:S(2)}) collective-permute-start(f32[3,64,128]{2,1,0:T(8,128)S(1)} %halve.1), channel_id=1, source_target_pairs={{0,16},{1,17},{2,18},{3,19},{4,20},{5,21},{6,22},{7,23},{8,24},{9,... | collective-permute-start | bytes 294920 | tf_op jit(solution)/shard_map/ppermute | solution.py:58
  31.0 5.7 %collective-permute-start.9 = (f32[384,128]{1,0:T(8,128)S(1)}, f32[384,128]{1,0:T(8,128)S(1)}, u32[]{:S(2)}, u32[]{:S(2)}) collective-permute-start(f32[384,128]{1,0:T(8,128)S(1)} %descend.1.refs_0_), channel_id=1, source_target_pairs={{0,2},{1,3},{2,0},{3,1},{4,6},{5,7},{6,4},{7,5},{8,10},{9,11},{10,... | collective-permute-start | bytes 589832 | tf_op jit(solution)/shard_map/ppermute | solution.py:58
  33.0 2.4 %collective-permute-start.10 = (f32[384,128]{1,0:T(8,128)S(1)}, f32[384,128]{1,0:T(8,128)S(1)}, u32[]{:S(2)}, u32[]{:S(2)}) collective-permute-start(f32[384,128]{1,0:T(8,128)S(1)} %broadcast_add_fusion.1), channel_id=1, source_target_pairs={{0,1},{1,0},{2,3},{3,2},{4,5},{5,4},{6,7},{7,6},{8,9},{9,8},{10,11... | collective-permute-start | bytes 589832 | tf_op jit(solution)/shard_map/ppermute | solution.py:58
  34.3 4.7 %collective-permute-start.13 = (f32[3,64,128]{2,1,0:T(8,128)S(1)}, f32[3,64,128]{2,1,0:T(8,128)S(1)}, u32[]{:S(2)}, u32[]{:S(2)}) collective-permute-start(f32[3,64,128]{2,1,0:T(8,128)S(1)} %broadcast_add_fusion.2), channel_id=1, source_target_pairs={{0,4},{1,5},{2,6},{3,7},{4,0},{5,1},{6,2},{7,3},{8,12},{9,13},{10,... | collective-permute-start | bytes 294920 | tf_op jit(solution)/shard_map/ppermute | solution.py:58
  36.7 2.8 %collective-permute-start.11 = (f32[384,128]{1,0:T(8,128)S(1)}, f32[384,128]{1,0:T(8,128)S(1)}, u32[]{:S(2)}, u32[]{:S(2)}) collective-permute-start(f32[384,128]{1,0:T(8,128)S(1)} %broadcast_add_fusion.refs_0_), channel_id=1, source_target_pairs={{0,1},{1,0},{2,3},{3,2},{4,5},{5,4},{6,7},{7,6},{8,9},{9,8},{10,11... | collective-permute-start | bytes 589832 | tf_op jit(solution)/shard_map/ppermute | solution.py:58

commit v9 on v8

--- a/solution.py
+++ b/solution.py
@@ -196,13 +196,19 @@
     forwards = refs[6 : 6 + levels - 1]
     solved = refs[6 + levels - 1]
     _, place, _, _ = plan.here()
+    panels = [plan.panel(place, level) for level in range(levels)]
+
+    def part(level, step, known):
+        columns = slice(step * width, (step + 1) * width)
+        return dot_split(back_hi[panels[level], :, columns], back_lo[panels[level], :, columns], known)
+
+    totals = [part(level, 0, forwards[level][...]) for level in range(levels - 1)]
     top = dot_split(fore_hi[0, :width], fore_lo[0, :width], value[...] + came[...])
-    above = []
-    for level in reversed(range(levels)):
-        forward = top if level == levels - 1 else forwards[level][...]
-        result = backward(plan, back_hi, back_lo, plan.panel(place, level), level, forward, above)
-        solved[pl.ds(level * width, width), :] = result
-        above = [result] + above
+    totals.append(part(levels - 1, 0, top))
+    for above in reversed(range(levels)):
+        solved[pl.ds(above * width, width), :] = totals[above]
+        for level in reversed(range(above)):
+            totals[level] = totals[level] + part(level, above - level, totals[above])
 
 
 def settled(base, gain_hi, gain_lo, part, column, width):

time: 40.8 us -> 40.8 us (level)
  no operation moved by 1% of the time
where the time goes in v9:
time: 40.8 us; the launch traced here: 40.7 us
  starting transfers between devices  15.6 us (38%)
  waiting for transfers between devices  12.6 us (31%)
  Pallas kernels  11.4 us (28%)
  between operations  0.83 us (2%)
    ppermute x14, starting transfers between devices, swap(): return lax.ppermute(value, ('leaf', 'rhs'), pairs)  15.6 us
    ppermute x14, waiting for transfers between devices, swap(): return lax.ppermute(value, ('leaf', 'rhs'), pairs)  12.6 us
    pallas_call x13, Pallas kernels, call(): pl.pallas_call(body, out_shape=[shape for shape, _ in outs], in_specs=spe...  11.4 us
  transfers between devices with their start and end apart: 14, of which 9 were waited for; matrix products, arithmetic and copies ran while one was open for 0% of the time, Pallas kernels for 17%

profile of v9, /device:TPU:0, one launch (start us, length us, event | category | flops | bytes accessed | tf_op | source)
XLA Modules:
  0.0 40.7 jit_solution(16706001032597484500)
XLA Ops:
  0.6 3.0 %lift.1 = (f32[224,128]{1,0:T(8,128)S(1)}, f32[544,128]{1,0:T(8,128)S(1)}, f32[512,256]{1,0:T(8,128)S(1)}, f32[512,256]{1,0:T(8,128)S(1)}, bf16[512,512]{1,0:T(8...) custom-call(f32[512,512]{1,0:T(8,128)} %refs_0_.2, ...), custom_call_target="tpu_custom_call" | custom-call | flops 1000 | bytes 1000 | tf_op jit(solution)/shard_map/lift/pallas_call | solution.py:309
  3.7 0.5 %collective-permute-start = (f32[544,128]{1,0:T(8,128)S(1)}, f32[544,128]{1,0:T(8,128)S(1)}, u32[]{:S(2)}, u32[]{:S(2)}) collective-permute-start(f32[544,128]{1,0:T(8,128)S(1)} %get-tuple-element.38), channel_id=1, source_target_pairs={{0,1},{1,0},{2,3},{3,2},{4,5},{5,4},{6,7},{7,6},{8,9},{9,8},{10,11... | collective-permute-start | bytes 835592 | tf_op jit(solution)/shard_map/ppermute | solution.py:58
  4.2 1.1 %own.1 = (f32[224,128]{1,0:T(8,128)S(1)}, f32[544,128]{1,0:T(8,128)S(1)}, f32[512,256]{1,0:T(8,128)S(1)}) custom-call(f32[512,256]{1,0:T(8,128)S(1)} %get-tuple-element.32.refs_0_, bf16[512,512]{1,0:T(8,128)(2,1)S(1)} %get-tuple-element.33.refs_1_.refs_0_, bf16[512,512]{1,0:T(8,128)(2,1)S(1)} %get-tuple-element.34.refs_2_.refs_1_, ...), custom_call_target="tpu_custom_call" | custom-call | flops 1000 | bytes 1000 | tf_op jit(solution)/shard_map/own/pallas_call | solution.py:309
  5.3 0.2 collective-permute-done.1
  5.5 2.9 %collective-permute-start.2 = (f32[224,128]{1,0:T(8,128)S(1)}, f32[224,128]{1,0:T(8,128)S(1)}, u32[]{:S(2)}, u32[]{:S(2)}) collective-permute-start(f32[224,128]{1,0:T(8,128)S(1)} %add.62.refs_6_), channel_id=1, source_target_pairs={{0,2},{1,3},{2,0},{3,1},{4,6},{5,7},{6,4},{7,5},{8,10},{9,11},{10,... | collective-permute-start | bytes 344072 | tf_op jit(solution)/shard_map/ppermute | solution.py:58
  8.5 0.1 collective-permute-start.3
  8.6 1.8 %turn.1 = (f32[512,256]{1,0:T(8,128)S(1)}, f32[512,256]{1,0:T(8,128)S(1)}, bf16[512,384]{1,0:T(8,128)(2,1)S(1)}, bf16[512,384]{1,0:T(8,128)(2,1)S(1)}, f32[8,128]{1,0:T(8,128)S(1)}) custom-call(bf16[512,512]{1,0:T(8,128)(2,1)S(1)} %get-tuple-element.33.refs_1_.refs_0_, bf16[512,512]{1,0:T(8,128)(2,1)S(1)} %get-tuple-element.34.refs_2_.refs_1_, ...), custom_call_target="tpu_custom_call" | custom-call | flops 1000 | bytes 1000 | tf_op jit(solution)/shard_map/turn/pallas_call | solution.py:309
  10.4 1.9 %collective-permute-done.2 = f32[224,128]{1,0:T(8,128)S(1)} collective-permute-done((f32[224,128]{1,0:T(8,128)S(1)}, f32[224,128]{1,0:T(8,128)S(1)}, u32[]{:S(2)}, u32[]{:S(2)}) %collective-permute-start.2) | collective-permute-done | bytes 114720 | tf_op jit(solution)/shard_map/ppermute | solution.py:58
  12.4 2.2 %collective-permute-start.4 = (f32[224,128]{1,0:T(8,128)S(1)}, f32[224,128]{1,0:T(8,128)S(1)}, u32[]{:S(2)}, u32[]{:S(2)}) collective-permute-start(f32[224,128]{1,0:T(8,128)S(1)} %fusion.refs_0_), channel_id=1, source_target_pairs={{0,4},{1,5},{2,6},{3,7},{4,0},{5,1},{6,2},{7,3},{8,12},{9,13},{10,... | collective-permute-start | bytes 344072 | tf_op jit(solution)/shard_map/ppermute | solution.py:58
  14.6 0.9 %collective-permute-start.5 = (f32[160,128]{1,0:T(8,128)S(1)}, f32[160,128]{1,0:T(8,128)S(1)}, u32[]{:S(2)}, u32[]{:S(2)}) collective-permute-start(f32[160,128]{1,0:T(8,128)S(1)} %fusion.1.refs_2_.refs_1_), channel_id=1, source_target_pairs={{0,4},{1,5},{2,6},{3,7},{4,0},{5,1},{6,2},{7,3},{8,12},{9,13},{10,... | collective-permute-start | bytes 245768 | tf_op jit(solution)/shard_map/ppermute | solution.py:58
  15.5 0.6 %ready.1 = (bf16[7,384,128]{2,1,0:T(8,128)(2,1)S(1)}, bf16[7,384,128]{2,1,0:T(8,128)(2,1)S(1)}, bf16[7,128,384]{2,1,0:T(8,128)(2,1)S(1)}, bf16[7,128,384]{2,1,0:T(8,128)(2,1)S(1)}) custom-call(f32[7,128,128]{2,1,0:T(8,128)S(1)} %copy-done.1, f32[10,128,128]{2,1,0:T(8,128)S(1)} %copy-done, f32[160,128]{1,0:T(8,128)S(1)} %fusion.1.refs_2_.refs_1_), custom_call_target="tpu_custom_call" | custom-call | flops 1000 | bytes 1000 | tf_op jit(solution)/shard_map/ready/pallas_call | solution.py:309
  16.1 2.0 %collective-permute-done.4.refs_2_ = f32[224,128]{1,0:T(8,128)S(1)} collective-permute-done((f32[224,128]{1,0:T(8,128)S(1)}, f32[224,128]{1,0:T(8,128)S(1)}, u32[]{:S(2)}, u32[]{:S(2)}) %collective-permute-start.4) | collective-permute-done | bytes 114720 | tf_op jit(solution)/shard_map/ppermute | solution.py:58
  18.1 1.0 %collective-permute-done.5.refs_3_ = f32[160,128]{1,0:T(8,128)S(1)} collective-permute-done((f32[160,128]{1,0:T(8,128)S(1)}, f32[160,128]{1,0:T(8,128)S(1)}, u32[]{:S(2)}, u32[]{:S(2)}) %collective-permute-start.5) | collective-permute-done | bytes 81952 | tf_op jit(solution)/shard_map/ppermute | solution.py:58
  19.1 0.2 climb.2
  19.3 1.6 %collective-permute-start.6 = (f32[256,128]{1,0:T(8,128)S(1)}, f32[256,128]{1,0:T(8,128)S(1)}, u32[]{:S(2)}, u32[]{:S(2)}) collective-permute-start(f32[256,128]{1,0:T(8,128)S(1)} %get-tuple-element.46.refs_0_), channel_id=1, source_target_pairs={{0,8},{1,9},{2,10},{3,11},{4,12},{5,13},{6,14},{7,15},{8,0},{9,1},... | collective-permute-start | bytes 393224 | tf_op jit(solution)/shard_map/ppermute | solution.py:58
  21.0 0.5 %collective-permute-start.8 = (f32[1,128,128]{2,1,0:T(8,128)S(1)}, f32[1,128,128]{2,1,0:T(8,128)S(1)}, u32[]{:S(2)}, u32[]{:S(2)}) collective-permute-start(f32[1,128,128]{2,1,0:T(8,128)S(1)} %bitcast.8), channel_id=1, source_target_pairs={{0,8},{1,9},{2,10},{3,11},{4,12},{5,13},{6,14},{7,15},{8,0},{9,1},... | collective-permute-start | bytes 196616 | tf_op jit(solution)/shard_map/ppermute | solution.py:58
  21.4 2.9 %collective-permute-done.6.refs_1_ = f32[256,128]{1,0:T(8,128)S(1)} collective-permute-done((f32[256,128]{1,0:T(8,128)S(1)}, f32[256,128]{1,0:T(8,128)S(1)}, u32[]{:S(2)}, u32[]{:S(2)}) %collective-permute-start.6) | collective-permute-done | bytes 131104 | tf_op jit(solution)/shard_map/ppermute | solution.py:58
  24.4 0.2 climb.3
  24.6 3.0 %collective-permute-start.7 = (f32[128,128]{1,0:T(8,128)S(1)}, f32[128,128]{1,0:T(8,128)S(1)}, u32[]{:S(2)}, u32[]{:S(2)}) collective-permute-start(f32[128,128]{1,0:T(8,128)S(1)} %get-tuple-element.47.refs_0_.refs_3_), channel_id=1, source_target_pairs={{0,16},{1,17},{2,18},{3,19},{4,20},{5,21},{6,22},{7,23},{8,24},{9,... | collective-permute-start | bytes 196616 | tf_op jit(solution)/shard_map/ppermute | solution.py:58
  27.6 0.8 %collective-permute-start.12 = (f32[3,64,128]{2,1,0:T(8,128)S(1)}, f32[3,64,128]{2,1,0:T(8,128)S(1)}, u32[]{:S(2)}, u32[]{:S(2)}) collective-permute-start(f32[3,64,128]{2,1,0:T(8,128)S(1)} %halve.1), channel_id=1, source_target_pairs={{0,16},{1,17},{2,18},{3,19},{4,20},{5,21},{6,22},{7,23},{8,24},{9,... | collective-permute-start | bytes 294920 | tf_op jit(solution)/shard_map/ppermute | solution.py:58
  28.4 1.8 %collective-permute-done.7.refs_1_ = f32[128,128]{1,0:T(8,128)S(1)} collective-permute-done((f32[128,128]{1,0:T(8,128)S(1)}, f32[128,128]{1,0:T(8,128)S(1)}, u32[]{:S(2)}, u32[]{:S(2)}) %collective-permute-start.7) | collective-permute-done | bytes 65568 | tf_op jit(solution)/shard_map/ppermute | solution.py:58
  30.2 0.8 %descend.1.refs_0_ = f32[384,128]{1,0:T(8,128)S(1)} custom-call(f32[128,128]{1,0:T(8,128)S(1)} %get-tuple-element.47.refs_0_.refs_3_, f32[128,128]{1,0:T(8,128)S(1)} %collective-permute-done.7.refs_1_, bf16[7,384,128]{2,1,0:T(8,128)(2,1)S(1)} %get-tuple-element.44.refs_4_.refs_2_, bf16[7,384,128]{2,1,0:T(8,128)(2,1)S(1)} %get-tuple-element.45.refs_5_.refs_3_, ...), custom_call_target="tpu_custom_call" | custom-call | flops 1000 | bytes 1000 | tf_op jit(solution)/shard_map/descend/pallas_call | solution.py:309
  31.0 1.6 %collective-permute-start.9 = (f32[384,128]{1,0:T(8,128)S(1)}, f32[384,128]{1,0:T(8,128)S(1)}, u32[]{:S(2)}, u32[]{:S(2)}) collective-permute-start(f32[384,128]{1,0:T(8,128)S(1)} %descend.1.refs_0_), channel_id=1, source_target_pairs={{0,2},{1,3},{2,0},{3,1},{4,6},{5,7},{6,4},{7,5},{8,10},{9,11},{10,... | collective-permute-start | bytes 589832 | tf_op jit(solution)/shard_map/ppermute | solution.py:58
  32.5 0.5 %settle.2 = (f32[512,128]{1,0:T(8,128)S(1)}, f32[8,128]{1,0:T(8,128)S(1)}) custom-call(f32[384,128]{1,0:T(8,128)S(1)} %descend.1.refs_0_, f32[512,256]{1,0:T(8,128)S(1)} %get-tuple-element.52.refs_1_, bf16[512,384]{1,0:T(8,128)(2,1)S(1)} %get-tuple-element.53.refs_2_, bf16[512,384]{1,0:T(8,128)(2,1)S(1)} %get-tuple-element.54.refs_3_), custom_call_target="tpu_custom_call" | custom-call | flops 1000 | bytes 1000 | tf_op jit(solution)/shard_map/settle/pallas_call | solution.py:309
  33.1 1.1 %collective-permute-done.12.refs_4_ = f32[3,64,128]{2,1,0:T(8,128)S(1)} collective-permute-done((f32[3,64,128]{2,1,0:T(8,128)S(1)}, f32[3,64,128]{2,1,0:T(8,128)S(1)}, u32[]{:S(2)}, u32[]{:S(2)}) %collective-permute-start.12) | collective-permute-done | bytes 98336 | tf_op jit(solution)/shard_map/ppermute | solution.py:58
  34.3 1.2 %collective-permute-start.13 = (f32[3,64,128]{2,1,0:T(8,128)S(1)}, f32[3,64,128]{2,1,0:T(8,128)S(1)}, u32[]{:S(2)}, u32[]{:S(2)}) collective-permute-start(f32[3,64,128]{2,1,0:T(8,128)S(1)} %broadcast_add_fusion.2), channel_id=1, source_target_pairs={{0,4},{1,5},{2,6},{3,7},{4,0},{5,1},{6,2},{7,3},{8,12},{9,13},{10,... | collective-permute-start | bytes 294920 | tf_op jit(solution)/shard_map/ppermute | solution.py:58
  35.4 1.2 %cross.1 = (f32[512,512]{1,0:T(8,128)}, f32[8,128]{1,0:T(8,128)S(1)}) custom-call(f32[384,128]{1,0:T(8,128)S(1)} %collective-permute-done.10.refs_0_, f32[512,256]{1,0:T(8,128)S(1)} %get-tuple-element.56.refs_1_, bf16[512,384]{1,0:T(8,128)(2,1)S(1)} %get-tuple-element.53.refs_2_, bf16[512,384]{1,0:T(8,128)(2,1)S(1)} %get-tuple-element.54.refs_3_, ...), custom_call_target="tpu_custom_call" | custom-call | flops 1000 | bytes 1000 | tf_op jit(solution)/shard_map/cross/pallas_call | solution.py:309
  36.7 0.2 collective-permute-start.11
  36.9 0.5 %settle.3 = (f32[512,128]{1,0:T(8,128)S(1)}, f32[8,128]{1,0:T(8,128)S(1)}) custom-call(f32[384,128]{1,0:T(8,128)S(1)} %broadcast_add_fusion.refs_0_, f32[512,256]{1,0:T(8,128)S(1)} %get-tuple-element.52.refs_1_, bf16[512,384]{1,0:T(8,128)(2,1)S(1)} %get-tuple-element.53.refs_2_, bf16[512,384]{1,0:T(8,128)(2,1)S(1)} %get-tuple-element.54.refs_3_), custom_call_target="tpu_custom_call" | custom-call | flops 1000 | bytes 1000 | tf_op jit(solution)/shard_map/settle/pallas_call | solution.py:309
  37.4 1.6 %collective-permute-done.13.refs_5_ = f32[3,64,128]{2,1,0:T(8,128)S(1)} collective-permute-done((f32[3,64,128]{2,1,0:T(8,128)S(1)}, f32[3,64,128]{2,1,0:T(8,128)S(1)}, u32[]{:S(2)}, u32[]{:S(2)}) %collective-permute-start.13) | collective-permute-done | bytes 98336 | tf_op jit(solution)/shard_map/ppermute | solution.py:58
  38.9 0.5 %top.1.refs_5_ = f32[896,128]{1,0:T(8,128)S(1)} custom-call(f32[384,128]{1,0:T(8,128)S(1)} %descend.1.refs_0_, bf16[7,128,384]{2,1,0:T(8,128)(2,1)S(1)} %get-tuple-element.48.refs_4_.refs_1_, bf16[7,128,384]{2,1,0:T(8,128)(2,1)S(1)} %get-tuple-element.49.refs_5_.refs_2_, f32[1,128,128]{2,1,0:T(8,128)S(1)} %collective-permute-done.8.refs_8_.refs_1_.refs_3_, ...), custom_call_target="tpu_custom_call" | custom-call | flops 5000000000 | bytes 1000 | tf_op jit(solution)/shard_map/top/pallas_call | solution.py:309
  39.5 1.2 %last.1 = (f32[512,512]{1,0:T(8,128)}, f32[896,128]{1,0:T(8,128)}) custom-call(f32[384,128]{1,0:T(8,128)S(1)} %collective-permute-done.11.refs_0_, f32[512,256]{1,0:T(8,128)S(1)} %get-tuple-element.56.refs_1_, bf16[512,384]{1,0:T(8,128)(2,1)S(1)} %get-tuple-element.53.refs_2_, ...), custom_call_target="tpu_custom_call", output_to_operand_aliasing={{0}: (6, {})} | custom-call | flops 1000 | bytes 1000 | tf_op jit(solution)/shard_map/last/pallas_call | solution.py:309
  (26 shorter events, 0.4 us)
Async XLA Ops:
  0.6 3.6 %copy-start.2 = (f32[896,128]{1,0:T(8,128)S(1)}, f32[896,128]{1,0:T(8,128)}, u32[]{:S(2)}) copy-start(f32[896,128]{1,0:T(8,128)} %refs_5_.1) | copy-start | bytes 1376260
  3.6 11.9 %copy-start = (f32[10,128,128]{2,1,0:T(8,128)S(1)}, f32[10,128,128]{2,1,0:T(8,128)}, u32[]{:S(2)}) copy-start(f32[10,128,128]{2,1,0:T(8,128)} %refs_1_.3) | copy-start | bytes 1966084
  3.6 11.9 %copy-start.1 = (f32[7,128,128]{2,1,0:T(8,128)S(1)}, f32[7,128,128]{2,1,0:T(8,128)}, u32[]{:S(2)}) copy-start(f32[7,128,128]{2,1,0:T(8,128)} %refs_0_.3) | copy-start | bytes 1376260
  3.7 4.8 %collective-permute-start = (f32[544,128]{1,0:T(8,128)S(1)}, f32[544,128]{1,0:T(8,128)S(1)}, u32[]{:S(2)}, u32[]{:S(2)}) collective-permute-start(f32[544,128]{1,0:T(8,128)S(1)} %get-tuple-element.38), channel_id=1, source_target_pairs={{0,1},{1,0},{2,3},{3,2},{4,5},{5,4},{6,7},{7,6},{8,9},{9,8},{10,11... | collective-permute-start | bytes 835592 | tf_op jit(solution)/shard_map/ppermute | solution.py:58
  4.2 1.3 %collective-permute-start.1 = (f32[224,128]{1,0:T(8,128)S(1)}, f32[224,128]{1,0:T(8,128)S(1)}, u32[]{:S(2)}, u32[]{:S(2)}) collective-permute-start(f32[224,128]{1,0:T(8,128)S(1)} %get-tuple-element.40), channel_id=1, source_target_pairs={{0,1},{1,0},{2,3},{3,2},{4,5},{5,4},{6,7},{7,6},{8,9},{9,8},{10,11... | collective-permute-start | bytes 344072 | tf_op jit(solution)/shard_map/ppermute | solution.py:58
  5.5 6.9 %collective-permute-start.2 = (f32[224,128]{1,0:T(8,128)S(1)}, f32[224,128]{1,0:T(8,128)S(1)}, u32[]{:S(2)}, u32[]{:S(2)}) collective-permute-start(f32[224,128]{1,0:T(8,128)S(1)} %add.62.refs_6_), channel_id=1, source_target_pairs={{0,2},{1,3},{2,0},{3,1},{4,6},{5,7},{6,4},{7,5},{8,10},{9,11},{10,... | collective-permute-start | bytes 344072 | tf_op jit(solution)/shard_map/ppermute | solution.py:58
  8.5 6.1 %collective-permute-start.3 = (f32[160,128]{1,0:T(8,128)S(1)}, f32[160,128]{1,0:T(8,128)S(1)}, u32[]{:S(2)}, u32[]{:S(2)}) collective-permute-start(f32[160,128]{1,0:T(8,128)S(1)} %slice_add_fusion.3.refs_7_), channel_id=1, source_target_pairs={{0,2},{1,3},{2,0},{3,1},{4,6},{5,7},{6,4},{7,5},{8,10},{9,11},{10,... | collective-permute-start | bytes 245768 | tf_op jit(solution)/shard_map/ppermute | solution.py:58
  12.4 5.7 %collective-permute-start.4 = (f32[224,128]{1,0:T(8,128)S(1)}, f32[224,128]{1,0:T(8,128)S(1)}, u32[]{:S(2)}, u32[]{:S(2)}) collective-permute-start(f32[224,128]{1,0:T(8,128)S(1)} %fusion.refs_0_), channel_id=1, source_target_pairs={{0,4},{1,5},{2,6},{3,7},{4,0},{5,1},{6,2},{7,3},{8,12},{9,13},{10,... | collective-permute-start | bytes 344072 | tf_op jit(solution)/shard_map/ppermute | solution.py:58
  14.6 4.5 %collective-permute-start.5 = (f32[160,128]{1,0:T(8,128)S(1)}, f32[160,128]{1,0:T(8,128)S(1)}, u32[]{:S(2)}, u32[]{:S(2)}) collective-permute-start(f32[160,128]{1,0:T(8,128)S(1)} %fusion.1.refs_2_.refs_1_), channel_id=1, source_target_pairs={{0,4},{1,5},{2,6},{3,7},{4,0},{5,1},{6,2},{7,3},{8,12},{9,13},{10,... | collective-permute-start | bytes 245768 | tf_op jit(solution)/shard_map/ppermute | solution.py:58
  19.3 5.0 %collective-permute-start.6 = (f32[256,128]{1,0:T(8,128)S(1)}, f32[256,128]{1,0:T(8,128)S(1)}, u32[]{:S(2)}, u32[]{:S(2)}) collective-permute-start(f32[256,128]{1,0:T(8,128)S(1)} %get-tuple-element.46.refs_0_), channel_id=1, source_target_pairs={{0,8},{1,9},{2,10},{3,11},{4,12},{5,13},{6,14},{7,15},{8,0},{9,1},... | collective-permute-start | bytes 393224 | tf_op jit(solution)/shard_map/ppermute | solution.py:58
  21.0 6.6 %collective-permute-start.8 = (f32[1,128,128]{2,1,0:T(8,128)S(1)}, f32[1,128,128]{2,1,0:T(8,128)S(1)}, u32[]{:S(2)}, u32[]{:S(2)}) collective-permute-start(f32[1,128,128]{2,1,0:T(8,128)S(1)} %bitcast.8), channel_id=1, source_target_pairs={{0,8},{1,9},{2,10},{3,11},{4,12},{5,13},{6,14},{7,15},{8,0},{9,1},... | collective-permute-start | bytes 196616 | tf_op jit(solution)/shard_map/ppermute | solution.py:58
  24.6 5.6 %collective-permute-start.7 = (f32[128,128]{1,0:T(8,128)S(1)}, f32[128,128]{1,0:T(8,128)S(1)}, u32[]{:S(2)}, u32[]{:S(2)}) collective-permute-start(f32[128,128]{1,0:T(8,128)S(1)} %get-tuple-element.47.refs_0_.refs_3_), channel_id=1, source_target_pairs={{0,16},{1,17},{2,18},{3,19},{4,20},{5,21},{6,22},{7,23},{8,24},{9,... | collective-permute-start | bytes 196616 | tf_op jit(solution)/shard_map/ppermute | solution.py:58
  27.6 6.6 %collective-permute-start.12 = (f32[3,64,128]{2,1,0:T(8,128)S(1)}, f32[3,64,128]{2,1,0:T(8,128)S(1)}, u32[]{:S(2)}, u32[]{:S(2)}) collective-permute-start(f32[3,64,128]{2,1,0:T(8,128)S(1)} %halve.1), channel_id=1, source_target_pairs={{0,16},{1,17},{2,18},{3,19},{4,20},{5,21},{6,22},{7,23},{8,24},{9,... | collective-permute-start | bytes 294920 | tf_op jit(solution)/shard_map/ppermute | solution.py:58
  31.0 5.7 %collective-permute-start.9 = (f32[384,128]{1,0:T(8,128)S(1)}, f32[384,128]{1,0:T(8,128)S(1)}, u32[]{:S(2)}, u32[]{:S(2)}) collective-permute-start(f32[384,128]{1,0:T(8,128)S(1)} %descend.1.refs_0_), channel_id=1, source_target_pairs={{0,2},{1,3},{2,0},{3,1},{4,6},{5,7},{6,4},{7,5},{8,10},{9,11},{10,... | collective-permute-start | bytes 589832 | tf_op jit(solution)/shard_map/ppermute | solution.py:58
  33.0 2.4 %collective-permute-start.10 = (f32[384,128]{1,0:T(8,128)S(1)}, f32[384,128]{1,0:T(8,128)S(1)}, u32[]{:S(2)}, u32[]{:S(2)}) collective-permute-start(f32[384,128]{1,0:T(8,128)S(1)} %broadcast_add_fusion.1), channel_id=1, source_target_pairs={{0,1},{1,0},{2,3},{3,2},{4,5},{5,4},{6,7},{7,6},{8,9},{9,8},{10,11... | collective-permute-start | bytes 589832 | tf_op jit(solution)/shard_map/ppermute | solution.py:58
  34.3 4.7 %collective-permute-start.13 = (f32[3,64,128]{2,1,0:T(8,128)S(1)}, f32[3,64,128]{2,1,0:T(8,128)S(1)}, u32[]{:S(2)}, u32[]{:S(2)}) collective-permute-start(f32[3,64,128]{2,1,0:T(8,128)S(1)} %broadcast_add_fusion.2), channel_id=1, source_target_pairs={{0,4},{1,5},{2,6},{3,7},{4,0},{5,1},{6,2},{7,3},{8,12},{9,13},{10,... | collective-permute-start | bytes 294920 | tf_op jit(solution)/shard_map/ppermute | solution.py:58
  36.7 2.8 %collective-permute-start.11 = (f32[384,128]{1,0:T(8,128)S(1)}, f32[384,128]{1,0:T(8,128)S(1)}, u32[]{:S(2)}, u32[]{:S(2)}) collective-permute-start(f32[384,128]{1,0:T(8,128)S(1)} %broadcast_add_fusion.refs_0_), channel_id=1, source_target_pairs={{0,1},{1,0},{2,3},{3,2},{4,5},{5,4},{6,7},{7,6},{8,9},{9,8},{10,11... | collective-permute-start | bytes 589832 | tf_op jit(solution)/shard_map/ppermute | solution.py:58

commit v10 on v8

--- a/solution.py
+++ b/solution.py
@@ -236,7 +236,7 @@
     for copy in copies:
         copy.start()
     known = split(part[...])
-    step = buffer.shape[0] // 2
+    step = buffer.shape[0] // 4
     for start in range(0, buffer.shape[0], step):
         rows = slice(start, start + step)
         change = dot(gain_hi[rows], known[0]) + (dot(gain_hi[rows], known[1]) + dot(gain_lo[rows], known[0]))
@@ -416,7 +416,7 @@
         [(pltpu.HBM(whole, F32), HBM_SPEC),
          (pltpu.HBM((panel_count * width, columns), F32), HBM_SPEC)],
         [last, base_other, gain_hi, gain_lo, far, top, out], anys=(6,), alias={6: 0},
-        scratch=[pltpu.VMEM((order, columns), F32), pltpu.SemaphoreType.DMA((4,))], name="last")
+        scratch=[pltpu.VMEM((order, columns), F32), pltpu.SemaphoreType.DMA((6,))], name="last")
     return out, top
 
 

time: 40.8 us -> 40.8 us (level)
  no operation moved by 1% of the time
where the time goes in v10:
time: 40.8 us; the launch traced here: 40.7 us
  starting transfers between devices  15.6 us (38%)
  waiting for transfers between devices  12.6 us (31%)
  Pallas kernels  11.4 us (28%)
  between operations  0.83 us (2%)
    ppermute x14, starting transfers between devices, swap(): return lax.ppermute(value, ('leaf', 'rhs'), pairs)  15.6 us
    ppermute x14, waiting for transfers between devices, swap(): return lax.ppermute(value, ('leaf', 'rhs'), pairs)  12.6 us
    pallas_call x13, Pallas kernels, call(): pl.pallas_call(body, out_shape=[shape for shape, _ in outs], in_specs=spe...  11.4 us
  transfers between devices with their start and end apart: 14, of which 9 were waited for; matrix products, arithmetic and copies ran while one was open for 0% of the time, Pallas kernels for 17%

profile of v10, /device:TPU:0, one launch (start us, length us, event | category | flops | bytes accessed | tf_op | source)
XLA Modules:
  0.0 40.7 jit_solution(14619013548471912831)
XLA Ops:
  0.6 3.0 %lift.1 = (f32[224,128]{1,0:T(8,128)S(1)}, f32[544,128]{1,0:T(8,128)S(1)}, f32[512,256]{1,0:T(8,128)S(1)}, f32[512,256]{1,0:T(8,128)S(1)}, bf16[512,512]{1,0:T(8...) custom-call(f32[512,512]{1,0:T(8,128)} %refs_0_.2, ...), custom_call_target="tpu_custom_call" | custom-call | flops 1000 | bytes 1000 | tf_op jit(solution)/shard_map/lift/pallas_call | solution.py:303
  3.7 0.5 %collective-permute-start = (f32[544,128]{1,0:T(8,128)S(1)}, f32[544,128]{1,0:T(8,128)S(1)}, u32[]{:S(2)}, u32[]{:S(2)}) collective-permute-start(f32[544,128]{1,0:T(8,128)S(1)} %get-tuple-element.38), channel_id=1, source_target_pairs={{0,1},{1,0},{2,3},{3,2},{4,5},{5,4},{6,7},{7,6},{8,9},{9,8},{10,11... | collective-permute-start | bytes 835592 | tf_op jit(solution)/shard_map/ppermute | solution.py:58
  4.2 1.1 %own.1 = (f32[224,128]{1,0:T(8,128)S(1)}, f32[544,128]{1,0:T(8,128)S(1)}, f32[512,256]{1,0:T(8,128)S(1)}) custom-call(f32[512,256]{1,0:T(8,128)S(1)} %get-tuple-element.32.refs_0_, bf16[512,512]{1,0:T(8,128)(2,1)S(1)} %get-tuple-element.33.refs_1_.refs_0_, bf16[512,512]{1,0:T(8,128)(2,1)S(1)} %get-tuple-element.34.refs_2_.refs_1_, ...), custom_call_target="tpu_custom_call" | custom-call | flops 1000 | bytes 1000 | tf_op jit(solution)/shard_map/own/pallas_call | solution.py:303
  5.3 0.2 collective-permute-done.1
  5.5 2.9 %collective-permute-start.2 = (f32[224,128]{1,0:T(8,128)S(1)}, f32[224,128]{1,0:T(8,128)S(1)}, u32[]{:S(2)}, u32[]{:S(2)}) collective-permute-start(f32[224,128]{1,0:T(8,128)S(1)} %add.62.refs_6_), channel_id=1, source_target_pairs={{0,2},{1,3},{2,0},{3,1},{4,6},{5,7},{6,4},{7,5},{8,10},{9,11},{10,... | collective-permute-start | bytes 344072 | tf_op jit(solution)/shard_map/ppermute | solution.py:58
  8.5 0.1 collective-permute-start.3
  8.6 1.8 %turn.1 = (f32[512,256]{1,0:T(8,128)S(1)}, f32[512,256]{1,0:T(8,128)S(1)}, bf16[512,384]{1,0:T(8,128)(2,1)S(1)}, bf16[512,384]{1,0:T(8,128)(2,1)S(1)}, f32[8,128]{1,0:T(8,128)S(1)}) custom-call(bf16[512,512]{1,0:T(8,128)(2,1)S(1)} %get-tuple-element.33.refs_1_.refs_0_, bf16[512,512]{1,0:T(8,128)(2,1)S(1)} %get-tuple-element.34.refs_2_.refs_1_, ...), custom_call_target="tpu_custom_call" | custom-call | flops 1000 | bytes 1000 | tf_op jit(solution)/shard_map/turn/pallas_call | solution.py:303
  10.4 1.9 %collective-permute-done.2 = f32[224,128]{1,0:T(8,128)S(1)} collective-permute-done((f32[224,128]{1,0:T(8,128)S(1)}, f32[224,128]{1,0:T(8,128)S(1)}, u32[]{:S(2)}, u32[]{:S(2)}) %collective-permute-start.2) | collective-permute-done | bytes 114720 | tf_op jit(solution)/shard_map/ppermute | solution.py:58
  12.4 2.2 %collective-permute-start.4 = (f32[224,128]{1,0:T(8,128)S(1)}, f32[224,128]{1,0:T(8,128)S(1)}, u32[]{:S(2)}, u32[]{:S(2)}) collective-permute-start(f32[224,128]{1,0:T(8,128)S(1)} %fusion.refs_0_), channel_id=1, source_target_pairs={{0,4},{1,5},{2,6},{3,7},{4,0},{5,1},{6,2},{7,3},{8,12},{9,13},{10,... | collective-permute-start | bytes 344072 | tf_op jit(solution)/shard_map/ppermute | solution.py:58
  14.6 0.9 %collective-permute-start.5 = (f32[160,128]{1,0:T(8,128)S(1)}, f32[160,128]{1,0:T(8,128)S(1)}, u32[]{:S(2)}, u32[]{:S(2)}) collective-permute-start(f32[160,128]{1,0:T(8,128)S(1)} %fusion.1.refs_2_.refs_1_), channel_id=1, source_target_pairs={{0,4},{1,5},{2,6},{3,7},{4,0},{5,1},{6,2},{7,3},{8,12},{9,13},{10,... | collective-permute-start | bytes 245768 | tf_op jit(solution)/shard_map/ppermute | solution.py:58
  15.5 0.6 %ready.1 = (bf16[7,384,128]{2,1,0:T(8,128)(2,1)S(1)}, bf16[7,384,128]{2,1,0:T(8,128)(2,1)S(1)}, bf16[7,128,384]{2,1,0:T(8,128)(2,1)S(1)}, bf16[7,128,384]{2,1,0:T(8,128)(2,1)S(1)}) custom-call(f32[7,128,128]{2,1,0:T(8,128)S(1)} %copy-done.1, f32[10,128,128]{2,1,0:T(8,128)S(1)} %copy-done, f32[160,128]{1,0:T(8,128)S(1)} %fusion.1.refs_2_.refs_1_), custom_call_target="tpu_custom_call" | custom-call | flops 1000 | bytes 1000 | tf_op jit(solution)/shard_map/ready/pallas_call | solution.py:303
  16.1 2.0 %collective-permute-done.4.refs_2_ = f32[224,128]{1,0:T(8,128)S(1)} collective-permute-done((f32[224,128]{1,0:T(8,128)S(1)}, f32[224,128]{1,0:T(8,128)S(1)}, u32[]{:S(2)}, u32[]{:S(2)}) %collective-permute-start.4) | collective-permute-done | bytes 114720 | tf_op jit(solution)/shard_map/ppermute | solution.py:58
  18.1 1.0 %collective-permute-done.5.refs_3_ = f32[160,128]{1,0:T(8,128)S(1)} collective-permute-done((f32[160,128]{1,0:T(8,128)S(1)}, f32[160,128]{1,0:T(8,128)S(1)}, u32[]{:S(2)}, u32[]{:S(2)}) %collective-permute-start.5) | collective-permute-done | bytes 81952 | tf_op jit(solution)/shard_map/ppermute | solution.py:58
  19.1 0.2 climb.2
  19.3 1.6 %collective-permute-start.6 = (f32[256,128]{1,0:T(8,128)S(1)}, f32[256,128]{1,0:T(8,128)S(1)}, u32[]{:S(2)}, u32[]{:S(2)}) collective-permute-start(f32[256,128]{1,0:T(8,128)S(1)} %get-tuple-element.46.refs_0_), channel_id=1, source_target_pairs={{0,8},{1,9},{2,10},{3,11},{4,12},{5,13},{6,14},{7,15},{8,0},{9,1},... | collective-permute-start | bytes 393224 | tf_op jit(solution)/shard_map/ppermute | solution.py:58
  21.0 0.5 %collective-permute-start.8 = (f32[1,128,128]{2,1,0:T(8,128)S(1)}, f32[1,128,128]{2,1,0:T(8,128)S(1)}, u32[]{:S(2)}, u32[]{:S(2)}) collective-permute-start(f32[1,128,128]{2,1,0:T(8,128)S(1)} %bitcast.8), channel_id=1, source_target_pairs={{0,8},{1,9},{2,10},{3,11},{4,12},{5,13},{6,14},{7,15},{8,0},{9,1},... | collective-permute-start | bytes 196616 | tf_op jit(solution)/shard_map/ppermute | solution.py:58
  21.4 2.9 %collective-permute-done.6.refs_1_ = f32[256,128]{1,0:T(8,128)S(1)} collective-permute-done((f32[256,128]{1,0:T(8,128)S(1)}, f32[256,128]{1,0:T(8,128)S(1)}, u32[]{:S(2)}, u32[]{:S(2)}) %collective-permute-start.6) | collective-permute-done | bytes 131104 | tf_op jit(solution)/shard_map/ppermute | solution.py:58
  24.4 0.2 climb.3
  24.6 3.0 %collective-permute-start.7 = (f32[128,128]{1,0:T(8,128)S(1)}, f32[128,128]{1,0:T(8,128)S(1)}, u32[]{:S(2)}, u32[]{:S(2)}) collective-permute-start(f32[128,128]{1,0:T(8,128)S(1)} %get-tuple-element.47.refs_0_.refs_3_), channel_id=1, source_target_pairs={{0,16},{1,17},{2,18},{3,19},{4,20},{5,21},{6,22},{7,23},{8,24},{9,... | collective-permute-start | bytes 196616 | tf_op jit(solution)/shard_map/ppermute | solution.py:58
  27.6 0.8 %collective-permute-start.12 = (f32[3,64,128]{2,1,0:T(8,128)S(1)}, f32[3,64,128]{2,1,0:T(8,128)S(1)}, u32[]{:S(2)}, u32[]{:S(2)}) collective-permute-start(f32[3,64,128]{2,1,0:T(8,128)S(1)} %halve.1), channel_id=1, source_target_pairs={{0,16},{1,17},{2,18},{3,19},{4,20},{5,21},{6,22},{7,23},{8,24},{9,... | collective-permute-start | bytes 294920 | tf_op jit(solution)/shard_map/ppermute | solution.py:58
  28.4 1.8 %collective-permute-done.7.refs_1_ = f32[128,128]{1,0:T(8,128)S(1)} collective-permute-done((f32[128,128]{1,0:T(8,128)S(1)}, f32[128,128]{1,0:T(8,128)S(1)}, u32[]{:S(2)}, u32[]{:S(2)}) %collective-permute-start.7) | collective-permute-done | bytes 65568 | tf_op jit(solution)/shard_map/ppermute | solution.py:58
  30.2 0.8 %descend.1.refs_0_ = f32[384,128]{1,0:T(8,128)S(1)} custom-call(f32[128,128]{1,0:T(8,128)S(1)} %get-tuple-element.47.refs_0_.refs_3_, f32[128,128]{1,0:T(8,128)S(1)} %collective-permute-done.7.refs_1_, bf16[7,384,128]{2,1,0:T(8,128)(2,1)S(1)} %get-tuple-element.44.refs_4_.refs_2_, bf16[7,384,128]{2,1,0:T(8,128)(2,1)S(1)} %get-tuple-element.45.refs_5_.refs_3_, ...), custom_call_target="tpu_custom_call" | custom-call | flops 1000 | bytes 1000 | tf_op jit(solution)/shard_map/descend/pallas_call | solution.py:303
  31.0 1.6 %collective-permute-start.9 = (f32[384,128]{1,0:T(8,128)S(1)}, f32[384,128]{1,0:T(8,128)S(1)}, u32[]{:S(2)}, u32[]{:S(2)}) collective-permute-start(f32[384,128]{1,0:T(8,128)S(1)} %descend.1.refs_0_), channel_id=1, source_target_pairs={{0,2},{1,3},{2,0},{3,1},{4,6},{5,7},{6,4},{7,5},{8,10},{9,11},{10,... | collective-permute-start | bytes 589832 | tf_op jit(solution)/shard_map/ppermute | solution.py:58
  32.5 0.5 %settle.2 = (f32[512,128]{1,0:T(8,128)S(1)}, f32[8,128]{1,0:T(8,128)S(1)}) custom-call(f32[384,128]{1,0:T(8,128)S(1)} %descend.1.refs_0_, f32[512,256]{1,0:T(8,128)S(1)} %get-tuple-element.52.refs_1_, bf16[512,384]{1,0:T(8,128)(2,1)S(1)} %get-tuple-element.53.refs_2_, bf16[512,384]{1,0:T(8,128)(2,1)S(1)} %get-tuple-element.54.refs_3_), custom_call_target="tpu_custom_call" | custom-call | flops 1000 | bytes 1000 | tf_op jit(solution)/shard_map/settle/pallas_call | solution.py:303
  33.1 1.1 %collective-permute-done.12.refs_4_ = f32[3,64,128]{2,1,0:T(8,128)S(1)} collective-permute-done((f32[3,64,128]{2,1,0:T(8,128)S(1)}, f32[3,64,128]{2,1,0:T(8,128)S(1)}, u32[]{:S(2)}, u32[]{:S(2)}) %collective-permute-start.12) | collective-permute-done | bytes 98336 | tf_op jit(solution)/shard_map/ppermute | solution.py:58
  34.3 1.2 %collective-permute-start.13 = (f32[3,64,128]{2,1,0:T(8,128)S(1)}, f32[3,64,128]{2,1,0:T(8,128)S(1)}, u32[]{:S(2)}, u32[]{:S(2)}) collective-permute-start(f32[3,64,128]{2,1,0:T(8,128)S(1)} %broadcast_add_fusion.2), channel_id=1, source_target_pairs={{0,4},{1,5},{2,6},{3,7},{4,0},{5,1},{6,2},{7,3},{8,12},{9,13},{10,... | collective-permute-start | bytes 294920 | tf_op jit(solution)/shard_map/ppermute | solution.py:58
  35.4 1.2 %cross.1 = (f32[512,512]{1,0:T(8,128)}, f32[8,128]{1,0:T(8,128)S(1)}) custom-call(f32[384,128]{1,0:T(8,128)S(1)} %collective-permute-done.10.refs_0_, f32[512,256]{1,0:T(8,128)S(1)} %get-tuple-element.56.refs_1_, bf16[512,384]{1,0:T(8,128)(2,1)S(1)} %get-tuple-element.53.refs_2_, bf16[512,384]{1,0:T(8,128)(2,1)S(1)} %get-tuple-element.54.refs_3_, ...), custom_call_target="tpu_custom_call" | custom-call | flops 1000 | bytes 1000 | tf_op jit(solution)/shard_map/cross/pallas_call | solution.py:303
  36.7 0.2 collective-permute-start.11
  36.9 0.5 %settle.3 = (f32[512,128]{1,0:T(8,128)S(1)}, f32[8,128]{1,0:T(8,128)S(1)}) custom-call(f32[384,128]{1,0:T(8,128)S(1)} %broadcast_add_fusion.refs_0_, f32[512,256]{1,0:T(8,128)S(1)} %get-tuple-element.52.refs_1_, bf16[512,384]{1,0:T(8,128)(2,1)S(1)} %get-tuple-element.53.refs_2_, bf16[512,384]{1,0:T(8,128)(2,1)S(1)} %get-tuple-element.54.refs_3_), custom_call_target="tpu_custom_call" | custom-call | flops 1000 | bytes 1000 | tf_op jit(solution)/shard_map/settle/pallas_call | solution.py:303
  37.4 1.6 %collective-permute-done.13.refs_5_ = f32[3,64,128]{2,1,0:T(8,128)S(1)} collective-permute-done((f32[3,64,128]{2,1,0:T(8,128)S(1)}, f32[3,64,128]{2,1,0:T(8,128)S(1)}, u32[]{:S(2)}, u32[]{:S(2)}) %collective-permute-start.13) | collective-permute-done | bytes 98336 | tf_op jit(solution)/shard_map/ppermute | solution.py:58
  38.9 0.5 %top.1.refs_5_ = f32[896,128]{1,0:T(8,128)S(1)} custom-call(f32[384,128]{1,0:T(8,128)S(1)} %descend.1.refs_0_, bf16[7,128,384]{2,1,0:T(8,128)(2,1)S(1)} %get-tuple-element.48.refs_4_.refs_1_, bf16[7,128,384]{2,1,0:T(8,128)(2,1)S(1)} %get-tuple-element.49.refs_5_.refs_2_, f32[1,128,128]{2,1,0:T(8,128)S(1)} %collective-permute-done.8.refs_8_.refs_1_.refs_3_, ...), custom_call_target="tpu_custom_call" | custom-call | flops 5000000000 | bytes 1000 | tf_op jit(solution)/shard_map/top/pallas_call | solution.py:303
  39.5 1.2 %last.1 = (f32[512,512]{1,0:T(8,128)}, f32[896,128]{1,0:T(8,128)}) custom-call(f32[384,128]{1,0:T(8,128)S(1)} %collective-permute-done.11.refs_0_, f32[512,256]{1,0:T(8,128)S(1)} %get-tuple-element.56.refs_1_, bf16[512,384]{1,0:T(8,128)(2,1)S(1)} %get-tuple-element.53.refs_2_, ...), custom_call_target="tpu_custom_call", output_to_operand_aliasing={{0}: (6, {})} | custom-call | flops 1000 | bytes 1000 | tf_op jit(solution)/shard_map/last/pallas_call | solution.py:303
  (26 shorter events, 0.4 us)
Async XLA Ops:
  0.6 3.6 %copy-start.2 = (f32[896,128]{1,0:T(8,128)S(1)}, f32[896,128]{1,0:T(8,128)}, u32[]{:S(2)}) copy-start(f32[896,128]{1,0:T(8,128)} %refs_5_.1) | copy-start | bytes 1376260
  3.6 11.9 %copy-start = (f32[10,128,128]{2,1,0:T(8,128)S(1)}, f32[10,128,128]{2,1,0:T(8,128)}, u32[]{:S(2)}) copy-start(f32[10,128,128]{2,1,0:T(8,128)} %refs_1_.3) | copy-start | bytes 1966084
  3.6 11.9 %copy-start.1 = (f32[7,128,128]{2,1,0:T(8,128)S(1)}, f32[7,128,128]{2,1,0:T(8,128)}, u32[]{:S(2)}) copy-start(f32[7,128,128]{2,1,0:T(8,128)} %refs_0_.3) | copy-start | bytes 1376260
  3.7 4.8 %collective-permute-start = (f32[544,128]{1,0:T(8,128)S(1)}, f32[544,128]{1,0:T(8,128)S(1)}, u32[]{:S(2)}, u32[]{:S(2)}) collective-permute-start(f32[544,128]{1,0:T(8,128)S(1)} %get-tuple-element.38), channel_id=1, source_target_pairs={{0,1},{1,0},{2,3},{3,2},{4,5},{5,4},{6,7},{7,6},{8,9},{9,8},{10,11... | collective-permute-start | bytes 835592 | tf_op jit(solution)/shard_map/ppermute | solution.py:58
  4.2 1.3 %collective-permute-start.1 = (f32[224,128]{1,0:T(8,128)S(1)}, f32[224,128]{1,0:T(8,128)S(1)}, u32[]{:S(2)}, u32[]{:S(2)}) collective-permute-start(f32[224,128]{1,0:T(8,128)S(1)} %get-tuple-element.40), channel_id=1, source_target_pairs={{0,1},{1,0},{2,3},{3,2},{4,5},{5,4},{6,7},{7,6},{8,9},{9,8},{10,11... | collective-permute-start | bytes 344072 | tf_op jit(solution)/shard_map/ppermute | solution.py:58
  5.5 6.9 %collective-permute-start.2 = (f32[224,128]{1,0:T(8,128)S(1)}, f32[224,128]{1,0:T(8,128)S(1)}, u32[]{:S(2)}, u32[]{:S(2)}) collective-permute-start(f32[224,128]{1,0:T(8,128)S(1)} %add.62.refs_6_), channel_id=1, source_target_pairs={{0,2},{1,3},{2,0},{3,1},{4,6},{5,7},{6,4},{7,5},{8,10},{9,11},{10,... | collective-permute-start | bytes 344072 | tf_op jit(solution)/shard_map/ppermute | solution.py:58
  8.5 6.1 %collective-permute-start.3 = (f32[160,128]{1,0:T(8,128)S(1)}, f32[160,128]{1,0:T(8,128)S(1)}, u32[]{:S(2)}, u32[]{:S(2)}) collective-permute-start(f32[160,128]{1,0:T(8,128)S(1)} %slice_add_fusion.3.refs_7_), channel_id=1, source_target_pairs={{0,2},{1,3},{2,0},{3,1},{4,6},{5,7},{6,4},{7,5},{8,10},{9,11},{10,... | collective-permute-start | bytes 245768 | tf_op jit(solution)/shard_map/ppermute | solution.py:58
  12.4 5.7 %collective-permute-start.4 = (f32[224,128]{1,0:T(8,128)S(1)}, f32[224,128]{1,0:T(8,128)S(1)}, u32[]{:S(2)}, u32[]{:S(2)}) collective-permute-start(f32[224,128]{1,0:T(8,128)S(1)} %fusion.refs_0_), channel_id=1, source_target_pairs={{0,4},{1,5},{2,6},{3,7},{4,0},{5,1},{6,2},{7,3},{8,12},{9,13},{10,... | collective-permute-start | bytes 344072 | tf_op jit(solution)/shard_map/ppermute | solution.py:58
  14.6 4.5 %collective-permute-start.5 = (f32[160,128]{1,0:T(8,128)S(1)}, f32[160,128]{1,0:T(8,128)S(1)}, u32[]{:S(2)}, u32[]{:S(2)}) collective-permute-start(f32[160,128]{1,0:T(8,128)S(1)} %fusion.1.refs_2_.refs_1_), channel_id=1, source_target_pairs={{0,4},{1,5},{2,6},{3,7},{4,0},{5,1},{6,2},{7,3},{8,12},{9,13},{10,... | collective-permute-start | bytes 245768 | tf_op jit(solution)/shard_map/ppermute | solution.py:58
  19.3 5.0 %collective-permute-start.6 = (f32[256,128]{1,0:T(8,128)S(1)}, f32[256,128]{1,0:T(8,128)S(1)}, u32[]{:S(2)}, u32[]{:S(2)}) collective-permute-start(f32[256,128]{1,0:T(8,128)S(1)} %get-tuple-element.46.refs_0_), channel_id=1, source_target_pairs={{0,8},{1,9},{2,10},{3,11},{4,12},{5,13},{6,14},{7,15},{8,0},{9,1},... | collective-permute-start | bytes 393224 | tf_op jit(solution)/shard_map/ppermute | solution.py:58
  21.0 6.6 %collective-permute-start.8 = (f32[1,128,128]{2,1,0:T(8,128)S(1)}, f32[1,128,128]{2,1,0:T(8,128)S(1)}, u32[]{:S(2)}, u32[]{:S(2)}) collective-permute-start(f32[1,128,128]{2,1,0:T(8,128)S(1)} %bitcast.8), channel_id=1, source_target_pairs={{0,8},{1,9},{2,10},{3,11},{4,12},{5,13},{6,14},{7,15},{8,0},{9,1},... | collective-permute-start | bytes 196616 | tf_op jit(solution)/shard_map/ppermute | solution.py:58
  24.6 5.6 %collective-permute-start.7 = (f32[128,128]{1,0:T(8,128)S(1)}, f32[128,128]{1,0:T(8,128)S(1)}, u32[]{:S(2)}, u32[]{:S(2)}) collective-permute-start(f32[128,128]{1,0:T(8,128)S(1)} %get-tuple-element.47.refs_0_.refs_3_), channel_id=1, source_target_pairs={{0,16},{1,17},{2,18},{3,19},{4,20},{5,21},{6,22},{7,23},{8,24},{9,... | collective-permute-start | bytes 196616 | tf_op jit(solution)/shard_map/ppermute | solution.py:58
  27.6 6.6 %collective-permute-start.12 = (f32[3,64,128]{2,1,0:T(8,128)S(1)}, f32[3,64,128]{2,1,0:T(8,128)S(1)}, u32[]{:S(2)}, u32[]{:S(2)}) collective-permute-start(f32[3,64,128]{2,1,0:T(8,128)S(1)} %halve.1), channel_id=1, source_target_pairs={{0,16},{1,17},{2,18},{3,19},{4,20},{5,21},{6,22},{7,23},{8,24},{9,... | collective-permute-start | bytes 294920 | tf_op jit(solution)/shard_map/ppermute | solution.py:58
  31.0 5.7 %collective-permute-start.9 = (f32[384,128]{1,0:T(8,128)S(1)}, f32[384,128]{1,0:T(8,128)S(1)}, u32[]{:S(2)}, u32[]{:S(2)}) collective-permute-start(f32[384,128]{1,0:T(8,128)S(1)} %descend.1.refs_0_), channel_id=1, source_target_pairs={{0,2},{1,3},{2,0},{3,1},{4,6},{5,7},{6,4},{7,5},{8,10},{9,11},{10,... | collective-permute-start | bytes 589832 | tf_op jit(solution)/shard_map/ppermute | solution.py:58
  33.0 2.4 %collective-permute-start.10 = (f32[384,128]{1,0:T(8,128)S(1)}, f32[384,128]{1,0:T(8,128)S(1)}, u32[]{:S(2)}, u32[]{:S(2)}) collective-permute-start(f32[384,128]{1,0:T(8,128)S(1)} %broadcast_add_fusion.1), channel_id=1, source_target_pairs={{0,1},{1,0},{2,3},{3,2},{4,5},{5,4},{6,7},{7,6},{8,9},{9,8},{10,11... | collective-permute-start | bytes 589832 | tf_op jit(solution)/shard_map/ppermute | solution.py:58
  34.3 4.7 %collective-permute-start.13 = (f32[3,64,128]{2,1,0:T(8,128)S(1)}, f32[3,64,128]{2,1,0:T(8,128)S(1)}, u32[]{:S(2)}, u32[]{:S(2)}) collective-permute-start(f32[3,64,128]{2,1,0:T(8,128)S(1)} %broadcast_add_fusion.2), channel_id=1, source_target_pairs={{0,4},{1,5},{2,6},{3,7},{4,0},{5,1},{6,2},{7,3},{8,12},{9,13},{10,... | collective-permute-start | bytes 294920 | tf_op jit(solution)/shard_map/ppermute | solution.py:58
  36.7 2.8 %collective-permute-start.11 = (f32[384,128]{1,0:T(8,128)S(1)}, f32[384,128]{1,0:T(8,128)S(1)}, u32[]{:S(2)}, u32[]{:S(2)}) collective-permute-start(f32[384,128]{1,0:T(8,128)S(1)} %broadcast_add_fusion.refs_0_), channel_id=1, source_target_pairs={{0,1},{1,0},{2,3},{3,2},{4,5},{5,4},{6,7},{7,6},{8,9},{9,8},{10,11... | collective-permute-start | bytes 589832 | tf_op jit(solution)/shard_map/ppermute | solution.py:58
